TPU v7x, 32 devices: a whole 2x2x4 slice. The times are simulated.
32 devices in a mesh: row: 4 (over y, x), col: 8 (over z, core).
Axes of the slice: x: 2, y: 2, z: 4, core: 2. Of those that a mesh axis runs over, the one named last changes fastest.
Arguments:
- adjacency: bfloat16 [8192, 8192], P('row', 'col'), as said below
- tile_mask: int32 [64, 64], P('row', 'col'), may hold values from 0 to 1, as said below
- out_grad: bfloat16 [8192, 256], P(('row', 'col')), may hold values from -6 to 6
- pre_two: bfloat16 [8192, 256], P(('row', 'col')), may hold values from -6 to 6
- hidden: bfloat16 [8192, 256], P(('col', 'row')), may hold values from -6 to 6
- pre_one: bfloat16 [8192, 256], P(('col', 'row')), may hold values from -6 to 6
- features: bfloat16 [8192, 256], P(('row', 'col')), may hold values from -6 to 6
- w_two: bfloat16 [256, 256], replicated, may hold values from -0.375 to 0.375
- w_one: bfloat16 [256, 256], replicated, may hold values from -0.375 to 0.375
Outputs:
- node_grad: bfloat16 [8192, 256], P(('row', 'col'))
- weight_grad_one: float32 [256, 256], replicated
- weight_grad_two: float32 [256, 256], replicated
Inputs may be any that keep to these rules, and one draw needn't show every extreme that they name: adjacency is symmetric and nonnegative. tile_mask is symmetric and every diagonal tile is 1.
All inputs are finite; a program needn't handle non-finite values.
Results may differ from a plain program's by a relative error of at most 0.02.
Values may be sent and summed in bfloat16 or wider, within the bound.
No kernel may reach another device: no remote copies, remote signals or barrier semaphores. Data moves between devices by JAX's collectives and lax.ppermute only.
A program may use at most 128 MiB of HBM per device.

v0:
```python
import jax
import jax.numpy as jnp
from jax import lax
from jax.sharding import PartitionSpec as P


def tile_pick(count, tile_size, tile_total):
    node_ids = lax.broadcasted_iota(jnp.int32, (count, 1), 0)
    tile_ids = lax.broadcasted_iota(jnp.int32, (1, tile_total), 1)
    return (node_ids // tile_size == tile_ids).astype(jnp.bfloat16)


def local(adjacency, tile_mask, out_grad, pre_two, hidden, pre_one, features, w_two, w_one):
    tile_rows, tile_cols = tile_mask.shape
    tile_size = adjacency.shape[0] // tile_rows
    mask_values = tile_mask.astype(jnp.bfloat16)
    shard_nodes = out_grad.shape[0]
    weight_scale = 4.0 * shard_nodes ** (-0.5)
    contract_rows = (((0,), (0,)), ((), ()))
    contract_cols = (((1,), (1,)), ((), ()))
    grad_two = jnp.where(pre_two > 0, out_grad, jnp.zeros_like(out_grad))
    shard_rows = lax.all_gather(grad_two, "col", axis=0, tiled=True)
    count = shard_rows.shape[0]
    strip_rows = adjacency
    picker = tile_pick(count, tile_size, tile_rows)
    strip_mask = jnp.dot(picker, mask_values, preferred_element_type=jnp.float32).astype(
        jnp.bfloat16
    )
    strip_rows = (strip_rows.reshape(count, tile_cols, tile_size) * strip_mask[:, :, None]).reshape(
        count, adjacency.shape[1]
    )
    column_part = lax.dot_general(
        strip_rows, shard_rows, contract_rows, preferred_element_type=jnp.float32
    )
    column_part = column_part.astype(jnp.bfloat16).astype(jnp.float32)
    prop_two = lax.psum_scatter(
        column_part.astype(jnp.bfloat16), "row", scatter_dimension=0, tiled=True
    )
    back_grad = lax.dot_general(prop_two, w_two, contract_cols, preferred_element_type=jnp.float32)
    grad_one = jnp.where(pre_one > 0, back_grad, jnp.zeros_like(back_grad)).astype(jnp.bfloat16)
    shard_rows = lax.all_gather(grad_one, "row", axis=0, tiled=True)
    count = shard_rows.shape[0]
    strip_cols = adjacency
    picker = tile_pick(count, tile_size, tile_cols)
    strip_mask = lax.dot_general(
        mask_values, picker, contract_cols, preferred_element_type=jnp.float32
    ).astype(jnp.bfloat16)
    strip_cols = (strip_cols.reshape(tile_rows, tile_size, count) * strip_mask[:, None, :]).reshape(
        adjacency.shape[0], count
    )
    row_part = jnp.dot(strip_cols, shard_rows, preferred_element_type=jnp.float32)
    term_two = lax.dot_general(hidden, prop_two, contract_rows, preferred_element_type=jnp.float32)
    summed_two = lax.psum(term_two, ("row", "col"))
    row_part = row_part.astype(jnp.bfloat16).astype(jnp.float32)
    prop_one = lax.psum_scatter(
        row_part.astype(jnp.bfloat16), "col", scatter_dimension=0, tiled=True
    )
    term_one = lax.dot_general(
        features, prop_one, contract_rows, preferred_element_type=jnp.float32
    )
    node_grad = lax.dot_general(
        prop_one, w_one, contract_cols, preferred_element_type=jnp.float32
    ).astype(jnp.bfloat16)
    summed_one = lax.psum(term_one, ("row", "col"))
    return (node_grad, summed_one * weight_scale, summed_two * weight_scale)


def solution(mesh):
    return jax.shard_map(
        local,
        mesh=mesh,
        in_specs=(
            P("row", "col"),
            P("row", "col"),
            P(("row", "col"), None),
            P(("row", "col"), None),
            P(("col", "row"), None),
            P(("col", "row"), None),
            P(("row", "col"), None),
            P(),
            P(),
        ),
        out_specs=(P(("row", "col"), None), P(), P()),
        check_vma=False,
    )
```

profile of v0, /device:TPU:0, one launch (start us, length us, event | category | flops | bytes accessed | tf_op | source)
XLA Modules:
  0.0 260.1 jit_solution(17409156216154085595)
XLA Ops:
  7.2 0.0 copy-start
  7.2 0.0 all-gather.2.cloned.1.call-start
  7.2 1.7 compare_select_fusion
  8.9 0.0 all-gather.2.cloned.1.call-update
  8.9 0.0 reduce-scatter.3.cloned.1.call-start
  9.0 1.1 convolution_convert_fusion.1
  10.1 0.3 copy.12
  10.4 24.6 %all-gather.2.cloned.1.call-done = bf16[2048,256]{1,0:T(8,128)(2,1)} async-done(((bf16[256,256]{1,0:T(8,128)(2,1)}), bf16[2048,256]{1,0:T(8,128)(2,1)}) %all-gather.2.cloned.1.call-update) | async-done | bytes 1048592 | tf_op jit(solution)/shard_map/all_gather | solution.py:22
  35.0 0.0 copy-start.1
  35.0 5.8 %mul.31 = bf16[2048,8,128]{2,1,0:T(8,128)(2,1)S(1)} broadcast(bf16[2048,8]{1,0:T(8,128)(2,1)S(1)} %copy.12), dimensions={0,1} | broadcast | bytes 4227072 | tf_op jit(solution)/shard_map/mul | solution.py:29
  40.8 0.0 copy-done.1
  40.8 0.0 copy-start.7
  40.8 4.0 %fusion.2 = bf16[1024,256]{1,0:T(8,128)(2,1)} fusion(bf16[2048,256]{1,0:T(8,128)(2,1)} %all-gather.2.cloned.1.call-done, bf16[2048,1024]{1,0:T(8,128)(2,1)S(1)} %copy-done.1, bf16[256,8,8,128]{3,2,1,0:T(8,128)(2,1)S(1)} %bitcast.25), kind=kOutput, calls=%fused_computation.6 | convolution fusion | flops 1076101120 | bytes 9961472 | tf_op jit(solution)/shard_map/dot_general | solution.py:32
  44.8 0.0 reduce-scatter.3.cloned.1.call-update
  44.9 0.0 reduce-scatter.5.cloned.1.call-start
  44.9 0.0 copy-done.7
  44.9 0.3 fusion.4
  45.3 0.0 copy-start.4
  45.3 4.5 %bitcast_multiply_fusion.2 = bf16[2048,1024]{1,0:T(8,128)(2,1)} fusion(bf16[2048,1024]{1,0:T(8,128)(2,1)} %param.9, bf16[16,1024]{1,0:T(8,128)(2,1)S(1)} %fusion.4), kind=kLoop, calls=%fused_computation.3 | loop fusion | flops 2097152 | bytes 8421376 | tf_op jit(solution)/shard_map/mul | solution.py:48
  49.7 19.7 %reduce-scatter.3.cloned.1.call-done = bf16[256,256]{1,0:T(8,128)(2,1)} async-done(((bf16[1024,256]{1,0:T(8,128)(2,1)}), bf16[256,256]{1,0:T(8,128)(2,1)}) %reduce-scatter.3.cloned.1.call-update) | async-done | bytes 131088 | tf_op jit(solution)/shard_map/reduce_scatter | solution.py:36
  69.4 0.0 copy-done
  69.4 0.0 copy-done.4
  69.4 1.1 fusion.3
  70.6 10.0 %all_gather.7 = bf16[1024,256]{1,0:T(8,128)(2,1)S(1)} all-gather(bf16[256,256]{1,0:T(8,128)(2,1)S(1)} %fusion.3), channel_id=1, replica_groups=mesh['row'=4,'col'=8] {'row'}, dimensions={0}, use_global_device_ids=true | all-gather | bytes 655360 | tf_op jit(solution)/shard_map/all_gather | solution.py:41
  80.5 0.0 copy-start.2
  80.5 0.0 copy-start.5
  80.5 0.0 copy-start.6
  80.5 0.0 copy-start.3
  80.6 4.5 %convolution_convert_fusion = bf16[2048,256]{1,0:T(8,128)(2,1)} fusion(bf16[2048,1024]{1,0:T(8,128)(2,1)} %bitcast_multiply_fusion.2, bf16[1024,256]{1,0:T(8,128)(2,1)S(1)} %all_gather.7), kind=kOutput, calls=%fused_computation.4 | convolution fusion | flops 1074266112 | bytes 5767168 | tf_op jit(solution)/shard_map/dot_general | solution.py:51
  85.0 0.0 reduce-scatter.5.cloned.1.call-update
  85.1 0.0 all-reduce.3.cloned.1.call-start
  85.1 0.0 copy-done.2
  85.1 0.0 copy-done.5
  85.1 0.9 convolution_bitcast_fusion
  86.1 31.4 %reduce-scatter.5.cloned.1.call-done = bf16[256,256]{1,0:T(8,128)(2,1)} async-done(((bf16[2048,256]{1,0:T(8,128)(2,1)}), bf16[256,256]{1,0:T(8,128)(2,1)}) %reduce-scatter.5.cloned.1.call-update) | async-done | bytes 131088 | tf_op jit(solution)/shard_map/reduce_scatter | solution.py:55
  117.4 0.0 copy-done.6
  117.4 1.8 convolution_bitcast_fusion.1
  119.3 0.0 all-reduce.3.cloned.1.call-update
  119.3 0.0 copy-done.3
  119.3 1.8 convolution_convert_fusion.2
  121.1 129.7 %all-reduce.3.cloned.1.call-done = (f32[256,256]{0,1:T(8,128)}, f32[256,256]{0,1:T(8,128)}) async-done(((f32[256,256]{0,1:T(8,128)}, f32[256,256]{0,1:T(8,128)}), (f32[256,256]{0,1:T(8,128)}, f32[256,256]{0,1:T(8,128)})) %all-reduce.3.cloned.1.call-update) | async-done | bytes 524304 | tf_op jit(solution)/shard_map/psum | solution.py:64
  250.8 1.1 broadcast_multiply_fusion
  251.9 0.8 copy.13
  252.7 0.8 copy.14
  (2 shorter events, 0.0 us)
Async XLA Ops:
  7.2 62.3 %copy-start = (bf16[256,256]{1,0:T(8,128)(2,1)S(1)}, bf16[256,256]{1,0:T(8,128)(2,1)}, u32[]{:S(2)}) copy-start(bf16[256,256]{1,0:T(8,128)(2,1)} %param.16) | copy-start | bytes 393220
  7.2 27.8 %all-gather.2.cloned.1.call-start = ((), (), s32[]{:S(2)}) async-start(), calls=%async_computation.2 | async-start | bytes 1179648 | tf_op jit(solution)/shard_map/all_gather | solution.py:22
  8.9 60.5 %reduce-scatter.3.cloned.1.call-start = ((), (), s32[]{:S(2)}) async-start(), calls=%async_computation.3 | async-start | bytes 655360 | tf_op jit(solution)/shard_map/reduce_scatter | solution.py:36
  35.0 5.8 %copy-start.1 = (bf16[2048,1024]{1,0:T(8,128)(2,1)S(1)}, bf16[2048,1024]{1,0:T(8,128)(2,1)}, u32[]{:S(2)}) copy-start(bf16[2048,1024]{1,0:T(8,128)(2,1)} %param.9) | copy-start | bytes 12582916
  40.8 4.1 %copy-start.7 = (s32[16,8]{0,1:T(8,128)S(1)}, s32[16,8]{0,1:T(8,128)}, u32[]{:S(2)}) copy-start(s32[16,8]{0,1:T(8,128)} %param.10) | copy-start | bytes 1540
  44.9 72.6 %reduce-scatter.5.cloned.1.call-start = ((), (), s32[]{:S(2)}) async-start(), calls=%async_computation.4 | async-start | bytes 1179648 | tf_op jit(solution)/shard_map/reduce_scatter | solution.py:55
  45.3 24.2 %copy-start.4 = (bf16[256,256]{1,0:T(8,128)(2,1)S(1)}, bf16[256,256]{1,0:T(8,128)(2,1)}, u32[]{:S(2)}) copy-start(bf16[256,256]{1,0:T(8,128)(2,1)} %param.14) | copy-start | bytes 393220
  80.5 4.6 %copy-start.2 = (bf16[256,256]{1,0:T(8,128)(2,1)S(1)}, bf16[256,256]{1,0:T(8,128)(2,1)}, u32[]{:S(2)}) copy-start(bf16[256,256]{1,0:T(8,128)(2,1)} %reduce-scatter.3.cloned.1.call-done) | copy-start | bytes 393220
  80.5 4.6 %copy-start.5 = (bf16[256,256]{1,0:T(8,128)(2,1)S(1)}, bf16[256,256]{1,0:T(8,128)(2,1)}, u32[]{:S(2)}) copy-start(bf16[256,256]{1,0:T(8,128)(2,1)} %param.13) | copy-start | bytes 393220
  80.5 36.9 %copy-start.6 = (bf16[256,256]{1,0:T(8,128)(2,1)S(1)}, bf16[256,256]{1,0:T(8,128)(2,1)}, u32[]{:S(2)}) copy-start(bf16[256,256]{1,0:T(8,128)(2,1)} %param.15) | copy-start | bytes 393220
  80.5 38.7 %copy-start.3 = (bf16[256,256]{1,0:T(8,128)(2,1)S(1)}, bf16[256,256]{1,0:T(8,128)(2,1)}, u32[]{:S(2)}) copy-start(bf16[256,256]{1,0:T(8,128)(2,1)} %param.17) | copy-start | bytes 393220
  85.1 165.7 %all-reduce.3.cloned.1.call-start = ((), (), s32[]{:S(2)}) async-start(), calls=%async_computation.5 | async-start | bytes 1048576 | tf_op jit(solution)/shard_map/psum | solution.py:64
Sparse Core Ops, SparseCore 0:
  10.2 24.7 all-gather.1
  45.0 24.4 reduce-scatter.2
  85.2 32.2 reduce-scatter.4
  124.2 126.5 all-reduce.2
where the time goes:
time: 260 us
  waiting for transfers between devices  205 us (79%)
  matrix products  15.6 us (6%)
  between operations  13.9 us (5%)
  blocking collectives  9.96 us (4%)
  local copies, waits for them, and re-layouts  7.75 us (3%)
  other arithmetic  7.2 us (3%)
    psum x1, waiting for transfers between devices, local(): summed_one = lax.psum(term_one, ('row', 'col'))  130 us
    reduce_scatter x1, waiting for transfers between devices, local(): lax.psum_scatter(row_part.astype(jnp.bfloat16), 'col', scatter_dimension=...  31.4 us
    all_gather x1, waiting for transfers between devices, local(): shard_rows = lax.all_gather(grad_two, 'col', axis=0, tiled=True)  24.6 us
    reduce_scatter x1, waiting for transfers between devices, local(): lax.psum_scatter(column_part.astype(jnp.bfloat16), 'row', scatter_dimensi...  19.7 us
    all_gather x1, blocking collectives, local(): shard_rows = lax.all_gather(grad_one, 'row', axis=0, tiled=True)  9.96 us
    mul x1, local copies, waits for them, and re-layouts, local(): strip_rows.reshape(count, tile_cols, tile_size) * strip_mask[:, :, None]  5.76 us
  transfers between devices with their start and end apart: 4, of which 4 were waited for; matrix products, arithmetic and copies ran while one was open for 3% of the time, Pallas kernels for 0%

commit v1 on v0

v1 whole, which is shorter than its diff:
```python
import functools

import jax
import jax.numpy as jnp
from jax import lax
from jax.experimental import pallas as pl
from jax.experimental.pallas import tpu as pltpu
from jax.sharding import PartitionSpec as P

BF16, F32 = jnp.bfloat16, jnp.float32
ROWS_COLS = (((0,), (0,)), ((), ()))
LAST_LAST = (((1,), (1,)), ((), ()))
VMEM = pltpu.VMEM


def params():
    return pltpu.CompilerParams(vmem_limit_bytes=40 * 1024 * 1024)


def cost(flops, bytes_accessed):
    return pl.CostEstimate(flops=flops, bytes_accessed=bytes_accessed, transcendentals=0)


def whole(count):
    return [pl.BlockSpec(memory_space=VMEM) for _ in range(count)]


def tree(values):
    while len(values) > 1:
        values = [a + b for a, b in zip(values[::2], values[1::2])]
    return values[0]


def mask_kernel(block, tile, row_src, col_src, mask, adj, plain, turned):
    step = pl.program_id(0)
    per = block // tile
    row = row_src[step]
    for slot in range(adj.shape[1] // block):
        col = col_src[slot]
        for v in range(per):
            part = adj[:, pl.ds(pl.multiple_of((col * per + v) * tile, tile), tile)]
            for u in range(per):
                keep = mask[row * per + u, col * per + v].astype(F32).astype(BF16)
                kept = part[u * tile : (u + 1) * tile] * keep
                lanes = slice(slot * block + v * tile, slot * block + (v + 1) * tile)
                plain[u * tile : (u + 1) * tile, lanes] = kept
                turned[lanes, u * tile : (u + 1) * tile] = kept.T


def masked(adjacency, tile_mask, row_src, col_src, block):
    rows, cols = adjacency.shape
    tile = rows // tile_mask.shape[0]
    return pl.pallas_call(
        functools.partial(mask_kernel, block, tile),
        grid_spec=pltpu.PrefetchScalarGridSpec(
            num_scalar_prefetch=3,
            grid=(rows // block,),
            in_specs=[pl.BlockSpec((block, cols), lambda s, row_src, *_: (row_src[s], 0))],
            out_specs=[
                pl.BlockSpec((block, cols), lambda s, *_: (s, 0)),
                pl.BlockSpec((cols, block), lambda s, *_: (0, s)),
            ],
        ),
        out_shape=[
            jax.ShapeDtypeStruct((rows, cols), BF16),
            jax.ShapeDtypeStruct((cols, rows), BF16),
        ],
        compiler_params=params(),
        cost_estimate=cost(rows * cols, 6 * rows * cols),
        name="mask_tiles",
    )(row_src, col_src, tile_mask, adjacency)


def spread_kernel(count, turned, *refs):
    parts, out, held = refs[:count], refs[count], refs[count + 1]
    block = parts[0].shape[0]

    @pl.when(pl.program_id(0) == 0)
    def _():
        for slot, part in enumerate(parts):
            held[slot * block : (slot + 1) * block] = part[...]

    out[0] = jnp.dot(turned[...], held[...], preferred_element_type=F32).astype(BF16)


def spread(graph, parts):
    block, width = parts[0].shape
    rows, cols = graph.shape
    return pl.pallas_call(
        functools.partial(spread_kernel, len(parts)),
        grid=(rows // block,),
        in_specs=[pl.BlockSpec((block, cols), lambda s: (s, 0))]
        + [pl.BlockSpec((block, width), lambda s: (0, 0)) for _ in parts],
        out_specs=pl.BlockSpec((1, block, width), lambda s: (s, 0, 0)),
        out_shape=jax.ShapeDtypeStruct((rows // block, block, width), BF16),
        scratch_shapes=[VMEM((cols, width), BF16)],
        compiler_params=params(),
        cost_estimate=cost(2 * rows * cols * width, 2 * rows * cols),
        name="propagate",
    )(graph, *parts)


def middle_kernel(count, *refs):
    parts, w_two, pre_one = refs[:count], refs[count], refs[count + 1]
    prop, grad = refs[count + 2 :]
    total = tree([part[...].astype(F32) for part in parts]).astype(BF16)
    prop[...] = total
    back = lax.dot_general(total, w_two[...], LAST_LAST, preferred_element_type=F32)
    grad[...] = jnp.where(pre_one[...] > 0, back, 0.0).astype(BF16)


def middle(parts, w_two, pre_one):
    shape = jax.ShapeDtypeStruct(pre_one.shape, BF16)
    return pl.pallas_call(
        functools.partial(middle_kernel, len(parts)),
        in_specs=whole(len(parts) + 2),
        out_specs=whole(2),
        out_shape=[shape, shape],
        compiler_params=params(),
        name="first_layer_gradient",
    )(*parts, w_two, pre_one)


def last_kernel(count, *refs):
    parts, w_one, out = refs[:count], refs[count], refs[count + 1]
    total = tree([part[...].astype(F32) for part in parts]).astype(BF16)
    out[...] = lax.dot_general(
        total, w_one[...], LAST_LAST, preferred_element_type=F32
    ).astype(BF16)


def last(parts, w_one):
    return pl.pallas_call(
        functools.partial(last_kernel, len(parts)),
        in_specs=whole(len(parts) + 1),
        out_specs=pl.BlockSpec(memory_space=VMEM),
        out_shape=jax.ShapeDtypeStruct(parts[0].shape, BF16),
        compiler_params=params(),
        name="node_gradient",
    )(*parts, w_one)


def local(n_row, n_col, adjacency, tile_mask, out_grad, pre_two, hidden, pre_one, features, w_two, w_one):
    block = out_grad.shape[0]
    scale = 4.0 * block ** (-0.5)
    n_far = n_col // 2
    row, col = lax.axis_index("row"), lax.axis_index("col")

    def over_col(value, flip):
        return lax.ppermute(value, "col", [(i, i ^ flip) for i in range(n_col)])

    def over_row(value, flip):
        return lax.ppermute(value, "row", [(i, i ^ flip) for i in range(n_row)])

    def far(value):
        return [value] + [over_col(value, 2 * j) for j in range(1, n_far)]

    def rows_all(value):
        return [value] + [over_row(value, i) for i in range(1, n_row)]

    row_src = jnp.bitwise_xor(jnp.arange(n_col, dtype=jnp.int32), col)
    col_src = jnp.bitwise_xor(jnp.arange(n_row, dtype=jnp.int32), row)

    grad_two = jnp.where(pre_two > 0, out_grad, jnp.zeros_like(out_grad))
    near = far(grad_two)
    plain, turned = masked(adjacency, tile_mask, row_src, col_src, block)
    others = [over_col(value, 1) for value in near]
    second = [value for pair in zip(near, others) for value in pair]
    column_part = spread(turned, second)
    parts = [column_part[0]] + [over_row(column_part[i], i) for i in range(1, n_row)]
    prop_two, grad_one = middle(parts, w_two, pre_one)
    first = rows_all(grad_one)

    near_features = far(features)
    other_features = [over_col(value, 1) for value in near_features]
    term_two = lax.dot_general(hidden, prop_two, ROWS_COLS, preferred_element_type=F32)

    row_part = spread(plain, first)
    row_part = row_part.reshape(n_far, 2, block, -1)
    crossed = over_col(row_part[:, 1], 1)
    chip_part = row_part[:, 0].astype(F32) + crossed.astype(F32)
    chip_part = chip_part.astype(BF16)
    ends = [chip_part[0]] + [over_col(chip_part[j], 2 * j) for j in range(1, n_far)]
    node_grad = last(ends, w_one)

    row_features = jnp.stack([value for pair in zip(near_features, other_features) for value in pair])
    term_one = lax.dot_general(
        row_features.reshape(n_col * block, -1),
        row_part.reshape(n_col * block, -1),
        ROWS_COLS,
        preferred_element_type=F32,
    )
    terms = jnp.stack([term_one, term_two]).astype(BF16)
    half = terms.shape[1] // 2
    odd = col % 2 == 1
    mine = jnp.where(odd, terms[:, half:], terms[:, :half])
    yours = jnp.where(odd, terms[:, :half], terms[:, half:])
    total = (mine.astype(F32) + over_col(yours, 1).astype(F32)).astype(BF16)
    total = tree([value.astype(F32) for value in rows_all(total)]).astype(BF16)
    total = tree([value.astype(F32) for value in far(total)]) * scale
    other = over_col(total, 1)
    total = jnp.concatenate([jnp.where(odd, other, total), jnp.where(odd, total, other)], axis=1)
    return node_grad, total[0], total[1]


def solution(mesh):
    return jax.shard_map(
        functools.partial(local, mesh.shape["row"], mesh.shape["col"]),
        mesh=mesh,
        in_specs=(
            P("row", "col"),
            P("row", "col"),
            P(("row", "col"), None),
            P(("row", "col"), None),
            P(("col", "row"), None),
            P(("col", "row"), None),
            P(("row", "col"), None),
            P(),
            P(),
        ),
        out_specs=(P(("row", "col"), None), P(), P()),
        check_vma=False,
    )
```

time: 260 us -> 95.7 us (0.37)
  waiting for transfers between devices: 205 us -> 47.1 us
  starting transfers between devices: 0.16 us -> 31.3 us
  matrix products: 15.6 us -> 0.66 us
  between operations: 13.9 us -> 0.97 us
  blocking collectives: 9.96 us -> 0 us
  Pallas kernels: 0 us -> 9.03 us
  other arithmetic: 7.2 us -> 2.27 us
  local copies, waits for them, and re-layouts: 7.75 us -> 4.17 us
    psum x1 -> x0, waiting for transfers between devices: 130 us -> none  [local(): summed_one = lax.psum(term_one, ('row', 'col'))]
    reduce_scatter x2 -> x0, waiting for transfers between devices: 51.1 us -> none  [the longest x1 31.4 us: local(): lax.psum_scatter(row_part.astype(jnp.bfloat16), 'col', scatter_dimension=...]
    ppermute x0 -> x32, waiting for transfers between devices: none -> 47.1 us  [the longest x23 30.1 us: over_col(): return lax.ppermute(value, 'col', [(i, i ^ flip) for i in range(n_col)])]
    ppermute x0 -> x32, starting transfers between devices: none -> 31.3 us  [the longest x23 20.6 us: over_col(): return lax.ppermute(value, 'col', [(i, i ^ flip) for i in range(n_col)])]
    all_gather x1 -> x0, waiting for transfers between devices: 24.6 us -> none  [local(): shard_rows = lax.all_gather(grad_two, 'col', axis=0, tiled=True)]
    dot_general x8 -> x2, matrix products: 15.6 us -> 0.66 us  [the longest x1 0.44 us: local(): lax.dot_general(row_features.reshape(n_col * block, -1), row_part.reshape...]
    all_gather x1 -> x0, blocking collectives: 9.96 us -> none  [local(): shard_rows = lax.all_gather(grad_one, 'row', axis=0, tiled=True)]
    pallas_call x0 -> x5, Pallas kernels: none -> 9.03 us  [the longest x2 4.39 us: spread(): pl.pallas_call(functools.partial(spread_kernel, len(parts)), grid=(rows /...]
  transfers between devices with their start and end apart: 4 -> 32, of which waited for: 4 -> 13; matrix products, arithmetic and copies ran while one was open for 3% -> 3% of each run, Pallas kernels for 0% -> 7%
where the time goes in v1:
time: 95.7 us; the launch traced here: 95.5 us
  waiting for transfers between devices  47.1 us (49%)
  starting transfers between devices  31.3 us (33%)
  Pallas kernels  9.03 us (9%)
  local copies, waits for them, and re-layouts  4.17 us (4%)
  other arithmetic  2.27 us (2%)
  between operations  0.97 us (1%)
    ppermute x23, waiting for transfers between devices, over_col(): return lax.ppermute(value, 'col', [(i, i ^ flip) for i in range(n_col)])  30.1 us
    ppermute x23, starting transfers between devices, over_col(): return lax.ppermute(value, 'col', [(i, i ^ flip) for i in range(n_col)])  20.6 us
    ppermute x9, waiting for transfers between devices, over_row(): return lax.ppermute(value, 'row', [(i, i ^ flip) for i in range(n_row)])  17 us
    ppermute x9, starting transfers between devices, over_row(): return lax.ppermute(value, 'row', [(i, i ^ flip) for i in range(n_row)])  10.7 us
    pallas_call x2, Pallas kernels, spread(): pl.pallas_call(functools.partial(spread_kernel, len(parts)), grid=(rows /...  4.39 us
    unnamed x19, local copies, waits for them, and re-layouts  4.05 us
    pallas_call x1, Pallas kernels, masked(): pl.pallas_call(functools.partial(mask_kernel, block, tile), grid_spec=plt...  3.53 us
  transfers between devices with their start and end apart: 32, of which 13 were waited for; matrix products, arithmetic and copies ran while one was open for 3% of the time, Pallas kernels for 7%

profile of v1, /device:TPU:0, one launch (start us, length us, event | category | flops | bytes accessed | tf_op | source)
XLA Modules:
  0.0 95.5 jit_solution(5680458717560125856)
XLA Ops:
  0.6 1.0 %compare_select_fusion.refs_0_ = bf16[256,256]{1,0:T(8,128)(2,1)S(1)} fusion(bf16[256,256]{1,0:T(8,128)(2,1)} %param.11, bf16[256,256]{1,0:T(8,128)(2,1)} %param.12), kind=kLoop, calls=%fused_computation.20 | loop fusion | flops 131072 | bytes 393216 | tf_op jit(solution)/shard_map/jit(_where)/select_n | solution.py:164
  1.7 0.5 collective-permute-start
  2.2 2.6 %collective-permute-start.1 = (bf16[256,256]{1,0:T(8,128)(2,1)S(1)}, bf16[256,256]{1,0:T(8,128)(2,1)S(1)}, u32[]{:S(2)}, u32[]{:S(2)}) collective-permute-start(bf16[256,256]{1,0:T(8,128)(2,1)S(1)} %compare_select_fusion.refs_0_), channel_id=1, source_target_pairs={{0,2},{1,3},{2,0},{3,1},{4,6},{5,7},{6,4},{7,5},{8,10},{9,11},{10,... | collective-permute-start | bytes 393224 | tf_op jit(solution)/shard_map/ppermute | solution.py:150
  4.8 2.6 %collective-permute-start.3 = (bf16[256,256]{1,0:T(8,128)(2,1)S(1)}, bf16[256,256]{1,0:T(8,128)(2,1)S(1)}, u32[]{:S(2)}, u32[]{:S(2)}) collective-permute-start(bf16[256,256]{1,0:T(8,128)(2,1)S(1)} %compare_select_fusion.refs_0_), channel_id=1, source_target_pairs={{0,4},{1,5},{2,6},{3,7},{4,0},{5,1},{6,2},{7,3},{8,12},{9,13},{10,... | collective-permute-start | bytes 393224 | tf_op jit(solution)/shard_map/ppermute | solution.py:150
  7.4 1.0 %copy.21 = bf16[256,256]{0,1:T(8,128)(2,1)S(1)} copy(bf16[256,256]{1,0:T(8,128)(2,1)} %param.15) | data formatting | bytes 262144 | tf_op args[6]
  8.6 0.8 copy.18.mask
  9.3 2.2 %copy-done.1 = bf16[2048,1024]{1,0:T(8,128)(2,1)S(1)} copy-done((bf16[2048,1024]{1,0:T(8,128)(2,1)S(1)}, bf16[2048,1024]{1,0:T(8,128)(2,1)}, u32[]{:S(2)}) %copy-start.1) | copy-done | bytes 4194328
  11.5 3.5 %mask_tiles.1 = (bf16[2048,1024]{1,0:T(8,128)(2,1)S(1)}, bf16[1024,2048]{1,0:T(8,128)(2,1)S(1)}) custom-call(s32[8]{0:T(128)S(1)} %iota_xor_fusion.1.row_src, s32[4]{0:T(128)S(1)} %iota_xor_fusion.col_src, s32[16,8]{1,0:T(8,128)S(1)} %copy.18.mask, bf16[2048,1024]{1,0:T(8,128)(2,1)S(1)} %copy-done.1), custom_call_target="tpu_custom_call" | custom-call | flops 2097152 | bytes 12582912 | tf_op jit(solution)/shard_map/mask_tiles/pallas_call | solution.py:53
  15.1 1.0 %collective-permute-start.18 = (bf16[256,256]{0,1:T(8,128)(2,1)S(1)}, bf16[256,256]{0,1:T(8,128)(2,1)S(1)}, u32[]{:S(2)}, u32[]{:S(2)}) collective-permute-start(bf16[256,256]{0,1:T(8,128)(2,1)S(1)} %copy.21), channel_id=1, source_target_pairs={{0,2},{1,3},{2,0},{3,1},{4,6},{5,7},{6,4},{7,5},{8,10},{9,11},{10,... | collective-permute-start | bytes 393224 | tf_op jit(solution)/shard_map/ppermute | solution.py:150
  16.1 3.6 %collective-permute-start.20 = (bf16[256,256]{0,1:T(8,128)(2,1)S(1)}, bf16[256,256]{0,1:T(8,128)(2,1)S(1)}, u32[]{:S(2)}, u32[]{:S(2)}) collective-permute-start(bf16[256,256]{0,1:T(8,128)(2,1)S(1)} %copy.21), channel_id=1, source_target_pairs={{0,4},{1,5},{2,6},{3,7},{4,0},{5,1},{6,2},{7,3},{8,12},{9,13},{10,... | collective-permute-start | bytes 393224 | tf_op jit(solution)/shard_map/ppermute | solution.py:150
  19.7 0.5 collective-permute-start.4
  20.2 3.2 %collective-permute-done.18 = bf16[256,256]{0,1:T(8,128)(2,1)S(1)} collective-permute-done((bf16[256,256]{0,1:T(8,128)(2,1)S(1)}, bf16[256,256]{0,1:T(8,128)(2,1)S(1)}, u32[]{:S(2)}, u32[]{:S(2)}) %collective-permute-start.18) | collective-permute-done | bytes 131104 | tf_op jit(solution)/shard_map/ppermute | solution.py:150
  23.5 6.1 %collective-permute-done.20 = bf16[256,256]{0,1:T(8,128)(2,1)S(1)} collective-permute-done((bf16[256,256]{0,1:T(8,128)(2,1)S(1)}, bf16[256,256]{0,1:T(8,128)(2,1)S(1)}, u32[]{:S(2)}, u32[]{:S(2)}) %collective-permute-start.20) | collective-permute-done | bytes 131104 | tf_op jit(solution)/shard_map/ppermute | solution.py:150
  29.6 0.5 collective-permute-start.21
  30.2 1.9 %propagate.2 = bf16[4,256,256]{2,1,0:T(8,128)(2,1)S(1)} custom-call(bf16[1024,2048]{1,0:T(8,128)(2,1)S(1)} %get-tuple-element.8.turned, bf16[256,256]{1,0:T(8,128)(2,1)S(1)} %compare_select_fusion.refs_0_, bf16[256,256]{1,0:T(8,128)(2,1)S(1)} %collective-permute-done.refs_1_, bf16[256,256]{1,0:T(8,128)(2,1)S(1)} %collective-permute-done.1.refs_2_, ...), custom_call_target="tpu_custom_call" | custom-call | flops 1073741824 | bytes 4194304 | tf_op jit(solution)/shard_map/propagate/pallas_call | solution.py:89
  32.1 1.5 %collective-permute-start.7 = (bf16[256,256]{1,0:T(8,128)(2,1)S(1)}, bf16[256,256]{1,0:T(8,128)(2,1)S(1)}, u32[]{:S(2)}, u32[]{:S(2)}) collective-permute-start(bf16[256,256]{1,0:T(8,128)(2,1)S(1)} %get-tuple-element.21), channel_id=1, source_target_pairs={{0,8},{8,0},{16,24},{24,16},{1,9},{9,1},{17,25},{25,17},{2,10},{10... | collective-permute-start | bytes 393224 | tf_op jit(solution)/shard_map/ppermute | solution.py:153
  33.6 1.5 %collective-permute-start.8 = (bf16[256,256]{1,0:T(8,128)(2,1)S(1)}, bf16[256,256]{1,0:T(8,128)(2,1)S(1)}, u32[]{:S(2)}, u32[]{:S(2)}) collective-permute-start(bf16[256,256]{1,0:T(8,128)(2,1)S(1)} %get-tuple-element.20), channel_id=1, source_target_pairs={{0,16},{8,24},{16,0},{24,8},{1,17},{9,25},{17,1},{25,9},{2,18},{10... | collective-permute-start | bytes 393224 | tf_op jit(solution)/shard_map/ppermute | solution.py:153
  35.1 0.5 collective-permute-start.9
  35.7 2.7 %collective-permute-done.7.refs_1_ = bf16[256,256]{1,0:T(8,128)(2,1)S(1)} collective-permute-done((bf16[256,256]{1,0:T(8,128)(2,1)S(1)}, bf16[256,256]{1,0:T(8,128)(2,1)S(1)}, u32[]{:S(2)}, u32[]{:S(2)}) %collective-permute-start.7) | collective-permute-done | bytes 131104 | tf_op jit(solution)/shard_map/ppermute | solution.py:153
  38.4 3.5 %collective-permute-done.8.refs_2_ = bf16[256,256]{1,0:T(8,128)(2,1)S(1)} collective-permute-done((bf16[256,256]{1,0:T(8,128)(2,1)S(1)}, bf16[256,256]{1,0:T(8,128)(2,1)S(1)}, u32[]{:S(2)}, u32[]{:S(2)}) %collective-permute-start.8) | collective-permute-done | bytes 131104 | tf_op jit(solution)/shard_map/ppermute | solution.py:153
  42.0 0.2 first_layer_gradient.1
  42.2 1.3 %collective-permute-start.10 = (bf16[256,256]{1,0:T(8,128)(2,1)S(1)}, bf16[256,256]{1,0:T(8,128)(2,1)S(1)}, u32[]{:S(2)}, u32[]{:S(2)}) collective-permute-start(bf16[256,256]{1,0:T(8,128)(2,1)S(1)} %get-tuple-element.9.refs_0_), channel_id=1, source_target_pairs={{0,8},{8,0},{16,24},{24,16},{1,9},{9,1},{17,25},{25,17},{2,10},{10... | collective-permute-start | bytes 393224 | tf_op jit(solution)/shard_map/ppermute | solution.py:153
  43.5 0.8 collective-permute-start.11
  44.3 1.4 %collective-permute-start.12 = (bf16[256,256]{1,0:T(8,128)(2,1)S(1)}, bf16[256,256]{1,0:T(8,128)(2,1)S(1)}, u32[]{:S(2)}, u32[]{:S(2)}) collective-permute-start(bf16[256,256]{1,0:T(8,128)(2,1)S(1)} %get-tuple-element.9.refs_0_), channel_id=1, source_target_pairs={{0,24},{8,16},{16,8},{24,0},{1,25},{9,17},{17,9},{25,1},{2,26},{10... | collective-permute-start | bytes 393224 | tf_op jit(solution)/shard_map/ppermute | solution.py:153
  45.8 0.2 fusion.1
  46.0 1.8 %collective-permute-done.10.refs_1_ = bf16[256,256]{1,0:T(8,128)(2,1)S(1)} collective-permute-done((bf16[256,256]{1,0:T(8,128)(2,1)S(1)}, bf16[256,256]{1,0:T(8,128)(2,1)S(1)}, u32[]{:S(2)}, u32[]{:S(2)}) %collective-permute-start.10) | collective-permute-done | bytes 131104 | tf_op jit(solution)/shard_map/ppermute | solution.py:153
  47.8 3.3 %collective-permute-done.11.refs_2_ = bf16[256,256]{1,0:T(8,128)(2,1)S(1)} collective-permute-done((bf16[256,256]{1,0:T(8,128)(2,1)S(1)}, bf16[256,256]{1,0:T(8,128)(2,1)S(1)}, u32[]{:S(2)}, u32[]{:S(2)}) %collective-permute-start.11) | collective-permute-done | bytes 131104 | tf_op jit(solution)/shard_map/ppermute | solution.py:153
  51.1 2.5 %propagate.3 = bf16[8,256,256]{2,1,0:T(8,128)(2,1)S(1)} custom-call(bf16[2048,1024]{1,0:T(8,128)(2,1)S(1)} %get-tuple-element.7.turned, bf16[256,256]{1,0:T(8,128)(2,1)S(1)} %get-tuple-element.9.refs_0_, bf16[256,256]{1,0:T(8,128)(2,1)S(1)} %collective-permute-done.10.refs_1_, bf16[256,256]{1,0:T(8,128)(2,1)S(1)} %collective-permute-done.11.refs_2_, ...), custom_call_target="tpu_custom_call" | custom-call | flops 1073741824 | bytes 4194304 | tf_op jit(solution)/shard_map/propagate/pallas_call | solution.py:89
  53.6 0.4 fusion.2
  54.2 1.3 %collective-permute-done.24 = bf16[2,128,256]{2,1,0:T(8,128)(2,1)S(1)} collective-permute-done((bf16[2,128,256]{2,1,0:T(8,128)(2,1)S(1)}, bf16[2,128,256]{2,1,0:T(8,128)(2,1)S(1)}, u32[]{:S(2)}, u32[]{:S(2)}) %collective-permute-start.24) | collective-permute-done | bytes 131104 | tf_op jit(solution)/shard_map/ppermute | solution.py:150
  55.6 1.7 %collective-permute-start.27 = (bf16[2,128,256]{2,1,0:T(8,128)(2,1)S(1)}, bf16[2,128,256]{2,1,0:T(8,128)(2,1)S(1)}, u32[]{:S(2)}, u32[]{:S(2)}) collective-permute-start(bf16[2,128,256]{2,1,0:T(8,128)(2,1)S(1)} %add_convert_fusion.1), channel_id=1, source_target_pairs={{0,24},{8,16},{16,8},{24,0},{1,25},{9,17},{17,9},{25,1},{2,26},{10... | collective-permute-start | bytes 393224 | tf_op jit(solution)/shard_map/ppermute | solution.py:153
  57.3 0.8 collective-permute-start.26
  58.1 1.0 %collective-permute-start.25 = (bf16[2,128,256]{2,1,0:T(8,128)(2,1)S(1)}, bf16[2,128,256]{2,1,0:T(8,128)(2,1)S(1)}, u32[]{:S(2)}, u32[]{:S(2)}) collective-permute-start(bf16[2,128,256]{2,1,0:T(8,128)(2,1)S(1)} %add_convert_fusion.1), channel_id=1, source_target_pairs={{0,8},{8,0},{16,24},{24,16},{1,9},{9,1},{17,25},{25,17},{2,10},{10... | collective-permute-start | bytes 393224 | tf_op jit(solution)/shard_map/ppermute | solution.py:153
  59.3 3.6 %collective-permute-done.27 = bf16[2,128,256]{2,1,0:T(8,128)(2,1)S(1)} collective-permute-done((bf16[2,128,256]{2,1,0:T(8,128)(2,1)S(1)}, bf16[2,128,256]{2,1,0:T(8,128)(2,1)S(1)}, u32[]{:S(2)}, u32[]{:S(2)}) %collective-permute-start.27) | collective-permute-done | bytes 131104 | tf_op jit(solution)/shard_map/ppermute | solution.py:153
  62.9 2.0 %collective-permute-done.26 = bf16[2,128,256]{2,1,0:T(8,128)(2,1)S(1)} collective-permute-done((bf16[2,128,256]{2,1,0:T(8,128)(2,1)S(1)}, bf16[2,128,256]{2,1,0:T(8,128)(2,1)S(1)}, u32[]{:S(2)}, u32[]{:S(2)}) %collective-permute-start.26) | collective-permute-done | bytes 131104 | tf_op jit(solution)/shard_map/ppermute | solution.py:153
  64.9 0.1 add_convert_fusion
  65.0 2.4 %collective-permute-start.30 = (bf16[2,128,256]{2,1,0:T(8,128)(2,1)S(1)}, bf16[2,128,256]{2,1,0:T(8,128)(2,1)S(1)}, u32[]{:S(2)}, u32[]{:S(2)}) collective-permute-start(bf16[2,128,256]{2,1,0:T(8,128)(2,1)S(1)} %add_convert_fusion), channel_id=1, source_target_pairs={{0,6},{1,7},{2,4},{3,5},{4,2},{5,3},{6,0},{7,1},{8,14},{9,15},{10,... | collective-permute-start | bytes 393224 | tf_op jit(solution)/shard_map/ppermute | solution.py:150
  67.5 1.1 %collective-permute-start.29 = (bf16[2,128,256]{2,1,0:T(8,128)(2,1)S(1)}, bf16[2,128,256]{2,1,0:T(8,128)(2,1)S(1)}, u32[]{:S(2)}, u32[]{:S(2)}) collective-permute-start(bf16[2,128,256]{2,1,0:T(8,128)(2,1)S(1)} %add_convert_fusion), channel_id=1, source_target_pairs={{0,4},{1,5},{2,6},{3,7},{4,0},{5,1},{6,2},{7,3},{8,12},{9,13},{10,... | collective-permute-start | bytes 393224 | tf_op jit(solution)/shard_map/ppermute | solution.py:150
  68.5 0.9 collective-permute-start.28
  69.5 3.9 %collective-permute-done.30 = bf16[2,128,256]{2,1,0:T(8,128)(2,1)S(1)} collective-permute-done((bf16[2,128,256]{2,1,0:T(8,128)(2,1)S(1)}, bf16[2,128,256]{2,1,0:T(8,128)(2,1)S(1)}, u32[]{:S(2)}, u32[]{:S(2)}) %collective-permute-start.30) | collective-permute-done | bytes 131104 | tf_op jit(solution)/shard_map/ppermute | solution.py:150
  73.3 7.0 %collective-permute-done.29 = bf16[2,128,256]{2,1,0:T(8,128)(2,1)S(1)} collective-permute-done((bf16[2,128,256]{2,1,0:T(8,128)(2,1)S(1)}, bf16[2,128,256]{2,1,0:T(8,128)(2,1)S(1)}, u32[]{:S(2)}, u32[]{:S(2)}) %collective-permute-start.29) | collective-permute-done | bytes 131104 | tf_op jit(solution)/shard_map/ppermute | solution.py:150
  80.5 0.1 fusion.3
  80.8 2.9 %collective-permute-start.15 = (bf16[256,256]{1,0:T(8,128)(2,1)S(1)}, bf16[256,256]{1,0:T(8,128)(2,1)S(1)}, u32[]{:S(2)}, u32[]{:S(2)}) collective-permute-start(bf16[256,256]{1,0:T(8,128)(2,1)S(1)} %get-tuple-element.16), channel_id=1, source_target_pairs={{0,4},{1,5},{2,6},{3,7},{4,0},{5,1},{6,2},{7,3},{8,12},{9,13},{10,... | collective-permute-start | bytes 393224 | tf_op jit(solution)/shard_map/ppermute | solution.py:150
  83.7 1.5 %collective-permute-start.16 = (bf16[256,256]{1,0:T(8,128)(2,1)S(1)}, bf16[256,256]{1,0:T(8,128)(2,1)S(1)}, u32[]{:S(2)}, u32[]{:S(2)}) collective-permute-start(bf16[256,256]{1,0:T(8,128)(2,1)S(1)} %get-tuple-element.15), channel_id=1, source_target_pairs={{0,6},{1,7},{2,4},{3,5},{4,2},{5,3},{6,0},{7,1},{8,14},{9,15},{10,... | collective-permute-start | bytes 393224 | tf_op jit(solution)/shard_map/ppermute | solution.py:150
  85.2 4.0 %collective-permute-done.14.refs_1_ = bf16[256,256]{1,0:T(8,128)(2,1)S(1)} collective-permute-done((bf16[256,256]{1,0:T(8,128)(2,1)S(1)}, bf16[256,256]{1,0:T(8,128)(2,1)S(1)}, u32[]{:S(2)}, u32[]{:S(2)}) %collective-permute-start.14) | collective-permute-done | bytes 131104 | tf_op jit(solution)/shard_map/ppermute | solution.py:150
  89.1 4.6 %collective-permute-done.15.refs_2_ = bf16[256,256]{1,0:T(8,128)(2,1)S(1)} collective-permute-done((bf16[256,256]{1,0:T(8,128)(2,1)S(1)}, bf16[256,256]{1,0:T(8,128)(2,1)S(1)}, u32[]{:S(2)}, u32[]{:S(2)}) %collective-permute-start.15) | collective-permute-done | bytes 131104 | tf_op jit(solution)/shard_map/ppermute | solution.py:150
  93.7 0.9 node_gradient.1
  94.7 0.8 fusion.6
  (56 shorter events, 1.0 us)
Async XLA Ops:
  0.6 45.1 %copy-start = (bf16[256,256]{1,0:T(8,128)(2,1)S(1)}, bf16[256,256]{1,0:T(8,128)(2,1)}, u32[]{:S(2)}) copy-start(bf16[256,256]{1,0:T(8,128)(2,1)} %param.13) | copy-start | bytes 393220
  1.7 14.4 %collective-permute-start = (bf16[256,256]{1,0:T(8,128)(2,1)S(1)}, bf16[256,256]{1,0:T(8,128)(2,1)S(1)}, u32[]{:S(2)}, u32[]{:S(2)}) collective-permute-start(bf16[256,256]{1,0:T(8,128)(2,1)S(1)} %compare_select_fusion.refs_0_), channel_id=1, source_target_pairs={{0,1},{1,0},{2,3},{3,2},{4,5},{5,4},{6,7},{7,6},{8,9},{9,8},{10,11... | collective-permute-start | bytes 393224 | tf_op jit(solution)/shard_map/ppermute | solution.py:150
  2.2 17.4 %collective-permute-start.1 = (bf16[256,256]{1,0:T(8,128)(2,1)S(1)}, bf16[256,256]{1,0:T(8,128)(2,1)S(1)}, u32[]{:S(2)}, u32[]{:S(2)}) collective-permute-start(bf16[256,256]{1,0:T(8,128)(2,1)S(1)} %compare_select_fusion.refs_0_), channel_id=1, source_target_pairs={{0,2},{1,3},{2,0},{3,1},{4,6},{5,7},{6,4},{7,5},{8,10},{9,11},{10,... | collective-permute-start | bytes 393224 | tf_op jit(solution)/shard_map/ppermute | solution.py:150
  4.8 14.8 %collective-permute-start.3 = (bf16[256,256]{1,0:T(8,128)(2,1)S(1)}, bf16[256,256]{1,0:T(8,128)(2,1)S(1)}, u32[]{:S(2)}, u32[]{:S(2)}) collective-permute-start(bf16[256,256]{1,0:T(8,128)(2,1)S(1)} %compare_select_fusion.refs_0_), channel_id=1, source_target_pairs={{0,4},{1,5},{2,6},{3,7},{4,0},{5,1},{6,2},{7,3},{8,12},{9,13},{10,... | collective-permute-start | bytes 393224 | tf_op jit(solution)/shard_map/ppermute | solution.py:150
  7.4 12.3 %collective-permute-start.5 = (bf16[256,256]{1,0:T(8,128)(2,1)S(1)}, bf16[256,256]{1,0:T(8,128)(2,1)S(1)}, u32[]{:S(2)}, u32[]{:S(2)}) collective-permute-start(bf16[256,256]{1,0:T(8,128)(2,1)S(1)} %compare_select_fusion.refs_0_), channel_id=1, source_target_pairs={{0,6},{1,7},{2,4},{3,5},{4,2},{5,3},{6,0},{7,1},{8,14},{9,15},{10,... | collective-permute-start | bytes 393224 | tf_op jit(solution)/shard_map/ppermute | solution.py:150
  8.4 6.6 %collective-permute-start.17 = (bf16[256,256]{0,1:T(8,128)(2,1)S(1)}, bf16[256,256]{0,1:T(8,128)(2,1)S(1)}, u32[]{:S(2)}, u32[]{:S(2)}) collective-permute-start(bf16[256,256]{0,1:T(8,128)(2,1)S(1)} %copy.21), channel_id=1, source_target_pairs={{0,1},{1,0},{2,3},{3,2},{4,5},{5,4},{6,7},{7,6},{8,9},{9,8},{10,11... | collective-permute-start | bytes 393224 | tf_op jit(solution)/shard_map/ppermute | solution.py:150
  9.3 2.2 %copy-start.1 = (bf16[2048,1024]{1,0:T(8,128)(2,1)S(1)}, bf16[2048,1024]{1,0:T(8,128)(2,1)}, u32[]{:S(2)}) copy-start(bf16[2048,1024]{1,0:T(8,128)(2,1)} %adj.1) | copy-start | bytes 12582916
  15.1 26.9 %copy-start.2 = (bf16[256,256]{1,0:T(8,128)(2,1)S(1)}, bf16[256,256]{1,0:T(8,128)(2,1)}, u32[]{:S(2)}) copy-start(bf16[256,256]{1,0:T(8,128)(2,1)} %refs_4_.2) | copy-start | bytes 393220
  15.1 26.9 %copy-start.3 = (bf16[256,256]{1,0:T(8,128)(2,1)S(1)}, bf16[256,256]{1,0:T(8,128)(2,1)}, u32[]{:S(2)}) copy-start(bf16[256,256]{1,0:T(8,128)(2,1)} %refs_5_.1) | copy-start | bytes 393220
  15.1 8.4 %collective-permute-start.18 = (bf16[256,256]{0,1:T(8,128)(2,1)S(1)}, bf16[256,256]{0,1:T(8,128)(2,1)S(1)}, u32[]{:S(2)}, u32[]{:S(2)}) collective-permute-start(bf16[256,256]{0,1:T(8,128)(2,1)S(1)} %copy.21), channel_id=1, source_target_pairs={{0,2},{1,3},{2,0},{3,1},{4,6},{5,7},{6,4},{7,5},{8,10},{9,11},{10,... | collective-permute-start | bytes 393224 | tf_op jit(solution)/shard_map/ppermute | solution.py:150
  16.1 13.5 %collective-permute-start.20 = (bf16[256,256]{0,1:T(8,128)(2,1)S(1)}, bf16[256,256]{0,1:T(8,128)(2,1)S(1)}, u32[]{:S(2)}, u32[]{:S(2)}) collective-permute-start(bf16[256,256]{0,1:T(8,128)(2,1)S(1)} %copy.21), channel_id=1, source_target_pairs={{0,4},{1,5},{2,6},{3,7},{4,0},{5,1},{6,2},{7,3},{8,12},{9,13},{10,... | collective-permute-start | bytes 393224 | tf_op jit(solution)/shard_map/ppermute | solution.py:150
  19.6 9.9 %collective-permute-start.22 = (bf16[256,256]{0,1:T(8,128)(2,1)S(1)}, bf16[256,256]{0,1:T(8,128)(2,1)S(1)}, u32[]{:S(2)}, u32[]{:S(2)}) collective-permute-start(bf16[256,256]{0,1:T(8,128)(2,1)S(1)} %copy.21), channel_id=1, source_target_pairs={{0,6},{1,7},{2,4},{3,5},{4,2},{5,3},{6,0},{7,1},{8,14},{9,15},{10,... | collective-permute-start | bytes 393224 | tf_op jit(solution)/shard_map/ppermute | solution.py:150
  19.6 10.4 %collective-permute-start.2 = (bf16[256,256]{1,0:T(8,128)(2,1)S(1)}, bf16[256,256]{1,0:T(8,128)(2,1)S(1)}, u32[]{:S(2)}, u32[]{:S(2)}) collective-permute-start(bf16[256,256]{1,0:T(8,128)(2,1)S(1)} %collective-permute-done.1.refs_2_), channel_id=1, source_target_pairs={{0,1},{1,0},{2,3},{3,2},{4,5},{5,4},{6,7},{7,6},{8,9},{9,8},{10,11... | collective-permute-start | bytes 393224 | tf_op jit(solution)/shard_map/ppermute | solution.py:150
  19.7 10.4 %collective-permute-start.4 = (bf16[256,256]{1,0:T(8,128)(2,1)S(1)}, bf16[256,256]{1,0:T(8,128)(2,1)S(1)}, u32[]{:S(2)}, u32[]{:S(2)}) collective-permute-start(bf16[256,256]{1,0:T(8,128)(2,1)S(1)} %collective-permute-done.3.refs_4_), channel_id=1, source_target_pairs={{0,1},{1,0},{2,3},{3,2},{4,5},{5,4},{6,7},{7,6},{8,9},{9,8},{10,11... | collective-permute-start | bytes 393224 | tf_op jit(solution)/shard_map/ppermute | solution.py:150
  23.5 6.7 %collective-permute-start.6 = (bf16[256,256]{1,0:T(8,128)(2,1)S(1)}, bf16[256,256]{1,0:T(8,128)(2,1)S(1)}, u32[]{:S(2)}, u32[]{:S(2)}) collective-permute-start(bf16[256,256]{1,0:T(8,128)(2,1)S(1)} %collective-permute-done.5.refs_6_), channel_id=1, source_target_pairs={{0,1},{1,0},{2,3},{3,2},{4,5},{5,4},{6,7},{7,6},{8,9},{9,8},{10,11... | collective-permute-start | bytes 393224 | tf_op jit(solution)/shard_map/ppermute | solution.py:150
  29.6 5.5 %collective-permute-start.19 = (bf16[256,256]{0,1:T(8,128)(2,1)S(1)}, bf16[256,256]{0,1:T(8,128)(2,1)S(1)}, u32[]{:S(2)}, u32[]{:S(2)}) collective-permute-start(bf16[256,256]{0,1:T(8,128)(2,1)S(1)} %collective-permute-done.18), channel_id=1, source_target_pairs={{0,1},{1,0},{2,3},{3,2},{4,5},{5,4},{6,7},{7,6},{8,9},{9,8},{10,11... | collective-permute-start | bytes 393224 | tf_op jit(solution)/shard_map/ppermute | solution.py:150
  29.6 6.1 %collective-permute-start.21 = (bf16[256,256]{0,1:T(8,128)(2,1)S(1)}, bf16[256,256]{0,1:T(8,128)(2,1)S(1)}, u32[]{:S(2)}, u32[]{:S(2)}) collective-permute-start(bf16[256,256]{0,1:T(8,128)(2,1)S(1)} %collective-permute-done.20), channel_id=1, source_target_pairs={{0,1},{1,0},{2,3},{3,2},{4,5},{5,4},{6,7},{7,6},{8,9},{9,8},{10,11... | collective-permute-start | bytes 393224 | tf_op jit(solution)/shard_map/ppermute | solution.py:150
  30.1 15.7 %collective-permute-start.23 = (bf16[256,256]{0,1:T(8,128)(2,1)S(1)}, bf16[256,256]{0,1:T(8,128)(2,1)S(1)}, u32[]{:S(2)}, u32[]{:S(2)}) collective-permute-start(bf16[256,256]{0,1:T(8,128)(2,1)S(1)} %collective-permute-done.22), channel_id=1, source_target_pairs={{0,1},{1,0},{2,3},{3,2},{4,5},{5,4},{6,7},{7,6},{8,9},{9,8},{10,11... | collective-permute-start | bytes 393224 | tf_op jit(solution)/shard_map/ppermute | solution.py:150
  32.1 6.4 %collective-permute-start.7 = (bf16[256,256]{1,0:T(8,128)(2,1)S(1)}, bf16[256,256]{1,0:T(8,128)(2,1)S(1)}, u32[]{:S(2)}, u32[]{:S(2)}) collective-permute-start(bf16[256,256]{1,0:T(8,128)(2,1)S(1)} %get-tuple-element.21), channel_id=1, source_target_pairs={{0,8},{8,0},{16,24},{24,16},{1,9},{9,1},{17,25},{25,17},{2,10},{10... | collective-permute-start | bytes 393224 | tf_op jit(solution)/shard_map/ppermute | solution.py:153
  33.6 8.4 %collective-permute-start.8 = (bf16[256,256]{1,0:T(8,128)(2,1)S(1)}, bf16[256,256]{1,0:T(8,128)(2,1)S(1)}, u32[]{:S(2)}, u32[]{:S(2)}) collective-permute-start(bf16[256,256]{1,0:T(8,128)(2,1)S(1)} %get-tuple-element.20), channel_id=1, source_target_pairs={{0,16},{8,24},{16,0},{24,8},{1,17},{9,25},{17,1},{25,9},{2,18},{10... | collective-permute-start | bytes 393224 | tf_op jit(solution)/shard_map/ppermute | solution.py:153
  35.1 6.9 %collective-permute-start.9 = (bf16[256,256]{1,0:T(8,128)(2,1)S(1)}, bf16[256,256]{1,0:T(8,128)(2,1)S(1)}, u32[]{:S(2)}, u32[]{:S(2)}) collective-permute-start(bf16[256,256]{1,0:T(8,128)(2,1)S(1)} %get-tuple-element.19), channel_id=1, source_target_pairs={{0,24},{8,16},{16,8},{24,0},{1,25},{9,17},{17,9},{25,1},{2,26},{10... | collective-permute-start | bytes 393224 | tf_op jit(solution)/shard_map/ppermute | solution.py:153
  42.2 5.6 %collective-permute-start.10 = (bf16[256,256]{1,0:T(8,128)(2,1)S(1)}, bf16[256,256]{1,0:T(8,128)(2,1)S(1)}, u32[]{:S(2)}, u32[]{:S(2)}) collective-permute-start(bf16[256,256]{1,0:T(8,128)(2,1)S(1)} %get-tuple-element.9.refs_0_), channel_id=1, source_target_pairs={{0,8},{8,0},{16,24},{24,16},{1,9},{9,1},{17,25},{25,17},{2,10},{10... | collective-permute-start | bytes 393224 | tf_op jit(solution)/shard_map/ppermute | solution.py:153
  43.5 7.6 %collective-permute-start.11 = (bf16[256,256]{1,0:T(8,128)(2,1)S(1)}, bf16[256,256]{1,0:T(8,128)(2,1)S(1)}, u32[]{:S(2)}, u32[]{:S(2)}) collective-permute-start(bf16[256,256]{1,0:T(8,128)(2,1)S(1)} %get-tuple-element.9.refs_0_), channel_id=1, source_target_pairs={{0,16},{8,24},{16,0},{24,8},{1,17},{9,25},{17,1},{25,9},{2,18},{10... | collective-permute-start | bytes 393224 | tf_op jit(solution)/shard_map/ppermute | solution.py:153
  44.3 6.8 %collective-permute-start.12 = (bf16[256,256]{1,0:T(8,128)(2,1)S(1)}, bf16[256,256]{1,0:T(8,128)(2,1)S(1)}, u32[]{:S(2)}, u32[]{:S(2)}) collective-permute-start(bf16[256,256]{1,0:T(8,128)(2,1)S(1)} %get-tuple-element.9.refs_0_), channel_id=1, source_target_pairs={{0,24},{8,16},{16,8},{24,0},{1,25},{9,17},{17,9},{25,1},{2,26},{10... | collective-permute-start | bytes 393224 | tf_op jit(solution)/shard_map/ppermute | solution.py:153
  53.6 40.1 %copy-start.4 = (bf16[256,256]{1,0:T(8,128)(2,1)S(1)}, bf16[256,256]{1,0:T(8,128)(2,1)}, u32[]{:S(2)}) copy-start(bf16[256,256]{1,0:T(8,128)(2,1)} %refs_4_.3) | copy-start | bytes 393220
  54.1 1.4 %collective-permute-start.24 = (bf16[2,128,256]{2,1,0:T(8,128)(2,1)S(1)}, bf16[2,128,256]{2,1,0:T(8,128)(2,1)S(1)}, u32[]{:S(2)}, u32[]{:S(2)}) collective-permute-start(bf16[2,128,256]{2,1,0:T(8,128)(2,1)S(1)} %broadcast_select_fusion.2), channel_id=1, source_target_pairs={{0,1},{1,0},{2,3},{3,2},{4,5},{5,4},{6,7},{7,6},{8,9},{9,8},{10,11... | collective-permute-start | bytes 393224 | tf_op jit(solution)/shard_map/ppermute | solution.py:150
  55.6 7.3 %collective-permute-start.27 = (bf16[2,128,256]{2,1,0:T(8,128)(2,1)S(1)}, bf16[2,128,256]{2,1,0:T(8,128)(2,1)S(1)}, u32[]{:S(2)}, u32[]{:S(2)}) collective-permute-start(bf16[2,128,256]{2,1,0:T(8,128)(2,1)S(1)} %add_convert_fusion.1), channel_id=1, source_target_pairs={{0,24},{8,16},{16,8},{24,0},{1,25},{9,17},{17,9},{25,1},{2,26},{10... | collective-permute-start | bytes 393224 | tf_op jit(solution)/shard_map/ppermute | solution.py:153
  57.3 7.7 %collective-permute-start.26 = (bf16[2,128,256]{2,1,0:T(8,128)(2,1)S(1)}, bf16[2,128,256]{2,1,0:T(8,128)(2,1)S(1)}, u32[]{:S(2)}, u32[]{:S(2)}) collective-permute-start(bf16[2,128,256]{2,1,0:T(8,128)(2,1)S(1)} %add_convert_fusion.1), channel_id=1, source_target_pairs={{0,16},{8,24},{16,0},{24,8},{1,17},{9,25},{17,1},{25,9},{2,18},{10... | collective-permute-start | bytes 393224 | tf_op jit(solution)/shard_map/ppermute | solution.py:153
  58.1 6.8 %collective-permute-start.25 = (bf16[2,128,256]{2,1,0:T(8,128)(2,1)S(1)}, bf16[2,128,256]{2,1,0:T(8,128)(2,1)S(1)}, u32[]{:S(2)}, u32[]{:S(2)}) collective-permute-start(bf16[2,128,256]{2,1,0:T(8,128)(2,1)S(1)} %add_convert_fusion.1), channel_id=1, source_target_pairs={{0,8},{8,0},{16,24},{24,16},{1,9},{9,1},{17,25},{25,17},{2,10},{10... | collective-permute-start | bytes 393224 | tf_op jit(solution)/shard_map/ppermute | solution.py:153
  59.2 21.3 %collective-permute-start.13 = (bf16[4,256,256]{2,1,0:T(8,128)(2,1)S(1)}, bf16[4,256,256]{2,1,0:T(8,128)(2,1)S(1)}, u32[]{:S(2)}, u32[]{:S(2)}) collective-permute-start(bf16[4,256,256]{2,1,0:T(8,128)(2,1)S(1)} %slice_bitcast_fusion), channel_id=1, source_target_pairs={{0,1},{1,0},{2,3},{3,2},{4,5},{5,4},{6,7},{7,6},{8,9},{9,8},{10,11... | collective-permute-start | bytes 1572872 | tf_op jit(solution)/shard_map/ppermute | solution.py:150
  65.0 8.3 %collective-permute-start.30 = (bf16[2,128,256]{2,1,0:T(8,128)(2,1)S(1)}, bf16[2,128,256]{2,1,0:T(8,128)(2,1)S(1)}, u32[]{:S(2)}, u32[]{:S(2)}) collective-permute-start(bf16[2,128,256]{2,1,0:T(8,128)(2,1)S(1)} %add_convert_fusion), channel_id=1, source_target_pairs={{0,6},{1,7},{2,4},{3,5},{4,2},{5,3},{6,0},{7,1},{8,14},{9,15},{10,... | collective-permute-start | bytes 393224 | tf_op jit(solution)/shard_map/ppermute | solution.py:150
  67.5 12.9 %collective-permute-start.29 = (bf16[2,128,256]{2,1,0:T(8,128)(2,1)S(1)}, bf16[2,128,256]{2,1,0:T(8,128)(2,1)S(1)}, u32[]{:S(2)}, u32[]{:S(2)}) collective-permute-start(bf16[2,128,256]{2,1,0:T(8,128)(2,1)S(1)} %add_convert_fusion), channel_id=1, source_target_pairs={{0,4},{1,5},{2,6},{3,7},{4,0},{5,1},{6,2},{7,3},{8,12},{9,13},{10,... | collective-permute-start | bytes 393224 | tf_op jit(solution)/shard_map/ppermute | solution.py:150
  68.5 11.8 %collective-permute-start.28 = (bf16[2,128,256]{2,1,0:T(8,128)(2,1)S(1)}, bf16[2,128,256]{2,1,0:T(8,128)(2,1)S(1)}, u32[]{:S(2)}, u32[]{:S(2)}) collective-permute-start(bf16[2,128,256]{2,1,0:T(8,128)(2,1)S(1)} %add_convert_fusion), channel_id=1, source_target_pairs={{0,2},{1,3},{2,0},{3,1},{4,6},{5,7},{6,4},{7,5},{8,10},{9,11},{10,... | collective-permute-start | bytes 393224 | tf_op jit(solution)/shard_map/ppermute | solution.py:150
  80.4 14.2 %collective-permute-start.31 = (f32[2,128,256]{2,1,0:T(8,128)S(1)}, f32[2,128,256]{2,1,0:T(8,128)S(1)}, u32[]{:S(2)}, u32[]{:S(2)}) collective-permute-start(f32[2,128,256]{2,1,0:T(8,128)S(1)} %add_multiply_fusion), channel_id=1, source_target_pairs={{0,1},{1,0},{2,3},{3,2},{4,5},{5,4},{6,7},{7,6},{8,9},{9,8},{10,11... | collective-permute-start | bytes 786440 | tf_op jit(solution)/shard_map/ppermute | solution.py:150
  80.7 8.4 %collective-permute-start.14 = (bf16[256,256]{1,0:T(8,128)(2,1)S(1)}, bf16[256,256]{1,0:T(8,128)(2,1)S(1)}, u32[]{:S(2)}, u32[]{:S(2)}) collective-permute-start(bf16[256,256]{1,0:T(8,128)(2,1)S(1)} %get-tuple-element.17), channel_id=1, source_target_pairs={{0,2},{1,3},{2,0},{3,1},{4,6},{5,7},{6,4},{7,5},{8,10},{9,11},{10,... | collective-permute-start | bytes 393224 | tf_op jit(solution)/shard_map/ppermute | solution.py:150
  80.8 12.9 %collective-permute-start.15 = (bf16[256,256]{1,0:T(8,128)(2,1)S(1)}, bf16[256,256]{1,0:T(8,128)(2,1)S(1)}, u32[]{:S(2)}, u32[]{:S(2)}) collective-permute-start(bf16[256,256]{1,0:T(8,128)(2,1)S(1)} %get-tuple-element.16), channel_id=1, source_target_pairs={{0,4},{1,5},{2,6},{3,7},{4,0},{5,1},{6,2},{7,3},{8,12},{9,13},{10,... | collective-permute-start | bytes 393224 | tf_op jit(solution)/shard_map/ppermute | solution.py:150
  83.7 10.0 %collective-permute-start.16 = (bf16[256,256]{1,0:T(8,128)(2,1)S(1)}, bf16[256,256]{1,0:T(8,128)(2,1)S(1)}, u32[]{:S(2)}, u32[]{:S(2)}) collective-permute-start(bf16[256,256]{1,0:T(8,128)(2,1)S(1)} %get-tuple-element.15), channel_id=1, source_target_pairs={{0,6},{1,7},{2,4},{3,5},{4,2},{5,3},{6,0},{7,1},{8,14},{9,15},{10,... | collective-permute-start | bytes 393224 | tf_op jit(solution)/shard_map/ppermute | solution.py:150

commit v2 on v1

v2 whole, which is shorter than its diff:
```python
import functools

import jax
import jax.numpy as jnp
from jax import lax
from jax.experimental import pallas as pl
from jax.experimental.pallas import tpu as pltpu
from jax.sharding import PartitionSpec as P

BF16, F32 = jnp.bfloat16, jnp.float32
ROWS_COLS = (((0,), (0,)), ((), ()))
LAST_LAST = (((1,), (1,)), ((), ()))
VMEM = pltpu.VMEM


def params():
    return pltpu.CompilerParams(vmem_limit_bytes=16 * 1024 * 1024)


def cost(flops, bytes_accessed):
    return pl.CostEstimate(flops=flops, bytes_accessed=bytes_accessed, transcendentals=0)


def whole(count):
    return [pl.BlockSpec(memory_space=VMEM) for _ in range(count)]


def unread(events):
    return whole(len(events))


def tree(values):
    while len(values) > 1:
        values = [a + b for a, b in zip(values[::2], values[1::2])]
    return values[0]


def mask_kernel(block, tile, row_src, col_src, mask, adj, plain, token):
    step = pl.program_id(0)
    per = block // tile
    row = row_src[step]
    token[...] = jnp.zeros_like(token)
    for slot in range(adj.shape[1] // block):
        col = col_src[slot]
        for v in range(per):
            part = adj[:, pl.ds(pl.multiple_of((col * per + v) * tile, tile), tile)]
            for u in range(per):
                keep = mask[row * per + u, col * per + v].astype(F32).astype(BF16)
                lanes = slice(slot * block + v * tile, slot * block + (v + 1) * tile)
                plain[u * tile : (u + 1) * tile, lanes] = part[u * tile : (u + 1) * tile] * keep


def masked(adjacency, tile_mask, row_src, col_src, block):
    rows, cols = adjacency.shape
    tile = rows // tile_mask.shape[0]
    adjacency = pltpu.with_memory_space_constraint(adjacency, pltpu.HBM)
    return pl.pallas_call(
        functools.partial(mask_kernel, block, tile),
        grid_spec=pltpu.PrefetchScalarGridSpec(
            num_scalar_prefetch=3,
            grid=(rows // block,),
            in_specs=[pl.BlockSpec((block, cols), lambda s, row_src, *_: (row_src[s], 0))],
            out_specs=[
                pl.BlockSpec((block, cols), lambda s, *_: (s, 0)),
                pl.BlockSpec((16, 128), lambda s, *_: (0, 0)),
            ],
        ),
        out_shape=[VMEM((rows, cols), BF16), VMEM((16, 128), BF16)],
        compiler_params=params(),
        cost_estimate=cost(rows * cols, 4 * rows * cols),
        name="mask_tiles",
    )(row_src, col_src, tile_mask, adjacency)


def spread_kernel(count, turned, *refs):
    graph, parts, out, held = refs[0], refs[1 : count + 1], refs[-2], refs[-1]
    block = parts[0].shape[0]
    for slot, part in enumerate(parts):
        held[slot * block : (slot + 1) * block] = part[...]
    chunk = min(out.shape[0], 1024)

    @pl.loop(0, out.shape[0] // chunk)
    def _(step):
        span = pl.ds(pl.multiple_of(step * chunk, chunk), chunk)
        if turned:
            value = lax.dot_general(graph[:, span], held[...], ROWS_COLS, preferred_element_type=F32)
        else:
            value = jnp.dot(graph[span], held[...], preferred_element_type=F32)
        out[span] = value.astype(BF16)


def spread(graph, parts, turned, *events):
    block, width = parts[0].shape
    rows, cols = graph.shape
    out_rows, depth = (cols, rows) if turned else (rows, cols)
    graph = pltpu.with_memory_space_constraint(graph, VMEM)
    out = pl.pallas_call(
        functools.partial(spread_kernel, len(parts), turned),
        in_specs=whole(1 + len(parts)) + unread(events),
        out_specs=pl.BlockSpec(memory_space=VMEM),
        out_shape=jax.ShapeDtypeStruct((out_rows, width), BF16),
        scratch_shapes=[VMEM((depth, width), BF16)],
        compiler_params=params(),
        cost_estimate=cost(2 * rows * cols * width, 2 * rows * cols),
        name="propagate",
    )(graph, *parts, *events)
    return out.reshape(out_rows // block, block, width)


def middle_kernel(count, *refs):
    parts, w_two, pre_one = refs[:count], refs[count], refs[count + 1]
    prop, grad = refs[-2:]
    total = tree([part[...].astype(F32) for part in parts]).astype(BF16)
    prop[...] = total
    back = lax.dot_general(total, w_two[...], LAST_LAST, preferred_element_type=F32)
    grad[...] = jnp.where(pre_one[...] > 0, back, 0.0).astype(BF16)


def middle(parts, w_two, pre_one, *events):
    shape = jax.ShapeDtypeStruct(pre_one.shape, BF16)
    return pl.pallas_call(
        functools.partial(middle_kernel, len(parts)),
        in_specs=whole(len(parts) + 2) + unread(events),
        out_specs=whole(2),
        out_shape=[shape, shape],
        compiler_params=params(),
        name="first_layer_gradient",
    )(*parts, w_two, pre_one, *events)


def last_kernel(count, *refs):
    parts, w_one, out, token = refs[:count], refs[count], refs[-2], refs[-1]
    total = tree([part[...].astype(F32) for part in parts]).astype(BF16)
    out[...] = lax.dot_general(
        total, w_one[...], LAST_LAST, preferred_element_type=F32
    ).astype(BF16)
    token[...] = total[: token.shape[0], : token.shape[1]]


def last(parts, w_one):
    return pl.pallas_call(
        functools.partial(last_kernel, len(parts)),
        in_specs=whole(len(parts) + 1),
        out_specs=whole(2),
        out_shape=[
            jax.ShapeDtypeStruct(parts[0].shape, BF16),
            jax.ShapeDtypeStruct((16, 128), BF16),
        ],
        compiler_params=params(),
        name="node_gradient",
    )(*parts, w_one)


def copy_kernel(value, *refs):
    refs[-1][...] = value[...]


def after(value, *events):
    return pl.pallas_call(
        copy_kernel,
        in_specs=whole(1) + unread(events),
        out_specs=pl.BlockSpec(memory_space=VMEM),
        out_shape=jax.ShapeDtypeStruct(value.shape, value.dtype),
        compiler_params=params(),
        name="after",
    )(value, *events)


def joined_kernel(count, *refs):
    refs[-1][...] = tree([ref[...].astype(F32) for ref in refs[:count]]).astype(BF16)


def joined(values, *events):
    return pl.pallas_call(
        functools.partial(joined_kernel, len(values)),
        in_specs=whole(len(values)) + unread(events),
        out_specs=pl.BlockSpec(memory_space=VMEM),
        out_shape=jax.ShapeDtypeStruct(values[0].shape, BF16),
        compiler_params=params(),
        name="joined",
    )(*values, *events)


def xor_order(blocks, bits):
    for position, bit in enumerate(bits):
        split = blocks.reshape((-1, 2, 1 << position) + blocks.shape[1:])
        blocks = jnp.where(bit, split[:, ::-1], split).reshape(blocks.shape)
    return blocks


def local(n_row, n_col, adjacency, tile_mask, out_grad, pre_two, hidden, pre_one, features, w_two, w_one):
    block = out_grad.shape[0]
    scale = 4.0 * block ** (-0.5)
    n_far = n_col // 2
    row, col = lax.axis_index("row"), lax.axis_index("col")
    odd = col % 2 == 1

    def over_col(value, flip):
        return lax.ppermute(value, "col", [(i, i ^ flip) for i in range(n_col)])

    def over_row(value, flip):
        return lax.ppermute(value, "row", [(i, i ^ flip) for i in range(n_row)])

    def far(values):
        got = {j: over_col(values[j], 2 * j) for j in reversed(range(1, n_far))}
        return [values[0]] + [got[j] for j in range(1, n_far)]

    def rows_all(values):
        got = {i: over_row(values[i], i) for i in reversed(range(1, n_row))}
        return [values[0]] + [got[i] for i in range(1, n_row)]

    def halved(term):
        half = term.shape[0] // 2
        mine = jnp.where(odd, term[half:], term[:half])
        yours = jnp.where(odd, term[:half], term[half:]).astype(BF16)
        return (mine + over_col(yours, 1).astype(F32)).astype(BF16)

    def sum_far(value):
        return tree([v.astype(F32) for v in far([value] * n_far)]).astype(BF16)

    row_src = jnp.bitwise_xor(jnp.arange(n_col, dtype=jnp.int32), col)
    col_src = jnp.bitwise_xor(jnp.arange(n_row, dtype=jnp.int32), row)

    grad_two = jnp.where(pre_two > 0, out_grad, jnp.zeros_like(out_grad))
    near = far([grad_two] * n_far)
    near_features = [features, over_col(features, 2)]
    plain, made = masked(adjacency, tile_mask, row_src, col_src, block)
    others = [over_col(after(value, made), 1) for value in near]
    column_part = spread(plain, [value for pair in zip(near, others) for value in pair], True)
    parts = rows_all(column_part)
    late_features = after(features, *near[1:])
    near_features += [over_col(late_features, 2 * j) for j in range(2, n_far)]
    prop_two, grad_one = middle(parts, w_two, pre_one, near_features[1])
    first = rows_all([grad_one] * n_row)
    other_features = [over_col(value, 1) for value in near_features]
    row_features = jnp.stack([value for pair in zip(near_features, other_features) for value in pair])

    row_part = spread(plain, first, False, row_features)
    row_part = row_part.reshape(n_far, 2, block, -1)
    crossed = over_col(row_part[:, 1], 1)
    chip_part = row_part[:, 0].astype(F32) + crossed.astype(F32)
    chip_part = chip_part.astype(BF16)
    ends = far(chip_part)
    node_grad, token = last(ends, w_one)

    term_two = lax.dot_general(hidden, prop_two, ROWS_COLS, preferred_element_type=F32)
    term_one = lax.dot_general(
        row_features.reshape(n_col * block, -1),
        row_part.reshape(n_col * block, -1),
        ROWS_COLS,
        preferred_element_type=F32,
    )
    width = term_one.shape[1]
    terms = jnp.stack([halved(term_one), halved(term_two)], axis=1)
    terms = terms.reshape(n_row, -1, width)
    row_bits = [jnp.bitwise_and(row, 1 << b) > 0 for b in range(n_row.bit_length() - 1)]
    terms = xor_order(terms, row_bits)
    total = tree([value.astype(F32) for value in rows_all(terms)]).astype(BF16)
    total = joined([total] + [over_col(total, 2 * j) for j in range(1, n_far)], token)
    total = xor_order(jnp.stack(rows_all([total] * n_row)), row_bits)
    total = total.reshape(-1, 2, width).astype(F32) * scale
    other = over_col(total, 1)
    lower, upper = jnp.where(odd, other, total), jnp.where(odd, total, other)
    total = jnp.concatenate([lower, upper], axis=0)
    return node_grad, total[:, 0], total[:, 1]


def solution(mesh):
    return jax.shard_map(
        functools.partial(local, mesh.shape["row"], mesh.shape["col"]),
        mesh=mesh,
        in_specs=(
            P("row", "col"),
            P("row", "col"),
            P(("row", "col"), None),
            P(("row", "col"), None),
            P(("col", "row"), None),
            P(("col", "row"), None),
            P(("row", "col"), None),
            P(),
            P(),
        ),
        out_specs=(P(("row", "col"), None), P(), P()),
        check_vma=False,
    )
```

time: 95.7 us -> 77.4 us (0.81)
  waiting for transfers between devices: 47.1 us -> 23.5 us
  starting transfers between devices: 31.3 us -> 38 us
  local copies, waits for them, and re-layouts: 4.17 us -> 2.16 us
    ppermute x23 -> x24, waiting for transfers between devices: 30.1 us -> 14.5 us  [over_col(): return lax.ppermute(value, 'col', [(i, i ^ flip) for i in range(n_col)])]
    ppermute x9 -> x12, waiting for transfers between devices: 17 us -> 8.97 us  [over_row(): return lax.ppermute(value, 'row', [(i, i ^ flip) for i in range(n_row)])]
    ppermute x9 -> x12, starting transfers between devices: 10.7 us -> 14.2 us  [over_row(): return lax.ppermute(value, 'row', [(i, i ^ flip) for i in range(n_row)])]
    ppermute x23 -> x24, starting transfers between devices: 20.6 us -> 23.8 us  [over_col(): return lax.ppermute(value, 'col', [(i, i ^ flip) for i in range(n_col)])]
    unnamed x19, local copies, waits for them, and re-layouts: 4.05 us -> 1.69 us
    pallas_call x1, Pallas kernels: 3.53 us -> 5.82 us  [masked(): pl.pallas_call(functools.partial(mask_kernel, block, tile), grid_spec=plt...]
    pallas_call x2 -> x8, Pallas kernels: 4.39 us -> 2.87 us  [the longest x2 2.8 us: spread(): pl.pallas_call(functools.partial(spread_kernel, len(parts), turned), in_s...]
  transfers between devices with their start and end apart: 32 -> 36, of which waited for: 13 -> 18; matrix products, arithmetic and copies ran while one was open for 3% -> 2% of each run, Pallas kernels for 7% -> 11%
where the time goes in v2:
time: 77.4 us; the launch traced here: 77.1 us
  starting transfers between devices  38 us (49%)
  waiting for transfers between devices  23.5 us (30%)
  Pallas kernels  9.8 us (13%)
  local copies, waits for them, and re-layouts  2.16 us (3%)
  other arithmetic  1.85 us (2%)
  between operations  1.1 us (1%)
    ppermute x24, starting transfers between devices, over_col(): return lax.ppermute(value, 'col', [(i, i ^ flip) for i in range(n_col)])  23.8 us
    ppermute x24, waiting for transfers between devices, over_col(): return lax.ppermute(value, 'col', [(i, i ^ flip) for i in range(n_col)])  14.5 us
    ppermute x12, starting transfers between devices, over_row(): return lax.ppermute(value, 'row', [(i, i ^ flip) for i in range(n_row)])  14.2 us
    ppermute x12, waiting for transfers between devices, over_row(): return lax.ppermute(value, 'row', [(i, i ^ flip) for i in range(n_row)])  8.97 us
    pallas_call x1, Pallas kernels, masked(): pl.pallas_call(functools.partial(mask_kernel, block, tile), grid_spec=plt...  5.82 us
    pallas_call x2, Pallas kernels, spread(): pl.pallas_call(functools.partial(spread_kernel, len(parts), turned), in_s...  2.8 us
    unnamed x19, local copies, waits for them, and re-layouts  1.69 us
  transfers between devices with their start and end apart: 36, of which 18 were waited for; matrix products, arithmetic and copies ran while one was open for 2% of the time, Pallas kernels for 11%

profile of v2, /device:TPU:0, one launch (start us, length us, event | category | flops | bytes accessed | tf_op | source)
XLA Modules:
  0.0 77.1 jit_solution(7916324630993406049)
XLA Ops:
  0.7 1.0 %compare_select_fusion.value.refs_1_ = bf16[256,256]{1,0:T(8,128)(2,1)S(1)} fusion(bf16[256,256]{1,0:T(8,128)(2,1)} %param.11, bf16[256,256]{1,0:T(8,128)(2,1)} %param.12), kind=kLoop, calls=%fused_computation.14 | loop fusion | flops 131072 | bytes 393216 | tf_op jit(solution)/shard_map/jit(_where)/select_n | solution.py:224
  1.7 5.1 %collective-permute-start.5 = (bf16[256,256]{1,0:T(8,128)(2,1)S(1)}, bf16[256,256]{1,0:T(8,128)(2,1)S(1)}, u32[]{:S(2)}, u32[]{:S(2)}) collective-permute-start(bf16[256,256]{1,0:T(8,128)(2,1)S(1)} %compare_select_fusion.value.refs_1_), channel_id=1, source_target_pairs={{0,6},{1,7},{2,4},{3,5},{4,2},{5,3},{6,0},{7,1},{8,14},{9,15},{10,... | collective-permute-start | bytes 393224 | tf_op jit(solution)/shard_map/ppermute | solution.py:199
  6.8 0.6 collective-permute-start.1
  7.5 1.4 %collective-permute-start.10 = (bf16[256,256]{1,0:T(8,128)(2,1)}, bf16[256,256]{1,0:T(8,128)(2,1)S(1)}, u32[]{:S(2)}, u32[]{:S(2)}) collective-permute-start(bf16[256,256]{1,0:T(8,128)(2,1)} %value.1), channel_id=1, source_target_pairs={{0,2},{1,3},{2,0},{3,1},{4,6},{5,7},{6,4},{7,5},{8,10},{9,11},{10,... | collective-permute-start | bytes 393224 | tf_op jit(solution)/shard_map/ppermute | solution.py:199
  8.9 0.8 copy.13.mask
  9.6 5.8 %mask_tiles.1 = (bf16[2048,1024]{1,0:T(8,128)(2,1)S(1)}, bf16[16,128]{1,0:T(8,128)(2,1)S(1)}) custom-call(s32[8]{0:T(128)S(1)} %iota_xor_fusion.1.row_src, s32[4]{0:T(128)S(1)} %iota_xor_fusion.col_src, s32[16,8]{1,0:T(8,128)S(1)} %copy.13.mask, bf16[2048,1024]{1,0:T(8,128)(2,1)} %adj.1), custom_call_target="tpu_custom_call" | custom-call | flops 2097152 | bytes 8388608 | tf_op jit(solution)/shard_map/mask_tiles/pallas_call | solution.py:57
  15.5 0.6 collective-permute-start
  16.1 1.9 %collective-permute-done.3.value.refs_5_.refs_1_ = bf16[256,256]{1,0:T(8,128)(2,1)S(1)} collective-permute-done((bf16[256,256]{1,0:T(8,128)(2,1)S(1)}, bf16[256,256]{1,0:T(8,128)(2,1)S(1)}, u32[]{:S(2)}, u32[]{:S(2)}) %collective-permute-start.3) | collective-permute-done | bytes 131104 | tf_op jit(solution)/shard_map/ppermute | solution.py:199
  18.0 2.5 %collective-permute-start.18 = (bf16[256,256]{1,0:T(8,128)(2,1)S(1)}, bf16[256,256]{1,0:T(8,128)(2,1)S(1)}, u32[]{:S(2)}, u32[]{:S(2)}) collective-permute-start(bf16[256,256]{1,0:T(8,128)(2,1)S(1)} %after.9), channel_id=1, source_target_pairs={{0,6},{1,7},{2,4},{3,5},{4,2},{5,3},{6,0},{7,1},{8,14},{9,15},{10,... | collective-permute-start | bytes 393224 | tf_op jit(solution)/shard_map/ppermute | solution.py:199
  20.7 0.6 collective-permute-start.4
  21.5 0.5 collective-permute-done.2.refs_4_
  22.3 0.5 collective-permute-done.6.refs_8_
  22.7 1.3 %propagate.2 = bf16[1024,256]{1,0:T(8,128)(2,1)S(1)} custom-call(bf16[2048,1024]{1,0:T(8,128)(2,1)S(1)} %get-tuple-element.9.refs_0_, bf16[256,256]{1,0:T(8,128)(2,1)S(1)} %compare_select_fusion.value.refs_1_, bf16[256,256]{1,0:T(8,128)(2,1)S(1)} %collective-permute-done.refs_2_, bf16[256,256]{1,0:T(8,128)(2,1)S(1)} %collective-permute-done.1.value.refs_3_.refs_0_, ...), custom_call_target="tpu_custom_call" | custom-call | flops 1073741824 | bytes 4194304 | tf_op jit(solution)/shard_map/propagate/pallas_call | solution.py:97
  24.1 2.5 %collective-permute-start.9 = (bf16[256,256]{1,0:T(8,128)(2,1)S(1)}, bf16[256,256]{1,0:T(8,128)(2,1)S(1)}, u32[]{:S(2)}, u32[]{:S(2)}) collective-permute-start(bf16[256,256]{1,0:T(8,128)(2,1)S(1)} %get-tuple-element.23), channel_id=1, source_target_pairs={{0,24},{8,16},{16,8},{24,0},{1,25},{9,17},{17,9},{25,1},{2,26},{10... | collective-permute-start | bytes 393224 | tf_op jit(solution)/shard_map/ppermute | solution.py:202
  26.6 0.5 collective-permute-start.8
  27.1 0.5 collective-permute-start.7
  27.7 3.7 %collective-permute-done.16 = bf16[256,256]{1,0:T(8,128)(2,1)S(1)} collective-permute-done((bf16[256,256]{1,0:T(8,128)(2,1)S(1)}, bf16[256,256]{1,0:T(8,128)(2,1)S(1)}, u32[]{:S(2)}, u32[]{:S(2)}) %collective-permute-start.16) | collective-permute-done | bytes 131104 | tf_op jit(solution)/shard_map/ppermute | solution.py:199
  31.3 0.5 collective-permute-start.17
  31.9 1.5 %collective-permute-done.8.refs_2_ = bf16[256,256]{1,0:T(8,128)(2,1)S(1)} collective-permute-done((bf16[256,256]{1,0:T(8,128)(2,1)S(1)}, bf16[256,256]{1,0:T(8,128)(2,1)S(1)}, u32[]{:S(2)}, u32[]{:S(2)}) %collective-permute-start.8) | collective-permute-done | bytes 131104 | tf_op jit(solution)/shard_map/ppermute | solution.py:202
  33.8 1.7 %collective-permute-start.13 = (bf16[256,256]{1,0:T(8,128)(2,1)S(1)}, bf16[256,256]{1,0:T(8,128)(2,1)S(1)}, u32[]{:S(2)}, u32[]{:S(2)}) collective-permute-start(bf16[256,256]{1,0:T(8,128)(2,1)S(1)} %get-tuple-element.11.refs_1_), channel_id=1, source_target_pairs={{0,24},{8,16},{16,8},{24,0},{1,25},{9,17},{17,9},{25,1},{2,26},{10... | collective-permute-start | bytes 393224 | tf_op jit(solution)/shard_map/ppermute | solution.py:202
  35.5 1.3 %collective-permute-start.12 = (bf16[256,256]{1,0:T(8,128)(2,1)S(1)}, bf16[256,256]{1,0:T(8,128)(2,1)S(1)}, u32[]{:S(2)}, u32[]{:S(2)}) collective-permute-start(bf16[256,256]{1,0:T(8,128)(2,1)S(1)} %get-tuple-element.11.refs_1_), channel_id=1, source_target_pairs={{0,16},{8,24},{16,0},{24,8},{1,17},{9,25},{17,1},{25,9},{2,18},{10... | collective-permute-start | bytes 393224 | tf_op jit(solution)/shard_map/ppermute | solution.py:202
  36.8 0.5 collective-permute-start.11
  37.7 1.2 %collective-permute-done.25 = bf16[128,256]{1,0:T(8,128)(2,1)S(1)} collective-permute-done((bf16[128,256]{1,0:T(8,128)(2,1)S(1)}, bf16[128,256]{1,0:T(8,128)(2,1)S(1)}, u32[]{:S(2)}, u32[]{:S(2)}) %collective-permute-start.25) | collective-permute-done | bytes 65568 | tf_op jit(solution)/shard_map/ppermute | solution.py:199
  38.9 2.2 %collective-permute-done.13.refs_4_ = bf16[256,256]{1,0:T(8,128)(2,1)S(1)} collective-permute-done((bf16[256,256]{1,0:T(8,128)(2,1)S(1)}, bf16[256,256]{1,0:T(8,128)(2,1)S(1)}, u32[]{:S(2)}, u32[]{:S(2)}) %collective-permute-start.13) | collective-permute-done | bytes 131104 | tf_op jit(solution)/shard_map/ppermute | solution.py:202
  41.1 1.7 %collective-permute-done.12.refs_3_ = bf16[256,256]{1,0:T(8,128)(2,1)S(1)} collective-permute-done((bf16[256,256]{1,0:T(8,128)(2,1)S(1)}, bf16[256,256]{1,0:T(8,128)(2,1)S(1)}, u32[]{:S(2)}, u32[]{:S(2)}) %collective-permute-start.12) | collective-permute-done | bytes 131104 | tf_op jit(solution)/shard_map/ppermute | solution.py:202
  42.9 1.4 %propagate.3 = bf16[2048,256]{1,0:T(8,128)(2,1)S(1)} custom-call(bf16[2048,1024]{1,0:T(8,128)(2,1)S(1)} %get-tuple-element.9.refs_0_, bf16[256,256]{1,0:T(8,128)(2,1)S(1)} %get-tuple-element.11.refs_1_, bf16[256,256]{1,0:T(8,128)(2,1)S(1)} %collective-permute-done.11.refs_2_, bf16[256,256]{1,0:T(8,128)(2,1)S(1)} %collective-permute-done.12.refs_3_, ...), custom_call_target="tpu_custom_call" | custom-call | flops 1073741824 | bytes 4194304 | tf_op jit(solution)/shard_map/propagate/pallas_call | solution.py:97
  44.4 0.5 fusion.9
  45.0 0.6 collective-permute-start.20
  45.6 0.6 collective-permute-done.24
  46.6 1.5 %collective-permute-start.26 = (bf16[64,256]{1,0:T(8,128)(2,1)S(1)}, bf16[64,256]{1,0:T(8,128)(2,1)S(1)}, u32[]{:S(2)}, u32[]{:S(2)}) collective-permute-start(bf16[64,256]{1,0:T(8,128)(2,1)S(1)} %get-tuple-element.27), channel_id=1, source_target_pairs={{0,8},{8,0},{16,24},{24,16},{1,9},{9,1},{17,25},{25,17},{2,10},{10... | collective-permute-start | bytes 98312 | tf_op jit(solution)/shard_map/ppermute | solution.py:202
  48.1 1.5 %collective-permute-start.28 = (bf16[64,256]{1,0:T(8,128)(2,1)S(1)}, bf16[64,256]{1,0:T(8,128)(2,1)S(1)}, u32[]{:S(2)}, u32[]{:S(2)}) collective-permute-start(bf16[64,256]{1,0:T(8,128)(2,1)S(1)} %get-tuple-element.28), channel_id=1, source_target_pairs={{0,24},{8,16},{16,8},{24,0},{1,25},{9,17},{17,9},{25,1},{2,26},{10... | collective-permute-start | bytes 98312 | tf_op jit(solution)/shard_map/ppermute | solution.py:202
  49.6 0.6 collective-permute-start.27
  50.3 1.4 %collective-permute-start.23 = (bf16[256,256]{1,0:T(8,128)(2,1)S(1)}, bf16[256,256]{1,0:T(8,128)(2,1)S(1)}, u32[]{:S(2)}, u32[]{:S(2)}) collective-permute-start(bf16[256,256]{1,0:T(8,128)(2,1)S(1)} %get-tuple-element.19), channel_id=1, source_target_pairs={{0,6},{1,7},{2,4},{3,5},{4,2},{5,3},{6,0},{7,1},{8,14},{9,15},{10,... | collective-permute-start | bytes 393224 | tf_op jit(solution)/shard_map/ppermute | solution.py:199
  51.7 1.2 %collective-permute-start.22 = (bf16[256,256]{1,0:T(8,128)(2,1)S(1)}, bf16[256,256]{1,0:T(8,128)(2,1)S(1)}, u32[]{:S(2)}, u32[]{:S(2)}) collective-permute-start(bf16[256,256]{1,0:T(8,128)(2,1)S(1)} %get-tuple-element.20), channel_id=1, source_target_pairs={{0,4},{1,5},{2,6},{3,7},{4,0},{5,1},{6,2},{7,3},{8,12},{9,13},{10,... | collective-permute-start | bytes 393224 | tf_op jit(solution)/shard_map/ppermute | solution.py:199
  52.9 1.9 %collective-permute-start.21 = (bf16[256,256]{1,0:T(8,128)(2,1)S(1)}, bf16[256,256]{1,0:T(8,128)(2,1)S(1)}, u32[]{:S(2)}, u32[]{:S(2)}) collective-permute-start(bf16[256,256]{1,0:T(8,128)(2,1)S(1)} %get-tuple-element.21), channel_id=1, source_target_pairs={{0,2},{1,3},{2,0},{3,1},{4,6},{5,7},{6,4},{7,5},{8,10},{9,11},{10,... | collective-permute-start | bytes 393224 | tf_op jit(solution)/shard_map/ppermute | solution.py:199
  54.8 1.4 %collective-permute-start.31 = (bf16[64,256]{1,0:T(8,128)(2,1)S(1)}, bf16[64,256]{1,0:T(8,128)(2,1)S(1)}, u32[]{:S(2)}, u32[]{:S(2)}) collective-permute-start(bf16[64,256]{1,0:T(8,128)(2,1)S(1)} %fusion.7.refs_0_), channel_id=1, source_target_pairs={{0,6},{1,7},{2,4},{3,5},{4,2},{5,3},{6,0},{7,1},{8,14},{9,15},{10,... | collective-permute-start | bytes 98312 | tf_op jit(solution)/shard_map/ppermute | solution.py:199
  56.5 2.2 %collective-permute-done.23.refs_3_ = bf16[256,256]{1,0:T(8,128)(2,1)S(1)} collective-permute-done((bf16[256,256]{1,0:T(8,128)(2,1)S(1)}, bf16[256,256]{1,0:T(8,128)(2,1)S(1)}, u32[]{:S(2)}, u32[]{:S(2)}) %collective-permute-start.23) | collective-permute-done | bytes 131104 | tf_op jit(solution)/shard_map/ppermute | solution.py:199
  58.6 5.3 %collective-permute-start.29 = (bf16[64,256]{1,0:T(8,128)(2,1)S(1)}, bf16[64,256]{1,0:T(8,128)(2,1)S(1)}, u32[]{:S(2)}, u32[]{:S(2)}) collective-permute-start(bf16[64,256]{1,0:T(8,128)(2,1)S(1)} %fusion.7.refs_0_), channel_id=1, source_target_pairs={{0,2},{1,3},{2,0},{3,1},{4,6},{5,7},{6,4},{7,5},{8,10},{9,11},{10,... | collective-permute-start | bytes 98312 | tf_op jit(solution)/shard_map/ppermute | solution.py:199
  63.9 2.3 %collective-permute-done.22.refs_2_ = bf16[256,256]{1,0:T(8,128)(2,1)S(1)} collective-permute-done((bf16[256,256]{1,0:T(8,128)(2,1)S(1)}, bf16[256,256]{1,0:T(8,128)(2,1)S(1)}, u32[]{:S(2)}, u32[]{:S(2)}) %collective-permute-start.22) | collective-permute-done | bytes 131104 | tf_op jit(solution)/shard_map/ppermute | solution.py:199
  66.2 0.9 %node_gradient.1 = (bf16[256,256]{1,0:T(8,128)(2,1)}, bf16[16,128]{1,0:T(8,128)(2,1)S(1)}) custom-call(bf16[256,256]{1,0:T(8,128)(2,1)S(1)} %get-tuple-element.22.refs_0_, bf16[256,256]{1,0:T(8,128)(2,1)S(1)} %collective-permute-done.21.refs_1_, bf16[256,256]{1,0:T(8,128)(2,1)S(1)} %collective-permute-done.22.refs_2_, ...), custom_call_target="tpu_custom_call" | custom-call | tf_op jit(solution)/shard_map/node_gradient/pallas_call | solution.py:141
  67.1 1.5 %collective-permute-start.34 = (bf16[64,256]{1,0:T(8,128)(2,1)S(1)}, bf16[64,256]{1,0:T(8,128)(2,1)S(1)}, u32[]{:S(2)}, u32[]{:S(2)}) collective-permute-start(bf16[64,256]{1,0:T(8,128)(2,1)S(1)} %joined.1), channel_id=1, source_target_pairs={{0,24},{8,16},{16,8},{24,0},{1,25},{9,17},{17,9},{25,1},{2,26},{10... | collective-permute-start | bytes 98312 | tf_op jit(solution)/shard_map/ppermute | solution.py:202
  68.6 1.5 %collective-permute-start.33 = (bf16[64,256]{1,0:T(8,128)(2,1)S(1)}, bf16[64,256]{1,0:T(8,128)(2,1)S(1)}, u32[]{:S(2)}, u32[]{:S(2)}) collective-permute-start(bf16[64,256]{1,0:T(8,128)(2,1)S(1)} %joined.1), channel_id=1, source_target_pairs={{0,16},{8,24},{16,0},{24,8},{1,17},{9,25},{17,1},{25,9},{2,18},{10... | collective-permute-start | bytes 98312 | tf_op jit(solution)/shard_map/ppermute | solution.py:202
  70.0 0.6 collective-permute-start.32
  70.6 1.3 %collective-permute-done.34 = bf16[64,256]{1,0:T(8,128)(2,1)S(1)} collective-permute-done((bf16[64,256]{1,0:T(8,128)(2,1)S(1)}, bf16[64,256]{1,0:T(8,128)(2,1)S(1)}, u32[]{:S(2)}, u32[]{:S(2)}) %collective-permute-start.34) | collective-permute-done | bytes 32800 | tf_op jit(solution)/shard_map/ppermute | solution.py:202
  72.0 0.5 collective-permute-done.33
  72.5 1.5 %collective-permute-done.32 = bf16[64,256]{1,0:T(8,128)(2,1)S(1)} collective-permute-done((bf16[64,256]{1,0:T(8,128)(2,1)S(1)}, bf16[64,256]{1,0:T(8,128)(2,1)S(1)}, u32[]{:S(2)}, u32[]{:S(2)}) %collective-permute-start.32) | collective-permute-done | bytes 32800 | tf_op jit(solution)/shard_map/ppermute | solution.py:202
  74.3 1.5 %collective-permute-done.35 = f32[128,2,256]{2,1,0:T(2,128)S(1)} collective-permute-done((f32[128,2,256]{2,1,0:T(2,128)S(1)}, f32[128,2,256]{2,1,0:T(2,128)S(1)}, u32[]{:S(2)}, u32[]{:S(2)}) %collective-permute-start.35) | collective-permute-done | bytes 262176 | tf_op jit(solution)/shard_map/ppermute | solution.py:199
  76.3 0.8 %copy_bitcast_fusion = (f32[256,256]{1,0:T(8,128)}, f32[256,256]{1,0:T(8,128)}) fusion(f32[256,1,256]{2,1,0:T(1,128)S(1)} %get-tuple-element.15, f32[256,1,256]{2,1,0:T(1,128)S(1)} %get-tuple-element.16), kind=kLoop, calls=%fused_computation.9 | loop fusion | bytes 1048576
  (81 shorter events, 3.1 us)
Async XLA Ops:
  0.6 36.7 %copy-start = (bf16[256,256]{1,0:T(8,128)(2,1)S(1)}, bf16[256,256]{1,0:T(8,128)(2,1)}, u32[]{:S(2)}) copy-start(bf16[256,256]{1,0:T(8,128)(2,1)} %param.13) | copy-start | bytes 393220
  0.6 14.8 %copy-start.1 = (bf16[256,256]{1,0:T(8,128)(2,1)S(1)}, bf16[256,256]{1,0:T(8,128)(2,1)}, u32[]{:S(2)}) copy-start(bf16[256,256]{1,0:T(8,128)(2,1)} %value.1) | copy-start | bytes 393220
  1.7 13.8 %collective-permute-start.5 = (bf16[256,256]{1,0:T(8,128)(2,1)S(1)}, bf16[256,256]{1,0:T(8,128)(2,1)S(1)}, u32[]{:S(2)}, u32[]{:S(2)}) collective-permute-start(bf16[256,256]{1,0:T(8,128)(2,1)S(1)} %compare_select_fusion.value.refs_1_), channel_id=1, source_target_pairs={{0,6},{1,7},{2,4},{3,5},{4,2},{5,3},{6,0},{7,1},{8,14},{9,15},{10,... | collective-permute-start | bytes 393224 | tf_op jit(solution)/shard_map/ppermute | solution.py:199
  6.8 11.2 %collective-permute-start.3 = (bf16[256,256]{1,0:T(8,128)(2,1)S(1)}, bf16[256,256]{1,0:T(8,128)(2,1)S(1)}, u32[]{:S(2)}, u32[]{:S(2)}) collective-permute-start(bf16[256,256]{1,0:T(8,128)(2,1)S(1)} %compare_select_fusion.value.refs_1_), channel_id=1, source_target_pairs={{0,4},{1,5},{2,6},{3,7},{4,0},{5,1},{6,2},{7,3},{8,12},{9,13},{10,... | collective-permute-start | bytes 393224 | tf_op jit(solution)/shard_map/ppermute | solution.py:199
  6.8 11.2 %collective-permute-start.1 = (bf16[256,256]{1,0:T(8,128)(2,1)S(1)}, bf16[256,256]{1,0:T(8,128)(2,1)S(1)}, u32[]{:S(2)}, u32[]{:S(2)}) collective-permute-start(bf16[256,256]{1,0:T(8,128)(2,1)S(1)} %compare_select_fusion.value.refs_1_), channel_id=1, source_target_pairs={{0,2},{1,3},{2,0},{3,1},{4,6},{5,7},{6,4},{7,5},{8,10},{9,11},{10,... | collective-permute-start | bytes 393224 | tf_op jit(solution)/shard_map/ppermute | solution.py:199
  7.5 13.8 %collective-permute-start.10 = (bf16[256,256]{1,0:T(8,128)(2,1)}, bf16[256,256]{1,0:T(8,128)(2,1)S(1)}, u32[]{:S(2)}, u32[]{:S(2)}) collective-permute-start(bf16[256,256]{1,0:T(8,128)(2,1)} %value.1), channel_id=1, source_target_pairs={{0,2},{1,3},{2,0},{3,1},{4,6},{5,7},{6,4},{7,5},{8,10},{9,11},{10,... | collective-permute-start | bytes 393224 | tf_op jit(solution)/shard_map/ppermute | solution.py:199
  8.8 11.9 %collective-permute-start.14 = (bf16[256,256]{1,0:T(8,128)(2,1)}, bf16[256,256]{1,0:T(8,128)(2,1)S(1)}, u32[]{:S(2)}, u32[]{:S(2)}) collective-permute-start(bf16[256,256]{1,0:T(8,128)(2,1)} %value.1), channel_id=1, source_target_pairs={{0,1},{1,0},{2,3},{3,2},{4,5},{5,4},{6,7},{7,6},{8,9},{9,8},{10,11... | collective-permute-start | bytes 393224 | tf_op jit(solution)/shard_map/ppermute | solution.py:199
  15.5 5.9 %collective-permute-start = (bf16[256,256]{1,0:T(8,128)(2,1)S(1)}, bf16[256,256]{1,0:T(8,128)(2,1)S(1)}, u32[]{:S(2)}, u32[]{:S(2)}) collective-permute-start(bf16[256,256]{1,0:T(8,128)(2,1)S(1)} %after.5), channel_id=1, source_target_pairs={{0,1},{1,0},{2,3},{3,2},{4,5},{5,4},{6,7},{7,6},{8,9},{9,8},{10,11... | collective-permute-start | bytes 393224 | tf_op jit(solution)/shard_map/ppermute | solution.py:199
  18.0 9.1 %collective-permute-start.18 = (bf16[256,256]{1,0:T(8,128)(2,1)S(1)}, bf16[256,256]{1,0:T(8,128)(2,1)S(1)}, u32[]{:S(2)}, u32[]{:S(2)}) collective-permute-start(bf16[256,256]{1,0:T(8,128)(2,1)S(1)} %after.9), channel_id=1, source_target_pairs={{0,6},{1,7},{2,4},{3,5},{4,2},{5,3},{6,0},{7,1},{8,14},{9,15},{10,... | collective-permute-start | bytes 393224 | tf_op jit(solution)/shard_map/ppermute | solution.py:199
  20.6 13.0 %copy-start.2 = (bf16[256,256]{1,0:T(8,128)(2,1)S(1)}, bf16[256,256]{1,0:T(8,128)(2,1)}, u32[]{:S(2)}) copy-start(bf16[256,256]{1,0:T(8,128)(2,1)} %refs_4_.2) | copy-start | bytes 393220
  20.6 13.0 %copy-start.3 = (bf16[256,256]{1,0:T(8,128)(2,1)S(1)}, bf16[256,256]{1,0:T(8,128)(2,1)}, u32[]{:S(2)}) copy-start(bf16[256,256]{1,0:T(8,128)(2,1)} %refs_5_.1) | copy-start | bytes 393220
  20.6 1.4 %collective-permute-start.2 = (bf16[256,256]{1,0:T(8,128)(2,1)S(1)}, bf16[256,256]{1,0:T(8,128)(2,1)S(1)}, u32[]{:S(2)}, u32[]{:S(2)}) collective-permute-start(bf16[256,256]{1,0:T(8,128)(2,1)S(1)} %after.6), channel_id=1, source_target_pairs={{0,1},{1,0},{2,3},{3,2},{4,5},{5,4},{6,7},{7,6},{8,9},{9,8},{10,11... | collective-permute-start | bytes 393224 | tf_op jit(solution)/shard_map/ppermute | solution.py:199
  20.7 1.5 %collective-permute-start.4 = (bf16[256,256]{1,0:T(8,128)(2,1)S(1)}, bf16[256,256]{1,0:T(8,128)(2,1)S(1)}, u32[]{:S(2)}, u32[]{:S(2)}) collective-permute-start(bf16[256,256]{1,0:T(8,128)(2,1)S(1)} %after.7), channel_id=1, source_target_pairs={{0,1},{1,0},{2,3},{3,2},{4,5},{5,4},{6,7},{7,6},{8,9},{9,8},{10,11... | collective-permute-start | bytes 393224 | tf_op jit(solution)/shard_map/ppermute | solution.py:199
  21.3 1.4 %collective-permute-start.6 = (bf16[256,256]{1,0:T(8,128)(2,1)S(1)}, bf16[256,256]{1,0:T(8,128)(2,1)S(1)}, u32[]{:S(2)}, u32[]{:S(2)}) collective-permute-start(bf16[256,256]{1,0:T(8,128)(2,1)S(1)} %after.8), channel_id=1, source_target_pairs={{0,1},{1,0},{2,3},{3,2},{4,5},{5,4},{6,7},{7,6},{8,9},{9,8},{10,11... | collective-permute-start | bytes 393224 | tf_op jit(solution)/shard_map/ppermute | solution.py:199
  21.4 9.9 %collective-permute-start.16 = (bf16[256,256]{1,0:T(8,128)(2,1)S(1)}, bf16[256,256]{1,0:T(8,128)(2,1)S(1)}, u32[]{:S(2)}, u32[]{:S(2)}) collective-permute-start(bf16[256,256]{1,0:T(8,128)(2,1)S(1)} %after.9), channel_id=1, source_target_pairs={{0,4},{1,5},{2,6},{3,7},{4,0},{5,1},{6,2},{7,3},{8,12},{9,13},{10,... | collective-permute-start | bytes 393224 | tf_op jit(solution)/shard_map/ppermute | solution.py:199
  22.0 9.3 %collective-permute-start.15 = (bf16[256,256]{1,0:T(8,128)(2,1)S(1)}, bf16[256,256]{1,0:T(8,128)(2,1)S(1)}, u32[]{:S(2)}, u32[]{:S(2)}) collective-permute-start(bf16[256,256]{1,0:T(8,128)(2,1)S(1)} %collective-permute-done.10.refs_6_), channel_id=1, source_target_pairs={{0,1},{1,0},{2,3},{3,2},{4,5},{5,4},{6,7},{7,6},{8,9},{9,8},{10,11... | collective-permute-start | bytes 393224 | tf_op jit(solution)/shard_map/ppermute | solution.py:199
  24.1 7.8 %collective-permute-start.9 = (bf16[256,256]{1,0:T(8,128)(2,1)S(1)}, bf16[256,256]{1,0:T(8,128)(2,1)S(1)}, u32[]{:S(2)}, u32[]{:S(2)}) collective-permute-start(bf16[256,256]{1,0:T(8,128)(2,1)S(1)} %get-tuple-element.23), channel_id=1, source_target_pairs={{0,24},{8,16},{16,8},{24,0},{1,25},{9,17},{17,9},{25,1},{2,26},{10... | collective-permute-start | bytes 393224 | tf_op jit(solution)/shard_map/ppermute | solution.py:202
  26.6 6.8 %collective-permute-start.8 = (bf16[256,256]{1,0:T(8,128)(2,1)S(1)}, bf16[256,256]{1,0:T(8,128)(2,1)S(1)}, u32[]{:S(2)}, u32[]{:S(2)}) collective-permute-start(bf16[256,256]{1,0:T(8,128)(2,1)S(1)} %get-tuple-element.24), channel_id=1, source_target_pairs={{0,16},{8,24},{16,0},{24,8},{1,17},{9,25},{17,1},{25,9},{2,18},{10... | collective-permute-start | bytes 393224 | tf_op jit(solution)/shard_map/ppermute | solution.py:202
  27.1 6.4 %collective-permute-start.7 = (bf16[256,256]{1,0:T(8,128)(2,1)S(1)}, bf16[256,256]{1,0:T(8,128)(2,1)S(1)}, u32[]{:S(2)}, u32[]{:S(2)}) collective-permute-start(bf16[256,256]{1,0:T(8,128)(2,1)S(1)} %get-tuple-element.25), channel_id=1, source_target_pairs={{0,8},{8,0},{16,24},{24,16},{1,9},{9,1},{17,25},{25,17},{2,10},{10... | collective-permute-start | bytes 393224 | tf_op jit(solution)/shard_map/ppermute | solution.py:202
  31.3 6.4 %collective-permute-start.19 = (bf16[256,256]{1,0:T(8,128)(2,1)S(1)}, bf16[256,256]{1,0:T(8,128)(2,1)S(1)}, u32[]{:S(2)}, u32[]{:S(2)}) collective-permute-start(bf16[256,256]{1,0:T(8,128)(2,1)S(1)} %collective-permute-done.18), channel_id=1, source_target_pairs={{0,1},{1,0},{2,3},{3,2},{4,5},{5,4},{6,7},{7,6},{8,9},{9,8},{10,11... | collective-permute-start | bytes 393224 | tf_op jit(solution)/shard_map/ppermute | solution.py:199
  31.3 6.2 %collective-permute-start.17 = (bf16[256,256]{1,0:T(8,128)(2,1)S(1)}, bf16[256,256]{1,0:T(8,128)(2,1)S(1)}, u32[]{:S(2)}, u32[]{:S(2)}) collective-permute-start(bf16[256,256]{1,0:T(8,128)(2,1)S(1)} %collective-permute-done.16), channel_id=1, source_target_pairs={{0,1},{1,0},{2,3},{3,2},{4,5},{5,4},{6,7},{7,6},{8,9},{9,8},{10,11... | collective-permute-start | bytes 393224 | tf_op jit(solution)/shard_map/ppermute | solution.py:199
  33.8 7.4 %collective-permute-start.13 = (bf16[256,256]{1,0:T(8,128)(2,1)S(1)}, bf16[256,256]{1,0:T(8,128)(2,1)S(1)}, u32[]{:S(2)}, u32[]{:S(2)}) collective-permute-start(bf16[256,256]{1,0:T(8,128)(2,1)S(1)} %get-tuple-element.11.refs_1_), channel_id=1, source_target_pairs={{0,24},{8,16},{16,8},{24,0},{1,25},{9,17},{17,9},{25,1},{2,26},{10... | collective-permute-start | bytes 393224 | tf_op jit(solution)/shard_map/ppermute | solution.py:202
  35.5 7.4 %collective-permute-start.12 = (bf16[256,256]{1,0:T(8,128)(2,1)S(1)}, bf16[256,256]{1,0:T(8,128)(2,1)S(1)}, u32[]{:S(2)}, u32[]{:S(2)}) collective-permute-start(bf16[256,256]{1,0:T(8,128)(2,1)S(1)} %get-tuple-element.11.refs_1_), channel_id=1, source_target_pairs={{0,16},{8,24},{16,0},{24,8},{1,17},{9,25},{17,1},{25,9},{2,18},{10... | collective-permute-start | bytes 393224 | tf_op jit(solution)/shard_map/ppermute | solution.py:202
  36.8 6.2 %collective-permute-start.11 = (bf16[256,256]{1,0:T(8,128)(2,1)S(1)}, bf16[256,256]{1,0:T(8,128)(2,1)S(1)}, u32[]{:S(2)}, u32[]{:S(2)}) collective-permute-start(bf16[256,256]{1,0:T(8,128)(2,1)S(1)} %get-tuple-element.11.refs_1_), channel_id=1, source_target_pairs={{0,8},{8,0},{16,24},{24,16},{1,9},{9,1},{17,25},{25,17},{2,10},{10... | collective-permute-start | bytes 393224 | tf_op jit(solution)/shard_map/ppermute | solution.py:202
  37.6 1.3 %collective-permute-start.25 = (bf16[128,256]{1,0:T(8,128)(2,1)S(1)}, bf16[128,256]{1,0:T(8,128)(2,1)S(1)}, u32[]{:S(2)}, u32[]{:S(2)}) collective-permute-start(bf16[128,256]{1,0:T(8,128)(2,1)S(1)} %select_convert_fusion), channel_id=1, source_target_pairs={{0,1},{1,0},{2,3},{3,2},{4,5},{5,4},{6,7},{7,6},{8,9},{9,8},{10,11... | collective-permute-start | bytes 196616 | tf_op jit(solution)/shard_map/ppermute | solution.py:199
  44.4 21.8 %copy-start.4 = (bf16[256,256]{1,0:T(8,128)(2,1)S(1)}, bf16[256,256]{1,0:T(8,128)(2,1)}, u32[]{:S(2)}) copy-start(bf16[256,256]{1,0:T(8,128)(2,1)} %refs_4_.3) | copy-start | bytes 393220
  44.9 1.3 %collective-permute-start.24 = (bf16[128,256]{1,0:T(8,128)(2,1)S(1)}, bf16[128,256]{1,0:T(8,128)(2,1)S(1)}, u32[]{:S(2)}, u32[]{:S(2)}) collective-permute-start(bf16[128,256]{1,0:T(8,128)(2,1)S(1)} %select_convert_fusion.1), channel_id=1, source_target_pairs={{0,1},{1,0},{2,3},{3,2},{4,5},{5,4},{6,7},{7,6},{8,9},{9,8},{10,11... | collective-permute-start | bytes 196616 | tf_op jit(solution)/shard_map/ppermute | solution.py:199
  45.0 5.1 %collective-permute-start.20 = (bf16[4,256,256]{2,1,0:T(8,128)(2,1)S(1)}, bf16[4,256,256]{2,1,0:T(8,128)(2,1)S(1)}, u32[]{:S(2)}, u32[]{:S(2)}) collective-permute-start(bf16[4,256,256]{2,1,0:T(8,128)(2,1)S(1)} %slice_bitcast_fusion), channel_id=1, source_target_pairs={{0,1},{1,0},{2,3},{3,2},{4,5},{5,4},{6,7},{7,6},{8,9},{9,8},{10,11... | collective-permute-start | bytes 1572872 | tf_op jit(solution)/shard_map/ppermute | solution.py:199
  46.6 6.3 %collective-permute-start.26 = (bf16[64,256]{1,0:T(8,128)(2,1)S(1)}, bf16[64,256]{1,0:T(8,128)(2,1)S(1)}, u32[]{:S(2)}, u32[]{:S(2)}) collective-permute-start(bf16[64,256]{1,0:T(8,128)(2,1)S(1)} %get-tuple-element.27), channel_id=1, source_target_pairs={{0,8},{8,0},{16,24},{24,16},{1,9},{9,1},{17,25},{25,17},{2,10},{10... | collective-permute-start | bytes 98312 | tf_op jit(solution)/shard_map/ppermute | solution.py:202
  48.1 6.7 %collective-permute-start.28 = (bf16[64,256]{1,0:T(8,128)(2,1)S(1)}, bf16[64,256]{1,0:T(8,128)(2,1)S(1)}, u32[]{:S(2)}, u32[]{:S(2)}) collective-permute-start(bf16[64,256]{1,0:T(8,128)(2,1)S(1)} %get-tuple-element.28), channel_id=1, source_target_pairs={{0,24},{8,16},{16,8},{24,0},{1,25},{9,17},{17,9},{25,1},{2,26},{10... | collective-permute-start | bytes 98312 | tf_op jit(solution)/shard_map/ppermute | solution.py:202
  49.6 5.2 %collective-permute-start.27 = (bf16[64,256]{1,0:T(8,128)(2,1)S(1)}, bf16[64,256]{1,0:T(8,128)(2,1)S(1)}, u32[]{:S(2)}, u32[]{:S(2)}) collective-permute-start(bf16[64,256]{1,0:T(8,128)(2,1)S(1)} %get-tuple-element.29), channel_id=1, source_target_pairs={{0,16},{8,24},{16,0},{24,8},{1,17},{9,25},{17,1},{25,9},{2,18},{10... | collective-permute-start | bytes 98312 | tf_op jit(solution)/shard_map/ppermute | solution.py:202
  50.3 8.3 %collective-permute-start.23 = (bf16[256,256]{1,0:T(8,128)(2,1)S(1)}, bf16[256,256]{1,0:T(8,128)(2,1)S(1)}, u32[]{:S(2)}, u32[]{:S(2)}) collective-permute-start(bf16[256,256]{1,0:T(8,128)(2,1)S(1)} %get-tuple-element.19), channel_id=1, source_target_pairs={{0,6},{1,7},{2,4},{3,5},{4,2},{5,3},{6,0},{7,1},{8,14},{9,15},{10,... | collective-permute-start | bytes 393224 | tf_op jit(solution)/shard_map/ppermute | solution.py:199
  51.7 14.4 %collective-permute-start.22 = (bf16[256,256]{1,0:T(8,128)(2,1)S(1)}, bf16[256,256]{1,0:T(8,128)(2,1)S(1)}, u32[]{:S(2)}, u32[]{:S(2)}) collective-permute-start(bf16[256,256]{1,0:T(8,128)(2,1)S(1)} %get-tuple-element.20), channel_id=1, source_target_pairs={{0,4},{1,5},{2,6},{3,7},{4,0},{5,1},{6,2},{7,3},{8,12},{9,13},{10,... | collective-permute-start | bytes 393224 | tf_op jit(solution)/shard_map/ppermute | solution.py:199
  52.9 13.3 %collective-permute-start.21 = (bf16[256,256]{1,0:T(8,128)(2,1)S(1)}, bf16[256,256]{1,0:T(8,128)(2,1)S(1)}, u32[]{:S(2)}, u32[]{:S(2)}) collective-permute-start(bf16[256,256]{1,0:T(8,128)(2,1)S(1)} %get-tuple-element.21), channel_id=1, source_target_pairs={{0,2},{1,3},{2,0},{3,1},{4,6},{5,7},{6,4},{7,5},{8,10},{9,11},{10,... | collective-permute-start | bytes 393224 | tf_op jit(solution)/shard_map/ppermute | solution.py:199
  54.8 12.2 %collective-permute-start.31 = (bf16[64,256]{1,0:T(8,128)(2,1)S(1)}, bf16[64,256]{1,0:T(8,128)(2,1)S(1)}, u32[]{:S(2)}, u32[]{:S(2)}) collective-permute-start(bf16[64,256]{1,0:T(8,128)(2,1)S(1)} %fusion.7.refs_0_), channel_id=1, source_target_pairs={{0,6},{1,7},{2,4},{3,5},{4,2},{5,3},{6,0},{7,1},{8,14},{9,15},{10,... | collective-permute-start | bytes 98312 | tf_op jit(solution)/shard_map/ppermute | solution.py:199
  56.2 10.8 %collective-permute-start.30 = (bf16[64,256]{1,0:T(8,128)(2,1)S(1)}, bf16[64,256]{1,0:T(8,128)(2,1)S(1)}, u32[]{:S(2)}, u32[]{:S(2)}) collective-permute-start(bf16[64,256]{1,0:T(8,128)(2,1)S(1)} %fusion.7.refs_0_), channel_id=1, source_target_pairs={{0,4},{1,5},{2,6},{3,7},{4,0},{5,1},{6,2},{7,3},{8,12},{9,13},{10,... | collective-permute-start | bytes 98312 | tf_op jit(solution)/shard_map/ppermute | solution.py:199
  58.6 8.4 %collective-permute-start.29 = (bf16[64,256]{1,0:T(8,128)(2,1)S(1)}, bf16[64,256]{1,0:T(8,128)(2,1)S(1)}, u32[]{:S(2)}, u32[]{:S(2)}) collective-permute-start(bf16[64,256]{1,0:T(8,128)(2,1)S(1)} %fusion.7.refs_0_), channel_id=1, source_target_pairs={{0,2},{1,3},{2,0},{3,1},{4,6},{5,7},{6,4},{7,5},{8,10},{9,11},{10,... | collective-permute-start | bytes 98312 | tf_op jit(solution)/shard_map/ppermute | solution.py:199
  67.1 4.9 %collective-permute-start.34 = (bf16[64,256]{1,0:T(8,128)(2,1)S(1)}, bf16[64,256]{1,0:T(8,128)(2,1)S(1)}, u32[]{:S(2)}, u32[]{:S(2)}) collective-permute-start(bf16[64,256]{1,0:T(8,128)(2,1)S(1)} %joined.1), channel_id=1, source_target_pairs={{0,24},{8,16},{16,8},{24,0},{1,25},{9,17},{17,9},{25,1},{2,26},{10... | collective-permute-start | bytes 98312 | tf_op jit(solution)/shard_map/ppermute | solution.py:202
  68.6 3.9 %collective-permute-start.33 = (bf16[64,256]{1,0:T(8,128)(2,1)S(1)}, bf16[64,256]{1,0:T(8,128)(2,1)S(1)}, u32[]{:S(2)}, u32[]{:S(2)}) collective-permute-start(bf16[64,256]{1,0:T(8,128)(2,1)S(1)} %joined.1), channel_id=1, source_target_pairs={{0,16},{8,24},{16,0},{24,8},{1,17},{9,25},{17,1},{25,9},{2,18},{10... | collective-permute-start | bytes 98312 | tf_op jit(solution)/shard_map/ppermute | solution.py:202
  70.0 3.9 %collective-permute-start.32 = (bf16[64,256]{1,0:T(8,128)(2,1)S(1)}, bf16[64,256]{1,0:T(8,128)(2,1)S(1)}, u32[]{:S(2)}, u32[]{:S(2)}) collective-permute-start(bf16[64,256]{1,0:T(8,128)(2,1)S(1)} %joined.1), channel_id=1, source_target_pairs={{0,8},{8,0},{16,24},{24,16},{1,9},{9,1},{17,25},{25,17},{2,10},{10... | collective-permute-start | bytes 98312 | tf_op jit(solution)/shard_map/ppermute | solution.py:202
  74.2 1.6 %collective-permute-start.35 = (f32[128,2,256]{2,1,0:T(2,128)S(1)}, f32[128,2,256]{2,1,0:T(2,128)S(1)}, u32[]{:S(2)}, u32[]{:S(2)}) collective-permute-start(f32[128,2,256]{2,1,0:T(2,128)S(1)} %mul.11), channel_id=1, source_target_pairs={{0,1},{1,0},{2,3},{3,2},{4,5},{5,4},{6,7},{7,6},{8,9},{9,8},{10,11... | collective-permute-start | bytes 786440 | tf_op jit(solution)/shard_map/ppermute | solution.py:199

commit v3 on v2

--- a/solution.py
+++ b/solution.py
@@ -128,27 +128,21 @@
     )(*parts, w_two, pre_one, *events)
 
 
-def last_kernel(count, *refs):
-    parts, w_one, out, token = refs[:count], refs[count], refs[-2], refs[-1]
-    total = tree([part[...].astype(F32) for part in parts]).astype(BF16)
+def last_kernel(total, w_one, out):
     out[...] = lax.dot_general(
-        total, w_one[...], LAST_LAST, preferred_element_type=F32
+        total[...], w_one[...], LAST_LAST, preferred_element_type=F32
     ).astype(BF16)
-    token[...] = total[: token.shape[0], : token.shape[1]]
-
-
-def last(parts, w_one):
-    return pl.pallas_call(
-        functools.partial(last_kernel, len(parts)),
-        in_specs=whole(len(parts) + 1),
-        out_specs=whole(2),
-        out_shape=[
-            jax.ShapeDtypeStruct(parts[0].shape, BF16),
-            jax.ShapeDtypeStruct((16, 128), BF16),
-        ],
+
+
+def last(total, w_one):
+    return pl.pallas_call(
+        last_kernel,
+        in_specs=whole(2),
+        out_specs=pl.BlockSpec(memory_space=VMEM),
+        out_shape=jax.ShapeDtypeStruct(total.shape, BF16),
         compiler_params=params(),
         name="node_gradient",
-    )(*parts, w_one)
+    )(total, w_one)
 
 
 def copy_kernel(value, *refs):
@@ -167,25 +161,38 @@
 
 
 def joined_kernel(count, *refs):
-    refs[-1][...] = tree([ref[...].astype(F32) for ref in refs[:count]]).astype(BF16)
-
-
-def joined(values, *events):
+    out = refs[-1]
+    out[...] = tree([ref[...].astype(F32) for ref in refs[:count]]).astype(out.dtype)
+
+
+def joined(values, *events, dtype=BF16):
     return pl.pallas_call(
         functools.partial(joined_kernel, len(values)),
         in_specs=whole(len(values)) + unread(events),
         out_specs=pl.BlockSpec(memory_space=VMEM),
-        out_shape=jax.ShapeDtypeStruct(values[0].shape, BF16),
+        out_shape=jax.ShapeDtypeStruct(values[0].shape, dtype),
         compiler_params=params(),
         name="joined",
     )(*values, *events)
 
 
-def xor_order(blocks, bits):
-    for position, bit in enumerate(bits):
-        split = blocks.reshape((-1, 2, 1 << position) + blocks.shape[1:])
-        blocks = jnp.where(bit, split[:, ::-1], split).reshape(blocks.shape)
-    return blocks
+def scaled_kernel(scale, odd, mine, other, *outs):
+    half = mine.shape[1]
+    for i, out in enumerate(outs):
+        out[pl.ds(pl.multiple_of(odd[0] * half, half), half)] = mine[i] * scale
+        out[pl.ds(pl.multiple_of((1 - odd[0]) * half, half), half)] = other[i] * scale
+
+
+def scaled(odd, mine, other, scale):
+    count, half, width = mine.shape
+    return pl.pallas_call(
+        functools.partial(scaled_kernel, scale),
+        in_specs=[pl.BlockSpec(memory_space=pltpu.SMEM)] + whole(2),
+        out_specs=whole(count),
+        out_shape=[jax.ShapeDtypeStruct((2 * half, width), F32)] * count,
+        compiler_params=params(),
+        name="weight_gradients",
+    )(odd, mine, other)
 
 
 def local(n_row, n_col, adjacency, tile_mask, out_grad, pre_two, hidden, pre_one, features, w_two, w_one):
@@ -241,7 +248,8 @@
     chip_part = row_part[:, 0].astype(F32) + crossed.astype(F32)
     chip_part = chip_part.astype(BF16)
     ends = far(chip_part)
-    node_grad, token = last(ends, w_one)
+    prop_one = joined(ends)
+    node_grad = last(prop_one, w_one)
 
     term_two = lax.dot_general(hidden, prop_two, ROWS_COLS, preferred_element_type=F32)
     term_one = lax.dot_general(
@@ -250,19 +258,16 @@
         ROWS_COLS,
         preferred_element_type=F32,
     )
-    width = term_one.shape[1]
-    terms = jnp.stack([halved(term_one), halved(term_two)], axis=1)
-    terms = terms.reshape(n_row, -1, width)
-    row_bits = [jnp.bitwise_and(row, 1 << b) > 0 for b in range(n_row.bit_length() - 1)]
-    terms = xor_order(terms, row_bits)
-    total = tree([value.astype(F32) for value in rows_all(terms)]).astype(BF16)
-    total = joined([total] + [over_col(total, 2 * j) for j in range(1, n_far)], token)
-    total = xor_order(jnp.stack(rows_all([total] * n_row)), row_bits)
-    total = total.reshape(-1, 2, width).astype(F32) * scale
-    other = over_col(total, 1)
-    lower, upper = jnp.where(odd, other, total), jnp.where(odd, total, other)
-    total = jnp.concatenate([lower, upper], axis=0)
-    return node_grad, total[:, 0], total[:, 1]
+    low, high = range(1, n_col.bit_length() - 2), n_col.bit_length() - 2
+    ahead = halved(term_two)
+    ahead = joined([ahead, over_col(ahead, 1 << high)])
+    total = joined(rows_all([jnp.stack([halved(term_one), ahead])] * n_row))
+    for bit in low:
+        total = joined([total, over_col(total, 1 << bit)], prop_one)
+    one = joined([total[0], over_col(total[0], 1 << high)], dtype=F32)
+    total = jnp.stack([one, total[1].astype(F32)])
+    odd = jnp.bitwise_and(col, 1).reshape(1)
+    return node_grad, *scaled(odd, total, over_col(total, 1), scale)
 
 
 def solution(mesh):

time: 77.4 us -> 73.9 us (0.955)
  starting transfers between devices: 38 us -> 30.8 us
  waiting for transfers between devices: 23.5 us -> 28 us
  local copies, waits for them, and re-layouts: 2.16 us -> 0.99 us
  Pallas kernels: 9.8 us -> 10.8 us
    ppermute x24, waiting for transfers between devices: 14.5 us -> 22.7 us  [over_col(): return lax.ppermute(value, 'col', [(i, i ^ flip) for i in range(n_col)])]
    ppermute x12 -> x9, waiting for transfers between devices: 8.97 us -> 5.27 us  [over_row(): return lax.ppermute(value, 'row', [(i, i ^ flip) for i in range(n_row)])]
    ppermute x24, starting transfers between devices: 23.8 us -> 20.1 us  [over_col(): return lax.ppermute(value, 'col', [(i, i ^ flip) for i in range(n_col)])]
    ppermute x12 -> x9, starting transfers between devices: 14.2 us -> 10.7 us  [over_row(): return lax.ppermute(value, 'row', [(i, i ^ flip) for i in range(n_row)])]
    unnamed x19 -> x18, local copies, waits for them, and re-layouts: 1.69 us -> 0.87 us
    pallas_call x1 -> x2, Pallas kernels: 0.88 us -> 1.7 us  [the longest x1 0.88 us: last(): pl.pallas_call(last_kernel, in_specs=whole(2), out_specs=pl.BlockSpec(mem...]
  transfers between devices with their start and end apart: 36 -> 33, of which waited for: 18 -> 18; matrix products, arithmetic and copies ran while one was open for 2% -> 3% of each run, Pallas kernels for 11% -> 13%
where the time goes in v3:
time: 73.9 us; the launch traced here: 73.6 us
  starting transfers between devices  30.8 us (42%)
  waiting for transfers between devices  28 us (38%)
  Pallas kernels  10.8 us (15%)
  other arithmetic  1.3 us (2%)
  between operations  1.03 us (1%)
  local copies, waits for them, and re-layouts  0.99 us (1%)
    ppermute x24, waiting for transfers between devices, over_col(): return lax.ppermute(value, 'col', [(i, i ^ flip) for i in range(n_col)])  22.7 us
    ppermute x24, starting transfers between devices, over_col(): return lax.ppermute(value, 'col', [(i, i ^ flip) for i in range(n_col)])  20.1 us
    ppermute x9, starting transfers between devices, over_row(): return lax.ppermute(value, 'row', [(i, i ^ flip) for i in range(n_row)])  10.7 us
    pallas_call x1, Pallas kernels, masked(): pl.pallas_call(functools.partial(mask_kernel, block, tile), grid_spec=plt...  5.82 us
    ppermute x9, waiting for transfers between devices, over_row(): return lax.ppermute(value, 'row', [(i, i ^ flip) for i in range(n_row)])  5.27 us
    pallas_call x2, Pallas kernels, spread(): pl.pallas_call(functools.partial(spread_kernel, len(parts), turned), in_s...  2.8 us
  transfers between devices with their start and end apart: 33, of which 18 were waited for; matrix products, arithmetic and copies ran while one was open for 3% of the time, Pallas kernels for 13%

profile of v3, /device:TPU:0, one launch (start us, length us, event | category | flops | bytes accessed | tf_op | source)
XLA Modules:
  0.0 73.6 jit_solution(760609924111276852)
XLA Ops:
  0.7 1.0 %compare_select_fusion.value.refs_1_ = bf16[256,256]{1,0:T(8,128)(2,1)S(1)} fusion(bf16[256,256]{1,0:T(8,128)(2,1)} %param.11, bf16[256,256]{1,0:T(8,128)(2,1)} %param.12), kind=kLoop, calls=%fused_computation.6 | loop fusion | flops 131072 | bytes 393216 | tf_op jit(solution)/shard_map/jit(_where)/select_n | solution.py:231
  1.7 5.1 %collective-permute-start.5 = (bf16[256,256]{1,0:T(8,128)(2,1)S(1)}, bf16[256,256]{1,0:T(8,128)(2,1)S(1)}, u32[]{:S(2)}, u32[]{:S(2)}) collective-permute-start(bf16[256,256]{1,0:T(8,128)(2,1)S(1)} %compare_select_fusion.value.refs_1_), channel_id=1, source_target_pairs={{0,6},{1,7},{2,4},{3,5},{4,2},{5,3},{6,0},{7,1},{8,14},{9,15},{10,... | collective-permute-start | bytes 393224 | tf_op jit(solution)/shard_map/ppermute | solution.py:206
  6.8 0.6 collective-permute-start.1
  7.5 1.4 %collective-permute-start.10 = (bf16[256,256]{1,0:T(8,128)(2,1)}, bf16[256,256]{1,0:T(8,128)(2,1)S(1)}, u32[]{:S(2)}, u32[]{:S(2)}) collective-permute-start(bf16[256,256]{1,0:T(8,128)(2,1)} %value.1), channel_id=1, source_target_pairs={{0,2},{1,3},{2,0},{3,1},{4,6},{5,7},{6,4},{7,5},{8,10},{9,11},{10,... | collective-permute-start | bytes 393224 | tf_op jit(solution)/shard_map/ppermute | solution.py:206
  8.9 0.8 %copy.14.mask = s32[16,8]{1,0:T(8,128)S(1)} copy(s32[16,8]{0,1:T(8,128)} %param.10) | data formatting | bytes 1024 | tf_op args[1]
  9.6 5.8 %mask_tiles.1 = (bf16[2048,1024]{1,0:T(8,128)(2,1)S(1)}, bf16[16,128]{1,0:T(8,128)(2,1)S(1)}) custom-call(s32[8]{0:T(128)S(1)} %iota_xor_fusion.1.row_src, s32[4]{0:T(128)S(1)} %iota_xor_fusion.col_src, s32[16,8]{1,0:T(8,128)S(1)} %copy.14.mask, bf16[2048,1024]{1,0:T(8,128)(2,1)} %adj.1), custom_call_target="tpu_custom_call" | custom-call | flops 2097152 | bytes 8388608 | tf_op jit(solution)/shard_map/mask_tiles/pallas_call | solution.py:57
  15.5 0.6 collective-permute-start
  16.1 1.9 %collective-permute-done.3.value.refs_5_.refs_1_ = bf16[256,256]{1,0:T(8,128)(2,1)S(1)} collective-permute-done((bf16[256,256]{1,0:T(8,128)(2,1)S(1)}, bf16[256,256]{1,0:T(8,128)(2,1)S(1)}, u32[]{:S(2)}, u32[]{:S(2)}) %collective-permute-start.3) | collective-permute-done | bytes 131104 | tf_op jit(solution)/shard_map/ppermute | solution.py:206
  18.0 2.5 %collective-permute-start.18 = (bf16[256,256]{1,0:T(8,128)(2,1)S(1)}, bf16[256,256]{1,0:T(8,128)(2,1)S(1)}, u32[]{:S(2)}, u32[]{:S(2)}) collective-permute-start(bf16[256,256]{1,0:T(8,128)(2,1)S(1)} %after.9), channel_id=1, source_target_pairs={{0,6},{1,7},{2,4},{3,5},{4,2},{5,3},{6,0},{7,1},{8,14},{9,15},{10,... | collective-permute-start | bytes 393224 | tf_op jit(solution)/shard_map/ppermute | solution.py:206
  20.7 0.6 collective-permute-start.4
  21.5 0.5 collective-permute-done.2.refs_4_
  22.3 0.5 collective-permute-done.6.refs_8_
  22.7 1.3 %propagate.2 = bf16[1024,256]{1,0:T(8,128)(2,1)S(1)} custom-call(bf16[2048,1024]{1,0:T(8,128)(2,1)S(1)} %get-tuple-element.9.refs_0_, bf16[256,256]{1,0:T(8,128)(2,1)S(1)} %compare_select_fusion.value.refs_1_, bf16[256,256]{1,0:T(8,128)(2,1)S(1)} %collective-permute-done.refs_2_, bf16[256,256]{1,0:T(8,128)(2,1)S(1)} %collective-permute-done.1.value.refs_3_.refs_0_, ...), custom_call_target="tpu_custom_call" | custom-call | flops 1073741824 | bytes 4194304 | tf_op jit(solution)/shard_map/propagate/pallas_call | solution.py:97
  24.1 2.5 %collective-permute-start.9 = (bf16[256,256]{1,0:T(8,128)(2,1)S(1)}, bf16[256,256]{1,0:T(8,128)(2,1)S(1)}, u32[]{:S(2)}, u32[]{:S(2)}) collective-permute-start(bf16[256,256]{1,0:T(8,128)(2,1)S(1)} %get-tuple-element.19), channel_id=1, source_target_pairs={{0,24},{8,16},{16,8},{24,0},{1,25},{9,17},{17,9},{25,1},{2,26},{10... | collective-permute-start | bytes 393224 | tf_op jit(solution)/shard_map/ppermute | solution.py:209
  26.6 0.5 collective-permute-start.8
  27.1 0.5 collective-permute-start.7
  27.7 3.7 %collective-permute-done.16 = bf16[256,256]{1,0:T(8,128)(2,1)S(1)} collective-permute-done((bf16[256,256]{1,0:T(8,128)(2,1)S(1)}, bf16[256,256]{1,0:T(8,128)(2,1)S(1)}, u32[]{:S(2)}, u32[]{:S(2)}) %collective-permute-start.16) | collective-permute-done | bytes 131104 | tf_op jit(solution)/shard_map/ppermute | solution.py:206
  31.3 0.5 collective-permute-start.17
  31.9 1.5 %collective-permute-done.8.refs_2_ = bf16[256,256]{1,0:T(8,128)(2,1)S(1)} collective-permute-done((bf16[256,256]{1,0:T(8,128)(2,1)S(1)}, bf16[256,256]{1,0:T(8,128)(2,1)S(1)}, u32[]{:S(2)}, u32[]{:S(2)}) %collective-permute-start.8) | collective-permute-done | bytes 131104 | tf_op jit(solution)/shard_map/ppermute | solution.py:209
  33.5 0.2 first_layer_gradient.1
  33.8 1.7 %collective-permute-start.13 = (bf16[256,256]{1,0:T(8,128)(2,1)S(1)}, bf16[256,256]{1,0:T(8,128)(2,1)S(1)}, u32[]{:S(2)}, u32[]{:S(2)}) collective-permute-start(bf16[256,256]{1,0:T(8,128)(2,1)S(1)} %get-tuple-element.11.refs_1_), channel_id=1, source_target_pairs={{0,24},{8,16},{16,8},{24,0},{1,25},{9,17},{17,9},{25,1},{2,26},{10... | collective-permute-start | bytes 393224 | tf_op jit(solution)/shard_map/ppermute | solution.py:209
  35.5 1.3 %collective-permute-start.12 = (bf16[256,256]{1,0:T(8,128)(2,1)S(1)}, bf16[256,256]{1,0:T(8,128)(2,1)S(1)}, u32[]{:S(2)}, u32[]{:S(2)}) collective-permute-start(bf16[256,256]{1,0:T(8,128)(2,1)S(1)} %get-tuple-element.11.refs_1_), channel_id=1, source_target_pairs={{0,16},{8,24},{16,0},{24,8},{1,17},{9,25},{17,1},{25,9},{2,18},{10... | collective-permute-start | bytes 393224 | tf_op jit(solution)/shard_map/ppermute | solution.py:209
  36.8 0.5 collective-permute-start.11
  37.3 0.2 convolution_bitcast_fusion
  37.7 1.2 %collective-permute-done.25 = bf16[128,256]{1,0:T(8,128)(2,1)S(1)} collective-permute-done((bf16[128,256]{1,0:T(8,128)(2,1)S(1)}, bf16[128,256]{1,0:T(8,128)(2,1)S(1)}, u32[]{:S(2)}, u32[]{:S(2)}) %collective-permute-start.25) | collective-permute-done | bytes 65568 | tf_op jit(solution)/shard_map/ppermute | solution.py:206
  38.9 2.4 %collective-permute-start.26 = (bf16[128,256]{1,0:T(8,128)(2,1)S(1)}, bf16[128,256]{1,0:T(8,128)(2,1)S(1)}, u32[]{:S(2)}, u32[]{:S(2)}) collective-permute-start(bf16[128,256]{1,0:T(8,128)(2,1)S(1)} %add_convert_fusion.refs_0_), channel_id=1, source_target_pairs={{0,4},{1,5},{2,6},{3,7},{4,0},{5,1},{6,2},{7,3},{8,12},{9,13},{10,... | collective-permute-start | bytes 196616 | tf_op jit(solution)/shard_map/ppermute | solution.py:206
  41.3 1.6 %collective-permute-done.12.refs_3_ = bf16[256,256]{1,0:T(8,128)(2,1)S(1)} collective-permute-done((bf16[256,256]{1,0:T(8,128)(2,1)S(1)}, bf16[256,256]{1,0:T(8,128)(2,1)S(1)}, u32[]{:S(2)}, u32[]{:S(2)}) %collective-permute-start.12) | collective-permute-done | bytes 131104 | tf_op jit(solution)/shard_map/ppermute | solution.py:209
  42.9 1.4 %propagate.3 = bf16[2048,256]{1,0:T(8,128)(2,1)S(1)} custom-call(bf16[2048,1024]{1,0:T(8,128)(2,1)S(1)} %get-tuple-element.9.refs_0_, bf16[256,256]{1,0:T(8,128)(2,1)S(1)} %get-tuple-element.11.refs_1_, bf16[256,256]{1,0:T(8,128)(2,1)S(1)} %collective-permute-done.11.refs_2_, bf16[256,256]{1,0:T(8,128)(2,1)S(1)} %collective-permute-done.12.refs_3_, ...), custom_call_target="tpu_custom_call" | custom-call | flops 1073741824 | bytes 4194304 | tf_op jit(solution)/shard_map/propagate/pallas_call | solution.py:97
  44.4 0.5 fusion.3
  45.0 0.6 collective-permute-start.24
  45.6 1.4 %collective-permute-done.24 = bf16[128,256]{1,0:T(8,128)(2,1)S(1)} collective-permute-done((bf16[128,256]{1,0:T(8,128)(2,1)S(1)}, bf16[128,256]{1,0:T(8,128)(2,1)S(1)}, u32[]{:S(2)}, u32[]{:S(2)}) %collective-permute-start.24) | collective-permute-done | bytes 65568 | tf_op jit(solution)/shard_map/ppermute | solution.py:206
  47.0 1.5 %collective-permute-start.29 = (bf16[2,128,256]{2,1,0:T(8,128)(2,1)S(1)}, bf16[2,128,256]{2,1,0:T(8,128)(2,1)S(1)}, u32[]{:S(2)}, u32[]{:S(2)}) collective-permute-start(bf16[2,128,256]{2,1,0:T(8,128)(2,1)S(1)} %pad_maximum_fusion.1.refs_0_), channel_id=1, source_target_pairs={{0,24},{8,16},{16,8},{24,0},{1,25},{9,17},{17,9},{25,1},{2,26},{10... | collective-permute-start | bytes 393224 | tf_op jit(solution)/shard_map/ppermute | solution.py:209
  48.5 1.5 %collective-permute-start.28 = (bf16[2,128,256]{2,1,0:T(8,128)(2,1)S(1)}, bf16[2,128,256]{2,1,0:T(8,128)(2,1)S(1)}, u32[]{:S(2)}, u32[]{:S(2)}) collective-permute-start(bf16[2,128,256]{2,1,0:T(8,128)(2,1)S(1)} %pad_maximum_fusion.1.refs_0_), channel_id=1, source_target_pairs={{0,16},{8,24},{16,0},{24,8},{1,17},{9,25},{17,1},{25,9},{2,18},{10... | collective-permute-start | bytes 393224 | tf_op jit(solution)/shard_map/ppermute | solution.py:209
  50.0 0.6 collective-permute-start.27
  50.8 1.4 %collective-permute-start.23 = (bf16[256,256]{1,0:T(8,128)(2,1)S(1)}, bf16[256,256]{1,0:T(8,128)(2,1)S(1)}, u32[]{:S(2)}, u32[]{:S(2)}) collective-permute-start(bf16[256,256]{1,0:T(8,128)(2,1)S(1)} %get-tuple-element.15), channel_id=1, source_target_pairs={{0,6},{1,7},{2,4},{3,5},{4,2},{5,3},{6,0},{7,1},{8,14},{9,15},{10,... | collective-permute-start | bytes 393224 | tf_op jit(solution)/shard_map/ppermute | solution.py:206
  52.2 1.2 %collective-permute-start.22 = (bf16[256,256]{1,0:T(8,128)(2,1)S(1)}, bf16[256,256]{1,0:T(8,128)(2,1)S(1)}, u32[]{:S(2)}, u32[]{:S(2)}) collective-permute-start(bf16[256,256]{1,0:T(8,128)(2,1)S(1)} %get-tuple-element.16), channel_id=1, source_target_pairs={{0,4},{1,5},{2,6},{3,7},{4,0},{5,1},{6,2},{7,3},{8,12},{9,13},{10,... | collective-permute-start | bytes 393224 | tf_op jit(solution)/shard_map/ppermute | solution.py:206
  53.3 1.0 %collective-permute-done.29.refs_3_ = bf16[2,128,256]{2,1,0:T(8,128)(2,1)S(1)} collective-permute-done((bf16[2,128,256]{2,1,0:T(8,128)(2,1)S(1)}, bf16[2,128,256]{2,1,0:T(8,128)(2,1)S(1)}, u32[]{:S(2)}, u32[]{:S(2)}) %collective-permute-start.29) | collective-permute-done | bytes 131104 | tf_op jit(solution)/shard_map/ppermute | solution.py:209
  54.4 1.0 %collective-permute-start.21 = (bf16[256,256]{1,0:T(8,128)(2,1)S(1)}, bf16[256,256]{1,0:T(8,128)(2,1)S(1)}, u32[]{:S(2)}, u32[]{:S(2)}) collective-permute-start(bf16[256,256]{1,0:T(8,128)(2,1)S(1)} %get-tuple-element.17), channel_id=1, source_target_pairs={{0,2},{1,3},{2,0},{3,1},{4,6},{5,7},{6,4},{7,5},{8,10},{9,11},{10,... | collective-permute-start | bytes 393224 | tf_op jit(solution)/shard_map/ppermute | solution.py:206
  55.4 0.9 %collective-permute-done.28.refs_2_ = bf16[2,128,256]{2,1,0:T(8,128)(2,1)S(1)} collective-permute-done((bf16[2,128,256]{2,1,0:T(8,128)(2,1)S(1)}, bf16[2,128,256]{2,1,0:T(8,128)(2,1)S(1)}, u32[]{:S(2)}, u32[]{:S(2)}) %collective-permute-start.28) | collective-permute-done | bytes 131104 | tf_op jit(solution)/shard_map/ppermute | solution.py:209
  56.4 1.1 %collective-permute-start.30 = (bf16[2,128,256]{2,1,0:T(8,128)(2,1)S(1)}, bf16[2,128,256]{2,1,0:T(8,128)(2,1)S(1)}, u32[]{:S(2)}, u32[]{:S(2)}) collective-permute-start(bf16[2,128,256]{2,1,0:T(8,128)(2,1)S(1)} %joined.7.refs_0_), channel_id=1, source_target_pairs={{0,2},{1,3},{2,0},{3,1},{4,6},{5,7},{6,4},{7,5},{8,10},{9,11},{10,... | collective-permute-start | bytes 393224 | tf_op jit(solution)/shard_map/ppermute | solution.py:206
  57.6 1.5 %collective-permute-done.23.refs_3_ = bf16[256,256]{1,0:T(8,128)(2,1)S(1)} collective-permute-done((bf16[256,256]{1,0:T(8,128)(2,1)S(1)}, bf16[256,256]{1,0:T(8,128)(2,1)S(1)}, u32[]{:S(2)}, u32[]{:S(2)}) %collective-permute-start.23) | collective-permute-done | bytes 131104 | tf_op jit(solution)/shard_map/ppermute | solution.py:206
  59.1 5.4 %collective-permute-done.22.refs_2_ = bf16[256,256]{1,0:T(8,128)(2,1)S(1)} collective-permute-done((bf16[256,256]{1,0:T(8,128)(2,1)S(1)}, bf16[256,256]{1,0:T(8,128)(2,1)S(1)}, u32[]{:S(2)}, u32[]{:S(2)}) %collective-permute-start.22) | collective-permute-done | bytes 131104 | tf_op jit(solution)/shard_map/ppermute | solution.py:206
  64.6 1.3 %collective-permute-done.30.refs_1_ = bf16[2,128,256]{2,1,0:T(8,128)(2,1)S(1)} collective-permute-done((bf16[2,128,256]{2,1,0:T(8,128)(2,1)S(1)}, bf16[2,128,256]{2,1,0:T(8,128)(2,1)S(1)}, u32[]{:S(2)}, u32[]{:S(2)}) %collective-permute-start.30) | collective-permute-done | bytes 131104 | tf_op jit(solution)/shard_map/ppermute | solution.py:206
  65.9 0.6 collective-permute-start.31
  66.5 4.6 %collective-permute-done.31.refs_1_ = bf16[128,256]{1,0:T(8,128)(2,1)S(1)} collective-permute-done((bf16[128,256]{1,0:T(8,128)(2,1)S(1)}, bf16[128,256]{1,0:T(8,128)(2,1)S(1)}, u32[]{:S(2)}, u32[]{:S(2)}) %collective-permute-start.31) | collective-permute-done | bytes 65568 | tf_op jit(solution)/shard_map/ppermute | solution.py:206
  71.3 0.9 %node_gradient.1 = bf16[256,256]{1,0:T(8,128)(2,1)} custom-call(bf16[256,256]{1,0:T(8,128)(2,1)S(1)} %joined.5.total.refs_2_, bf16[256,256]{1,0:T(8,128)(2,1)S(1)} %copy-done.4), custom_call_target="tpu_custom_call" | custom-call | tf_op jit(solution)/shard_map/node_gradient/pallas_call | solution.py:138
  72.2 0.6 collective-permute-done.32.other
  72.8 0.8 %weight_gradients.1 = (f32[256,256]{1,0:T(8,128)}, f32[256,256]{1,0:T(8,128)}) custom-call(s32[1]{0:T(128)} %bitcast.15.odd, f32[2,128,256]{2,1,0:T(8,128)S(1)} %pad_maximum_fusion.mine, f32[2,128,256]{2,1,0:T(8,128)S(1)} %collective-permute-done.32.other), custom_call_target="tpu_custom_call" | custom-call | tf_op jit(solution)/shard_map/weight_gradients/pallas_call | solution.py:188
  (69 shorter events, 1.7 us)
Async XLA Ops:
  0.6 36.7 %copy-start = (bf16[256,256]{1,0:T(8,128)(2,1)S(1)}, bf16[256,256]{1,0:T(8,128)(2,1)}, u32[]{:S(2)}) copy-start(bf16[256,256]{1,0:T(8,128)(2,1)} %param.13) | copy-start | bytes 393220
  0.6 14.8 %copy-start.1 = (bf16[256,256]{1,0:T(8,128)(2,1)S(1)}, bf16[256,256]{1,0:T(8,128)(2,1)}, u32[]{:S(2)}) copy-start(bf16[256,256]{1,0:T(8,128)(2,1)} %value.1) | copy-start | bytes 393220
  1.7 13.8 %collective-permute-start.5 = (bf16[256,256]{1,0:T(8,128)(2,1)S(1)}, bf16[256,256]{1,0:T(8,128)(2,1)S(1)}, u32[]{:S(2)}, u32[]{:S(2)}) collective-permute-start(bf16[256,256]{1,0:T(8,128)(2,1)S(1)} %compare_select_fusion.value.refs_1_), channel_id=1, source_target_pairs={{0,6},{1,7},{2,4},{3,5},{4,2},{5,3},{6,0},{7,1},{8,14},{9,15},{10,... | collective-permute-start | bytes 393224 | tf_op jit(solution)/shard_map/ppermute | solution.py:206
  6.8 11.2 %collective-permute-start.3 = (bf16[256,256]{1,0:T(8,128)(2,1)S(1)}, bf16[256,256]{1,0:T(8,128)(2,1)S(1)}, u32[]{:S(2)}, u32[]{:S(2)}) collective-permute-start(bf16[256,256]{1,0:T(8,128)(2,1)S(1)} %compare_select_fusion.value.refs_1_), channel_id=1, source_target_pairs={{0,4},{1,5},{2,6},{3,7},{4,0},{5,1},{6,2},{7,3},{8,12},{9,13},{10,... | collective-permute-start | bytes 393224 | tf_op jit(solution)/shard_map/ppermute | solution.py:206
  6.8 11.2 %collective-permute-start.1 = (bf16[256,256]{1,0:T(8,128)(2,1)S(1)}, bf16[256,256]{1,0:T(8,128)(2,1)S(1)}, u32[]{:S(2)}, u32[]{:S(2)}) collective-permute-start(bf16[256,256]{1,0:T(8,128)(2,1)S(1)} %compare_select_fusion.value.refs_1_), channel_id=1, source_target_pairs={{0,2},{1,3},{2,0},{3,1},{4,6},{5,7},{6,4},{7,5},{8,10},{9,11},{10,... | collective-permute-start | bytes 393224 | tf_op jit(solution)/shard_map/ppermute | solution.py:206
  7.5 13.8 %collective-permute-start.10 = (bf16[256,256]{1,0:T(8,128)(2,1)}, bf16[256,256]{1,0:T(8,128)(2,1)S(1)}, u32[]{:S(2)}, u32[]{:S(2)}) collective-permute-start(bf16[256,256]{1,0:T(8,128)(2,1)} %value.1), channel_id=1, source_target_pairs={{0,2},{1,3},{2,0},{3,1},{4,6},{5,7},{6,4},{7,5},{8,10},{9,11},{10,... | collective-permute-start | bytes 393224 | tf_op jit(solution)/shard_map/ppermute | solution.py:206
  8.8 11.9 %collective-permute-start.14 = (bf16[256,256]{1,0:T(8,128)(2,1)}, bf16[256,256]{1,0:T(8,128)(2,1)S(1)}, u32[]{:S(2)}, u32[]{:S(2)}) collective-permute-start(bf16[256,256]{1,0:T(8,128)(2,1)} %value.1), channel_id=1, source_target_pairs={{0,1},{1,0},{2,3},{3,2},{4,5},{5,4},{6,7},{7,6},{8,9},{9,8},{10,11... | collective-permute-start | bytes 393224 | tf_op jit(solution)/shard_map/ppermute | solution.py:206
  15.5 5.9 %collective-permute-start = (bf16[256,256]{1,0:T(8,128)(2,1)S(1)}, bf16[256,256]{1,0:T(8,128)(2,1)S(1)}, u32[]{:S(2)}, u32[]{:S(2)}) collective-permute-start(bf16[256,256]{1,0:T(8,128)(2,1)S(1)} %after.5), channel_id=1, source_target_pairs={{0,1},{1,0},{2,3},{3,2},{4,5},{5,4},{6,7},{7,6},{8,9},{9,8},{10,11... | collective-permute-start | bytes 393224 | tf_op jit(solution)/shard_map/ppermute | solution.py:206
  18.0 9.1 %collective-permute-start.18 = (bf16[256,256]{1,0:T(8,128)(2,1)S(1)}, bf16[256,256]{1,0:T(8,128)(2,1)S(1)}, u32[]{:S(2)}, u32[]{:S(2)}) collective-permute-start(bf16[256,256]{1,0:T(8,128)(2,1)S(1)} %after.9), channel_id=1, source_target_pairs={{0,6},{1,7},{2,4},{3,5},{4,2},{5,3},{6,0},{7,1},{8,14},{9,15},{10,... | collective-permute-start | bytes 393224 | tf_op jit(solution)/shard_map/ppermute | solution.py:206
  20.6 13.0 %copy-start.2 = (bf16[256,256]{1,0:T(8,128)(2,1)S(1)}, bf16[256,256]{1,0:T(8,128)(2,1)}, u32[]{:S(2)}) copy-start(bf16[256,256]{1,0:T(8,128)(2,1)} %refs_4_.1) | copy-start | bytes 393220
  20.6 12.9 %copy-start.3 = (bf16[256,256]{1,0:T(8,128)(2,1)S(1)}, bf16[256,256]{1,0:T(8,128)(2,1)}, u32[]{:S(2)}) copy-start(bf16[256,256]{1,0:T(8,128)(2,1)} %refs_5_.1) | copy-start | bytes 393220
  20.6 1.4 %collective-permute-start.2 = (bf16[256,256]{1,0:T(8,128)(2,1)S(1)}, bf16[256,256]{1,0:T(8,128)(2,1)S(1)}, u32[]{:S(2)}, u32[]{:S(2)}) collective-permute-start(bf16[256,256]{1,0:T(8,128)(2,1)S(1)} %after.6), channel_id=1, source_target_pairs={{0,1},{1,0},{2,3},{3,2},{4,5},{5,4},{6,7},{7,6},{8,9},{9,8},{10,11... | collective-permute-start | bytes 393224 | tf_op jit(solution)/shard_map/ppermute | solution.py:206
  20.7 1.5 %collective-permute-start.4 = (bf16[256,256]{1,0:T(8,128)(2,1)S(1)}, bf16[256,256]{1,0:T(8,128)(2,1)S(1)}, u32[]{:S(2)}, u32[]{:S(2)}) collective-permute-start(bf16[256,256]{1,0:T(8,128)(2,1)S(1)} %after.7), channel_id=1, source_target_pairs={{0,1},{1,0},{2,3},{3,2},{4,5},{5,4},{6,7},{7,6},{8,9},{9,8},{10,11... | collective-permute-start | bytes 393224 | tf_op jit(solution)/shard_map/ppermute | solution.py:206
  21.3 1.4 %collective-permute-start.6 = (bf16[256,256]{1,0:T(8,128)(2,1)S(1)}, bf16[256,256]{1,0:T(8,128)(2,1)S(1)}, u32[]{:S(2)}, u32[]{:S(2)}) collective-permute-start(bf16[256,256]{1,0:T(8,128)(2,1)S(1)} %after.8), channel_id=1, source_target_pairs={{0,1},{1,0},{2,3},{3,2},{4,5},{5,4},{6,7},{7,6},{8,9},{9,8},{10,11... | collective-permute-start | bytes 393224 | tf_op jit(solution)/shard_map/ppermute | solution.py:206
  21.4 9.9 %collective-permute-start.16 = (bf16[256,256]{1,0:T(8,128)(2,1)S(1)}, bf16[256,256]{1,0:T(8,128)(2,1)S(1)}, u32[]{:S(2)}, u32[]{:S(2)}) collective-permute-start(bf16[256,256]{1,0:T(8,128)(2,1)S(1)} %after.9), channel_id=1, source_target_pairs={{0,4},{1,5},{2,6},{3,7},{4,0},{5,1},{6,2},{7,3},{8,12},{9,13},{10,... | collective-permute-start | bytes 393224 | tf_op jit(solution)/shard_map/ppermute | solution.py:206
  22.0 9.3 %collective-permute-start.15 = (bf16[256,256]{1,0:T(8,128)(2,1)S(1)}, bf16[256,256]{1,0:T(8,128)(2,1)S(1)}, u32[]{:S(2)}, u32[]{:S(2)}) collective-permute-start(bf16[256,256]{1,0:T(8,128)(2,1)S(1)} %collective-permute-done.10.refs_6_), channel_id=1, source_target_pairs={{0,1},{1,0},{2,3},{3,2},{4,5},{5,4},{6,7},{7,6},{8,9},{9,8},{10,11... | collective-permute-start | bytes 393224 | tf_op jit(solution)/shard_map/ppermute | solution.py:206
  24.1 7.8 %collective-permute-start.9 = (bf16[256,256]{1,0:T(8,128)(2,1)S(1)}, bf16[256,256]{1,0:T(8,128)(2,1)S(1)}, u32[]{:S(2)}, u32[]{:S(2)}) collective-permute-start(bf16[256,256]{1,0:T(8,128)(2,1)S(1)} %get-tuple-element.19), channel_id=1, source_target_pairs={{0,24},{8,16},{16,8},{24,0},{1,25},{9,17},{17,9},{25,1},{2,26},{10... | collective-permute-start | bytes 393224 | tf_op jit(solution)/shard_map/ppermute | solution.py:209
  26.6 6.8 %collective-permute-start.8 = (bf16[256,256]{1,0:T(8,128)(2,1)S(1)}, bf16[256,256]{1,0:T(8,128)(2,1)S(1)}, u32[]{:S(2)}, u32[]{:S(2)}) collective-permute-start(bf16[256,256]{1,0:T(8,128)(2,1)S(1)} %get-tuple-element.20), channel_id=1, source_target_pairs={{0,16},{8,24},{16,0},{24,8},{1,17},{9,25},{17,1},{25,9},{2,18},{10... | collective-permute-start | bytes 393224 | tf_op jit(solution)/shard_map/ppermute | solution.py:209
  27.1 6.4 %collective-permute-start.7 = (bf16[256,256]{1,0:T(8,128)(2,1)S(1)}, bf16[256,256]{1,0:T(8,128)(2,1)S(1)}, u32[]{:S(2)}, u32[]{:S(2)}) collective-permute-start(bf16[256,256]{1,0:T(8,128)(2,1)S(1)} %get-tuple-element.21), channel_id=1, source_target_pairs={{0,8},{8,0},{16,24},{24,16},{1,9},{9,1},{17,25},{25,17},{2,10},{10... | collective-permute-start | bytes 393224 | tf_op jit(solution)/shard_map/ppermute | solution.py:209
  31.3 6.4 %collective-permute-start.19 = (bf16[256,256]{1,0:T(8,128)(2,1)S(1)}, bf16[256,256]{1,0:T(8,128)(2,1)S(1)}, u32[]{:S(2)}, u32[]{:S(2)}) collective-permute-start(bf16[256,256]{1,0:T(8,128)(2,1)S(1)} %collective-permute-done.18), channel_id=1, source_target_pairs={{0,1},{1,0},{2,3},{3,2},{4,5},{5,4},{6,7},{7,6},{8,9},{9,8},{10,11... | collective-permute-start | bytes 393224 | tf_op jit(solution)/shard_map/ppermute | solution.py:206
  31.3 6.2 %collective-permute-start.17 = (bf16[256,256]{1,0:T(8,128)(2,1)S(1)}, bf16[256,256]{1,0:T(8,128)(2,1)S(1)}, u32[]{:S(2)}, u32[]{:S(2)}) collective-permute-start(bf16[256,256]{1,0:T(8,128)(2,1)S(1)} %collective-permute-done.16), channel_id=1, source_target_pairs={{0,1},{1,0},{2,3},{3,2},{4,5},{5,4},{6,7},{7,6},{8,9},{9,8},{10,11... | collective-permute-start | bytes 393224 | tf_op jit(solution)/shard_map/ppermute | solution.py:206
  33.8 7.5 %collective-permute-start.13 = (bf16[256,256]{1,0:T(8,128)(2,1)S(1)}, bf16[256,256]{1,0:T(8,128)(2,1)S(1)}, u32[]{:S(2)}, u32[]{:S(2)}) collective-permute-start(bf16[256,256]{1,0:T(8,128)(2,1)S(1)} %get-tuple-element.11.refs_1_), channel_id=1, source_target_pairs={{0,24},{8,16},{16,8},{24,0},{1,25},{9,17},{17,9},{25,1},{2,26},{10... | collective-permute-start | bytes 393224 | tf_op jit(solution)/shard_map/ppermute | solution.py:209
  35.5 7.4 %collective-permute-start.12 = (bf16[256,256]{1,0:T(8,128)(2,1)S(1)}, bf16[256,256]{1,0:T(8,128)(2,1)S(1)}, u32[]{:S(2)}, u32[]{:S(2)}) collective-permute-start(bf16[256,256]{1,0:T(8,128)(2,1)S(1)} %get-tuple-element.11.refs_1_), channel_id=1, source_target_pairs={{0,16},{8,24},{16,0},{24,8},{1,17},{9,25},{17,1},{25,9},{2,18},{10... | collective-permute-start | bytes 393224 | tf_op jit(solution)/shard_map/ppermute | solution.py:209
  36.8 6.2 %collective-permute-start.11 = (bf16[256,256]{1,0:T(8,128)(2,1)S(1)}, bf16[256,256]{1,0:T(8,128)(2,1)S(1)}, u32[]{:S(2)}, u32[]{:S(2)}) collective-permute-start(bf16[256,256]{1,0:T(8,128)(2,1)S(1)} %get-tuple-element.11.refs_1_), channel_id=1, source_target_pairs={{0,8},{8,0},{16,24},{24,16},{1,9},{9,1},{17,25},{25,17},{2,10},{10... | collective-permute-start | bytes 393224 | tf_op jit(solution)/shard_map/ppermute | solution.py:209
  37.6 1.3 %collective-permute-start.25 = (bf16[128,256]{1,0:T(8,128)(2,1)S(1)}, bf16[128,256]{1,0:T(8,128)(2,1)S(1)}, u32[]{:S(2)}, u32[]{:S(2)}) collective-permute-start(bf16[128,256]{1,0:T(8,128)(2,1)S(1)} %select_convert_fusion), channel_id=1, source_target_pairs={{0,1},{1,0},{2,3},{3,2},{4,5},{5,4},{6,7},{7,6},{8,9},{9,8},{10,11... | collective-permute-start | bytes 196616 | tf_op jit(solution)/shard_map/ppermute | solution.py:206
  38.9 6.7 %collective-permute-start.26 = (bf16[128,256]{1,0:T(8,128)(2,1)S(1)}, bf16[128,256]{1,0:T(8,128)(2,1)S(1)}, u32[]{:S(2)}, u32[]{:S(2)}) collective-permute-start(bf16[128,256]{1,0:T(8,128)(2,1)S(1)} %add_convert_fusion.refs_0_), channel_id=1, source_target_pairs={{0,4},{1,5},{2,6},{3,7},{4,0},{5,1},{6,2},{7,3},{8,12},{9,13},{10,... | collective-permute-start | bytes 196616 | tf_op jit(solution)/shard_map/ppermute | solution.py:206
  44.9 26.4 %copy-start.4 = (bf16[256,256]{1,0:T(8,128)(2,1)S(1)}, bf16[256,256]{1,0:T(8,128)(2,1)}, u32[]{:S(2)}) copy-start(bf16[256,256]{1,0:T(8,128)(2,1)} %w_one.1) | copy-start | bytes 393220
  44.9 5.7 %collective-permute-start.20 = (bf16[4,256,256]{2,1,0:T(8,128)(2,1)S(1)}, bf16[4,256,256]{2,1,0:T(8,128)(2,1)S(1)}, u32[]{:S(2)}, u32[]{:S(2)}) collective-permute-start(bf16[4,256,256]{2,1,0:T(8,128)(2,1)S(1)} %slice_bitcast_fusion), channel_id=1, source_target_pairs={{0,1},{1,0},{2,3},{3,2},{4,5},{5,4},{6,7},{7,6},{8,9},{9,8},{10,11... | collective-permute-start | bytes 1572872 | tf_op jit(solution)/shard_map/ppermute | solution.py:206
  45.0 2.0 %collective-permute-start.24 = (bf16[128,256]{1,0:T(8,128)(2,1)S(1)}, bf16[128,256]{1,0:T(8,128)(2,1)S(1)}, u32[]{:S(2)}, u32[]{:S(2)}) collective-permute-start(bf16[128,256]{1,0:T(8,128)(2,1)S(1)} %select_convert_fusion.1), channel_id=1, source_target_pairs={{0,1},{1,0},{2,3},{3,2},{4,5},{5,4},{6,7},{7,6},{8,9},{9,8},{10,11... | collective-permute-start | bytes 196616 | tf_op jit(solution)/shard_map/ppermute | solution.py:206
  47.0 7.3 %collective-permute-start.29 = (bf16[2,128,256]{2,1,0:T(8,128)(2,1)S(1)}, bf16[2,128,256]{2,1,0:T(8,128)(2,1)S(1)}, u32[]{:S(2)}, u32[]{:S(2)}) collective-permute-start(bf16[2,128,256]{2,1,0:T(8,128)(2,1)S(1)} %pad_maximum_fusion.1.refs_0_), channel_id=1, source_target_pairs={{0,24},{8,16},{16,8},{24,0},{1,25},{9,17},{17,9},{25,1},{2,26},{10... | collective-permute-start | bytes 393224 | tf_op jit(solution)/shard_map/ppermute | solution.py:209
  48.5 7.8 %collective-permute-start.28 = (bf16[2,128,256]{2,1,0:T(8,128)(2,1)S(1)}, bf16[2,128,256]{2,1,0:T(8,128)(2,1)S(1)}, u32[]{:S(2)}, u32[]{:S(2)}) collective-permute-start(bf16[2,128,256]{2,1,0:T(8,128)(2,1)S(1)} %pad_maximum_fusion.1.refs_0_), channel_id=1, source_target_pairs={{0,16},{8,24},{16,0},{24,8},{1,17},{9,25},{17,1},{25,9},{2,18},{10... | collective-permute-start | bytes 393224 | tf_op jit(solution)/shard_map/ppermute | solution.py:209
  50.0 6.4 %collective-permute-start.27 = (bf16[2,128,256]{2,1,0:T(8,128)(2,1)S(1)}, bf16[2,128,256]{2,1,0:T(8,128)(2,1)S(1)}, u32[]{:S(2)}, u32[]{:S(2)}) collective-permute-start(bf16[2,128,256]{2,1,0:T(8,128)(2,1)S(1)} %pad_maximum_fusion.1.refs_0_), channel_id=1, source_target_pairs={{0,8},{8,0},{16,24},{24,16},{1,9},{9,1},{17,25},{25,17},{2,10},{10... | collective-permute-start | bytes 393224 | tf_op jit(solution)/shard_map/ppermute | solution.py:209
  50.8 8.3 %collective-permute-start.23 = (bf16[256,256]{1,0:T(8,128)(2,1)S(1)}, bf16[256,256]{1,0:T(8,128)(2,1)S(1)}, u32[]{:S(2)}, u32[]{:S(2)}) collective-permute-start(bf16[256,256]{1,0:T(8,128)(2,1)S(1)} %get-tuple-element.15), channel_id=1, source_target_pairs={{0,6},{1,7},{2,4},{3,5},{4,2},{5,3},{6,0},{7,1},{8,14},{9,15},{10,... | collective-permute-start | bytes 393224 | tf_op jit(solution)/shard_map/ppermute | solution.py:206
  52.2 12.3 %collective-permute-start.22 = (bf16[256,256]{1,0:T(8,128)(2,1)S(1)}, bf16[256,256]{1,0:T(8,128)(2,1)S(1)}, u32[]{:S(2)}, u32[]{:S(2)}) collective-permute-start(bf16[256,256]{1,0:T(8,128)(2,1)S(1)} %get-tuple-element.16), channel_id=1, source_target_pairs={{0,4},{1,5},{2,6},{3,7},{4,0},{5,1},{6,2},{7,3},{8,12},{9,13},{10,... | collective-permute-start | bytes 393224 | tf_op jit(solution)/shard_map/ppermute | solution.py:206
  54.4 10.1 %collective-permute-start.21 = (bf16[256,256]{1,0:T(8,128)(2,1)S(1)}, bf16[256,256]{1,0:T(8,128)(2,1)S(1)}, u32[]{:S(2)}, u32[]{:S(2)}) collective-permute-start(bf16[256,256]{1,0:T(8,128)(2,1)S(1)} %get-tuple-element.17), channel_id=1, source_target_pairs={{0,2},{1,3},{2,0},{3,1},{4,6},{5,7},{6,4},{7,5},{8,10},{9,11},{10,... | collective-permute-start | bytes 393224 | tf_op jit(solution)/shard_map/ppermute | solution.py:206
  56.4 9.4 %collective-permute-start.30 = (bf16[2,128,256]{2,1,0:T(8,128)(2,1)S(1)}, bf16[2,128,256]{2,1,0:T(8,128)(2,1)S(1)}, u32[]{:S(2)}, u32[]{:S(2)}) collective-permute-start(bf16[2,128,256]{2,1,0:T(8,128)(2,1)S(1)} %joined.7.refs_0_), channel_id=1, source_target_pairs={{0,2},{1,3},{2,0},{3,1},{4,6},{5,7},{6,4},{7,5},{8,10},{9,11},{10,... | collective-permute-start | bytes 393224 | tf_op jit(solution)/shard_map/ppermute | solution.py:206
  65.9 5.2 %collective-permute-start.31 = (bf16[128,256]{1,0:T(8,128)(2,1)S(1)}, bf16[128,256]{1,0:T(8,128)(2,1)S(1)}, u32[]{:S(2)}, u32[]{:S(2)}) collective-permute-start(bf16[128,256]{1,0:T(8,128)(2,1)S(1)} %get-tuple-element.23.refs_0_), channel_id=1, source_target_pairs={{0,4},{1,5},{2,6},{3,7},{4,0},{5,1},{6,2},{7,3},{8,12},{9,13},{10,... | collective-permute-start | bytes 196616 | tf_op jit(solution)/shard_map/ppermute | solution.py:206
  71.2 1.6 %collective-permute-start.32 = (f32[2,128,256]{2,1,0:T(8,128)S(1)}, f32[2,128,256]{2,1,0:T(8,128)S(1)}, u32[]{:S(2)}, u32[]{:S(2)}) collective-permute-start(f32[2,128,256]{2,1,0:T(8,128)S(1)} %pad_maximum_fusion.mine), channel_id=1, source_target_pairs={{0,1},{1,0},{2,3},{3,2},{4,5},{5,4},{6,7},{7,6},{8,9},{9,8},{10,11... | collective-permute-start | bytes 786440 | tf_op jit(solution)/shard_map/ppermute | solution.py:206

commit v4 on v3

--- a/solution.py
+++ b/solution.py
@@ -67,7 +67,6 @@
         ),
         out_shape=[VMEM((rows, cols), BF16), VMEM((16, 128), BF16)],
         compiler_params=params(),
-        cost_estimate=cost(rows * cols, 4 * rows * cols),
         name="mask_tiles",
     )(row_src, col_src, tile_mask, adjacency)
 
@@ -101,31 +100,48 @@
         out_shape=jax.ShapeDtypeStruct((out_rows, width), BF16),
         scratch_shapes=[VMEM((depth, width), BF16)],
         compiler_params=params(),
-        cost_estimate=cost(2 * rows * cols * width, 2 * rows * cols),
+        cost_estimate=(cost(2 * rows * cols * width, 2 * rows * cols)) if turned else (cost(24_000_000_000, 1_000_000)),
         name="propagate",
     )(graph, *parts, *events)
     return out.reshape(out_rows // block, block, width)
 
 
-def middle_kernel(count, *refs):
-    parts, w_two, pre_one = refs[:count], refs[count], refs[count + 1]
-    prop, grad = refs[-2:]
+def put_halves(term, odd, both, mine, yours):
+    half = mine.shape[0]
+    both[...] = term
+    mine[...] = both[pl.ds(pl.multiple_of(odd * half, half), half)]
+    yours[...] = both[pl.ds(pl.multiple_of((1 - odd) * half, half), half)].astype(BF16)
+
+
+def half_shapes(width, columns):
+    return [
+        jax.ShapeDtypeStruct((width // 2, columns), F32),
+        jax.ShapeDtypeStruct((width // 2, columns), BF16),
+    ]
+
+
+def middle_kernel(count, odd, *refs):
+    parts = refs[:count]
+    w_two, pre_one, hidden = refs[count : count + 3]
+    grad, mine, yours, both = refs[-4:]
     total = tree([part[...].astype(F32) for part in parts]).astype(BF16)
-    prop[...] = total
     back = lax.dot_general(total, w_two[...], LAST_LAST, preferred_element_type=F32)
     grad[...] = jnp.where(pre_one[...] > 0, back, 0.0).astype(BF16)
-
-
-def middle(parts, w_two, pre_one, *events):
-    shape = jax.ShapeDtypeStruct(pre_one.shape, BF16)
+    term = lax.dot_general(hidden[...], total, ROWS_COLS, preferred_element_type=F32)
+    put_halves(term, odd[0], both, mine, yours)
+
+
+def middle(odd, parts, w_two, pre_one, hidden, *events):
+    width = hidden.shape[1]
     return pl.pallas_call(
         functools.partial(middle_kernel, len(parts)),
-        in_specs=whole(len(parts) + 2) + unread(events),
-        out_specs=whole(2),
-        out_shape=[shape, shape],
+        in_specs=[pl.BlockSpec(memory_space=pltpu.SMEM)] + whole(len(parts) + 3) + unread(events),
+        out_specs=whole(3),
+        out_shape=[jax.ShapeDtypeStruct(pre_one.shape, BF16)] + half_shapes(width, width),
+        scratch_shapes=[VMEM((width, width), F32)],
         compiler_params=params(),
         name="first_layer_gradient",
-    )(*parts, w_two, pre_one, *events)
+    )(odd, *parts, w_two, pre_one, hidden, *events)
 
 
 def last_kernel(total, w_one, out):
@@ -199,8 +215,9 @@
     block = out_grad.shape[0]
     scale = 4.0 * block ** (-0.5)
     n_far = n_col // 2
+    high = n_col.bit_length() - 2
     row, col = lax.axis_index("row"), lax.axis_index("col")
-    odd = col % 2 == 1
+    odd = jnp.bitwise_and(col, 1).reshape(1)
 
     def over_col(value, flip):
         return lax.ppermute(value, "col", [(i, i ^ flip) for i in range(n_col)])
@@ -208,66 +225,69 @@
     def over_row(value, flip):
         return lax.ppermute(value, "row", [(i, i ^ flip) for i in range(n_row)])
 
-    def far(values):
-        got = {j: over_col(values[j], 2 * j) for j in reversed(range(1, n_far))}
+    def far(values, back):
+        order = range(1, n_far)
+        got = {j: over_col(values[j], 2 * j) for j in (reversed(order) if back else order)}
         return [values[0]] + [got[j] for j in range(1, n_far)]
 
-    def rows_all(values):
-        got = {i: over_row(values[i], i) for i in reversed(range(1, n_row))}
+    def rows_all(values, back):
+        order = range(1, n_row)
+        got = {i: over_row(values[i], i) for i in (reversed(order) if back else order)}
         return [values[0]] + [got[i] for i in range(1, n_row)]
 
-    def halved(term):
-        half = term.shape[0] // 2
-        mine = jnp.where(odd, term[half:], term[:half])
-        yours = jnp.where(odd, term[:half], term[half:]).astype(BF16)
-        return (mine + over_col(yours, 1).astype(F32)).astype(BF16)
-
-    def sum_far(value):
-        return tree([v.astype(F32) for v in far([value] * n_far)]).astype(BF16)
+    def halved(mine, yours):
+        return joined([mine, over_col(yours, 1)])
 
     row_src = jnp.bitwise_xor(jnp.arange(n_col, dtype=jnp.int32), col)
     col_src = jnp.bitwise_xor(jnp.arange(n_row, dtype=jnp.int32), row)
-
     grad_two = jnp.where(pre_two > 0, out_grad, jnp.zeros_like(out_grad))
-    near = far([grad_two] * n_far)
+    near = far([grad_two] * n_far, 1)
     near_features = [features, over_col(features, 2)]
     plain, made = masked(adjacency, tile_mask, row_src, col_src, block)
     others = [over_col(after(value, made), 1) for value in near]
     column_part = spread(plain, [value for pair in zip(near, others) for value in pair], True)
-    parts = rows_all(column_part)
-    late_features = after(features, *near[1:])
-    near_features += [over_col(late_features, 2 * j) for j in range(2, n_far)]
-    prop_two, grad_one = middle(parts, w_two, pre_one, near_features[1])
-    first = rows_all([grad_one] * n_row)
+    parts = rows_all(column_part, 1)
+    late_features = after(features, column_part)
+    late = {j: over_col(late_features, 2 * j) for j in range(2, n_far)}
+    near_features += [late[j] for j in range(2, n_far)]
+    grad_one, *halves_two = middle(odd, parts, w_two, pre_one, hidden)
+    first = rows_all([grad_one] * n_row, 1)
     other_features = [over_col(value, 1) for value in near_features]
-    row_features = jnp.stack([value for pair in zip(near_features, other_features) for value in pair])
-
-    row_part = spread(plain, first, False, row_features)
-    row_part = row_part.reshape(n_far, 2, block, -1)
-    crossed = over_col(row_part[:, 1], 1)
-    chip_part = row_part[:, 0].astype(F32) + crossed.astype(F32)
-    chip_part = chip_part.astype(BF16)
-    ends = far(chip_part)
-    prop_one = joined(ends)
-    node_grad = last(prop_one, w_one)
-
-    term_two = lax.dot_general(hidden, prop_two, ROWS_COLS, preferred_element_type=F32)
-    term_one = lax.dot_general(
+    all_features = [value for pair in zip(near_features, other_features) for value in pair]
+    two = halved(*halves_two)
+    two = joined(far([two] * n_far, 1))
+    row_features = jnp.stack(all_features)
+    row_part = spread(plain, first, False, row_features).reshape(n_far, 2, block, -1)
+    term = lax.dot_general(
         row_features.reshape(n_col * block, -1),
         row_part.reshape(n_col * block, -1),
         ROWS_COLS,
         preferred_element_type=F32,
     )
-    low, high = range(1, n_col.bit_length() - 2), n_col.bit_length() - 2
-    ahead = halved(term_two)
-    ahead = joined([ahead, over_col(ahead, 1 << high)])
-    total = joined(rows_all([jnp.stack([halved(term_one), ahead])] * n_row))
-    for bit in low:
-        total = joined([total, over_col(total, 1 << bit)], prop_one)
-    one = joined([total[0], over_col(total[0], 1 << high)], dtype=F32)
-    total = jnp.stack([one, total[1].astype(F32)])
-    odd = jnp.bitwise_and(col, 1).reshape(1)
-    return node_grad, *scaled(odd, total, over_col(total, 1), scale)
+    half = term.shape[0] // 2
+    is_odd = odd[0] == 1
+    halves_one = (
+        jnp.where(is_odd, term[half:], term[:half]),
+        jnp.where(is_odd, term[:half], term[half:]).astype(BF16),
+    )
+    crossed = over_col(row_part[:, 1], 1)
+    held = (row_part[:, 0].astype(F32) + crossed.astype(F32)).astype(BF16)
+    one = halved(*halves_one)
+    steps = []
+    for bit in range(1, high + 1):
+        pairs = held.reshape((-1, 2) + held.shape[1:])
+        held = joined([pairs[:, 0], over_col(pairs[:, 1], 1 << bit)])
+        steps.append(held)
+    prop_one, step_one = held[0], steps[0]
+    total = joined(rows_all([jnp.stack([one, two])] * n_row, 1), step_one)
+    one, two = total[0], total[1].astype(F32)
+    for bit in range(1, high):
+        one = joined([one, over_col(one, 1 << bit)])
+    one = joined([one, over_col(one, 1 << high)], prop_one, dtype=F32)
+    node_grad = last(prop_one, w_one)
+    one, = scaled(odd, one[None], over_col(one, 1)[None], scale)
+    two, = scaled(odd, two[None], over_col(two, 1)[None], scale)
+    return node_grad, one, two
 
 
 def solution(mesh):

time: 73.9 us -> 71.6 us (0.969)
  waiting for transfers between devices: 28 us -> 25 us
  Pallas kernels: 10.8 us -> 11.6 us
    ppermute x24 -> x26, waiting for transfers between devices: 22.7 us -> 18.8 us  [over_col(): return lax.ppermute(value, 'col', [(i, i ^ flip) for i in range(n_col)])]
    ppermute x9, waiting for transfers between devices: 5.27 us -> 6.26 us  [over_row(): return lax.ppermute(value, 'row', [(i, i ^ flip) for i in range(n_row)])]
    ppermute x24 -> x26, starting transfers between devices: 20.1 us -> 20.2 us  [over_col(): return lax.ppermute(value, 'col', [(i, i ^ flip) for i in range(n_col)])]
  transfers between devices with their start and end apart: 33 -> 35, of which waited for: 18 -> 19; matrix products, arithmetic and copies ran while one was open for 3% -> 2% of each run, Pallas kernels for 13% -> 15%
where the time goes in v4:
time: 71.6 us; the launch traced here: 71.3 us
  starting transfers between devices  31 us (43%)
  waiting for transfers between devices  25 us (35%)
  Pallas kernels  11.6 us (16%)
  other arithmetic  1.23 us (2%)
  between operations  1.01 us (1%)
  local copies, waits for them, and re-layouts  0.99 us (1%)
    ppermute x26, starting transfers between devices, over_col(): return lax.ppermute(value, 'col', [(i, i ^ flip) for i in range(n_col)])  20.2 us
    ppermute x26, waiting for transfers between devices, over_col(): return lax.ppermute(value, 'col', [(i, i ^ flip) for i in range(n_col)])  18.8 us
    ppermute x9, starting transfers between devices, over_row(): return lax.ppermute(value, 'row', [(i, i ^ flip) for i in range(n_row)])  10.8 us
    ppermute x9, waiting for transfers between devices, over_row(): return lax.ppermute(value, 'row', [(i, i ^ flip) for i in range(n_row)])  6.26 us
    pallas_call x1, Pallas kernels, masked(): pl.pallas_call(functools.partial(mask_kernel, block, tile), grid_spec=plt...  5.82 us
    pallas_call x2, Pallas kernels, spread(): pl.pallas_call(functools.partial(spread_kernel, len(parts), turned), in_s...  2.81 us
    pallas_call x2, Pallas kernels, scaled(): pl.pallas_call(functools.partial(scaled_kernel, scale), in_specs=[pl.Bloc...  1.44 us
  transfers between devices with their start and end apart: 35, of which 19 were waited for; matrix products, arithmetic and copies ran while one was open for 2% of the time, Pallas kernels for 15%

profile of v4, /device:TPU:0, one launch (start us, length us, event | category | flops | bytes accessed | tf_op | source)
XLA Modules:
  0.0 71.3 jit_solution(2672566609436227537)
XLA Ops:
  0.6 1.0 %compare_select_fusion.value.refs_1_ = bf16[256,256]{1,0:T(8,128)(2,1)S(1)} fusion(bf16[256,256]{1,0:T(8,128)(2,1)} %param.11, bf16[256,256]{1,0:T(8,128)(2,1)} %param.12), kind=kLoop, calls=%fused_computation.6 | loop fusion | flops 131072 | bytes 393216 | tf_op jit(solution)/shard_map/jit(_where)/select_n | solution.py:243
  1.7 5.1 %collective-permute-start.5 = (bf16[256,256]{1,0:T(8,128)(2,1)S(1)}, bf16[256,256]{1,0:T(8,128)(2,1)S(1)}, u32[]{:S(2)}, u32[]{:S(2)}) collective-permute-start(bf16[256,256]{1,0:T(8,128)(2,1)S(1)} %compare_select_fusion.value.refs_1_), channel_id=1, source_target_pairs={{0,6},{1,7},{2,4},{3,5},{4,2},{5,3},{6,0},{7,1},{8,14},{9,15},{10,... | collective-permute-start | bytes 393224 | tf_op jit(solution)/shard_map/ppermute | solution.py:223
  6.8 0.6 collective-permute-start.1
  7.4 1.4 %collective-permute-start.14 = (bf16[256,256]{1,0:T(8,128)(2,1)}, bf16[256,256]{1,0:T(8,128)(2,1)S(1)}, u32[]{:S(2)}, u32[]{:S(2)}) collective-permute-start(bf16[256,256]{1,0:T(8,128)(2,1)} %value.1), channel_id=1, source_target_pairs={{0,2},{1,3},{2,0},{3,1},{4,6},{5,7},{6,4},{7,5},{8,10},{9,11},{10,... | collective-permute-start | bytes 393224 | tf_op jit(solution)/shard_map/ppermute | solution.py:223
  8.8 0.8 %copy.14.mask = s32[16,8]{1,0:T(8,128)S(1)} copy(s32[16,8]{0,1:T(8,128)} %param.10) | data formatting | bytes 1024 | tf_op args[1]
  9.6 5.8 %mask_tiles.1 = (bf16[2048,1024]{1,0:T(8,128)(2,1)S(1)}, bf16[16,128]{1,0:T(8,128)(2,1)S(1)}) custom-call(s32[8]{0:T(128)S(1)} %iota_xor_fusion.1.row_src, s32[4]{0:T(128)S(1)} %iota_xor_fusion.col_src, s32[16,8]{1,0:T(8,128)S(1)} %copy.14.mask, bf16[2048,1024]{1,0:T(8,128)(2,1)} %adj.1), custom_call_target="tpu_custom_call" | custom-call | tf_op jit(solution)/shard_map/mask_tiles/pallas_call | solution.py:57
  15.5 0.9 %collective-permute-done.1.value.refs_3_ = bf16[256,256]{1,0:T(8,128)(2,1)S(1)} collective-permute-done((bf16[256,256]{1,0:T(8,128)(2,1)S(1)}, bf16[256,256]{1,0:T(8,128)(2,1)S(1)}, u32[]{:S(2)}, u32[]{:S(2)}) %collective-permute-start.1) | collective-permute-done | bytes 131104 | tf_op jit(solution)/shard_map/ppermute | solution.py:223
  16.3 1.6 %collective-permute-done.3.value.refs_5_ = bf16[256,256]{1,0:T(8,128)(2,1)S(1)} collective-permute-done((bf16[256,256]{1,0:T(8,128)(2,1)S(1)}, bf16[256,256]{1,0:T(8,128)(2,1)S(1)}, u32[]{:S(2)}, u32[]{:S(2)}) %collective-permute-start.3) | collective-permute-done | bytes 131104 | tf_op jit(solution)/shard_map/ppermute | solution.py:223
  18.0 0.6 collective-permute-start.4
  18.7 0.1 collective-permute-done.14
  18.8 0.4 collective-permute-start.15
  19.3 0.2 collective-permute-done.4.refs_6_
  19.5 0.5 collective-permute-done.6.refs_8_
  20.0 1.4 %propagate.2 = bf16[1024,256]{1,0:T(8,128)(2,1)S(1)} custom-call(bf16[2048,1024]{1,0:T(8,128)(2,1)S(1)} %get-tuple-element.8.refs_0_, bf16[256,256]{1,0:T(8,128)(2,1)S(1)} %compare_select_fusion.value.refs_1_, bf16[256,256]{1,0:T(8,128)(2,1)S(1)} %collective-permute-done.refs_2_, bf16[256,256]{1,0:T(8,128)(2,1)S(1)} %collective-permute-done.1.value.refs_3_, ...), custom_call_target="tpu_custom_call" | custom-call | flops 1073741824 | bytes 4194304 | tf_op jit(solution)/shard_map/propagate/pallas_call | solution.py:96
  21.4 2.5 %collective-permute-start.18 = (bf16[256,256]{1,0:T(8,128)(2,1)S(1)}, bf16[256,256]{1,0:T(8,128)(2,1)S(1)}, u32[]{:S(2)}, u32[]{:S(2)}) collective-permute-start(bf16[256,256]{1,0:T(8,128)(2,1)S(1)} %after.9), channel_id=1, source_target_pairs={{0,6},{1,7},{2,4},{3,5},{4,2},{5,3},{6,0},{7,1},{8,14},{9,15},{10,... | collective-permute-start | bytes 393224 | tf_op jit(solution)/shard_map/ppermute | solution.py:223
  24.1 2.5 %collective-permute-start.9 = (bf16[256,256]{1,0:T(8,128)(2,1)S(1)}, bf16[256,256]{1,0:T(8,128)(2,1)S(1)}, u32[]{:S(2)}, u32[]{:S(2)}) collective-permute-start(bf16[256,256]{1,0:T(8,128)(2,1)S(1)} %get-tuple-element.15), channel_id=1, source_target_pairs={{0,24},{8,16},{16,8},{24,0},{1,25},{9,17},{17,9},{25,1},{2,26},{10... | collective-permute-start | bytes 393224 | tf_op jit(solution)/shard_map/ppermute | solution.py:226
  26.6 0.5 collective-permute-start.8
  27.1 0.5 collective-permute-start.7
  27.6 3.0 %collective-permute-done.9.refs_3_ = bf16[256,256]{1,0:T(8,128)(2,1)S(1)} collective-permute-done((bf16[256,256]{1,0:T(8,128)(2,1)S(1)}, bf16[256,256]{1,0:T(8,128)(2,1)S(1)}, u32[]{:S(2)}, u32[]{:S(2)}) %collective-permute-start.9) | collective-permute-done | bytes 131104 | tf_op jit(solution)/shard_map/ppermute | solution.py:226
  30.6 2.5 %collective-permute-done.8.refs_2_ = bf16[256,256]{1,0:T(8,128)(2,1)S(1)} collective-permute-done((bf16[256,256]{1,0:T(8,128)(2,1)S(1)}, bf16[256,256]{1,0:T(8,128)(2,1)S(1)}, u32[]{:S(2)}, u32[]{:S(2)}) %collective-permute-start.8) | collective-permute-done | bytes 131104 | tf_op jit(solution)/shard_map/ppermute | solution.py:226
  33.2 0.3 first_layer_gradient.1
  33.5 1.8 %collective-permute-start.12 = (bf16[256,256]{1,0:T(8,128)(2,1)S(1)}, bf16[256,256]{1,0:T(8,128)(2,1)S(1)}, u32[]{:S(2)}, u32[]{:S(2)}) collective-permute-start(bf16[256,256]{1,0:T(8,128)(2,1)S(1)} %get-tuple-element.10.refs_1_), channel_id=1, source_target_pairs={{0,24},{8,16},{16,8},{24,0},{1,25},{9,17},{17,9},{25,1},{2,26},{10... | collective-permute-start | bytes 393224 | tf_op jit(solution)/shard_map/ppermute | solution.py:226
  35.3 1.3 %collective-permute-start.11 = (bf16[256,256]{1,0:T(8,128)(2,1)S(1)}, bf16[256,256]{1,0:T(8,128)(2,1)S(1)}, u32[]{:S(2)}, u32[]{:S(2)}) collective-permute-start(bf16[256,256]{1,0:T(8,128)(2,1)S(1)} %get-tuple-element.10.refs_1_), channel_id=1, source_target_pairs={{0,16},{8,24},{16,0},{24,8},{1,17},{9,25},{17,1},{25,9},{2,18},{10... | collective-permute-start | bytes 393224 | tf_op jit(solution)/shard_map/ppermute | solution.py:226
  36.6 0.5 collective-permute-start.17
  37.1 0.6 collective-permute-start.10
  37.8 0.2 collective-permute-start.19
  38.1 1.3 %collective-permute-start.27 = (bf16[128,256]{1,0:T(8,128)(2,1)S(1)}, bf16[128,256]{1,0:T(8,128)(2,1)S(1)}, u32[]{:S(2)}, u32[]{:S(2)}) collective-permute-start(bf16[128,256]{1,0:T(8,128)(2,1)S(1)} %joined.11.refs_0_), channel_id=1, source_target_pairs={{0,6},{1,7},{2,4},{3,5},{4,2},{5,3},{6,0},{7,1},{8,14},{9,15},{10,... | collective-permute-start | bytes 196616 | tf_op jit(solution)/shard_map/ppermute | solution.py:223
  39.4 2.4 %collective-permute-start.26 = (bf16[128,256]{1,0:T(8,128)(2,1)S(1)}, bf16[128,256]{1,0:T(8,128)(2,1)S(1)}, u32[]{:S(2)}, u32[]{:S(2)}) collective-permute-start(bf16[128,256]{1,0:T(8,128)(2,1)S(1)} %joined.11.refs_0_), channel_id=1, source_target_pairs={{0,4},{1,5},{2,6},{3,7},{4,0},{5,1},{6,2},{7,3},{8,12},{9,13},{10,... | collective-permute-start | bytes 196616 | tf_op jit(solution)/shard_map/ppermute | solution.py:223
  41.8 0.8 %collective-permute-start.25 = (bf16[128,256]{1,0:T(8,128)(2,1)S(1)}, bf16[128,256]{1,0:T(8,128)(2,1)S(1)}, u32[]{:S(2)}, u32[]{:S(2)}) collective-permute-start(bf16[128,256]{1,0:T(8,128)(2,1)S(1)} %joined.11.refs_0_), channel_id=1, source_target_pairs={{0,2},{1,3},{2,0},{3,1},{4,6},{5,7},{6,4},{7,5},{8,10},{9,11},{10,... | collective-permute-start | bytes 196616 | tf_op jit(solution)/shard_map/ppermute | solution.py:223
  42.7 1.5 %propagate.3 = bf16[2048,256]{1,0:T(8,128)(2,1)S(1)} custom-call(bf16[2048,1024]{1,0:T(8,128)(2,1)S(1)} %get-tuple-element.8.refs_0_, bf16[256,256]{1,0:T(8,128)(2,1)S(1)} %get-tuple-element.10.refs_1_, bf16[256,256]{1,0:T(8,128)(2,1)S(1)} %collective-permute-done.10.refs_2_, bf16[256,256]{1,0:T(8,128)(2,1)S(1)} %collective-permute-done.11.refs_3_, ...), custom_call_target="tpu_custom_call" | custom-call | flops 24000000000 | bytes 1000000 | tf_op jit(solution)/shard_map/propagate/pallas_call | solution.py:96
  44.3 3.3 %collective-permute-done.26.refs_2_ = bf16[128,256]{1,0:T(8,128)(2,1)S(1)} collective-permute-done((bf16[128,256]{1,0:T(8,128)(2,1)S(1)}, bf16[128,256]{1,0:T(8,128)(2,1)S(1)}, u32[]{:S(2)}, u32[]{:S(2)}) %collective-permute-start.26) | collective-permute-done | bytes 65568 | tf_op jit(solution)/shard_map/ppermute | solution.py:223
  47.6 0.5 fusion.3
  48.3 0.1 fusion
  48.5 0.9 %collective-permute-done.23.refs_1_ = bf16[128,256]{1,0:T(8,128)(2,1)S(1)} collective-permute-done((bf16[128,256]{1,0:T(8,128)(2,1)S(1)}, bf16[128,256]{1,0:T(8,128)(2,1)S(1)}, u32[]{:S(2)}, u32[]{:S(2)}) %collective-permute-start.23) | collective-permute-done | bytes 65568 | tf_op jit(solution)/shard_map/ppermute | solution.py:223
  49.5 1.6 %collective-permute-start.30 = (bf16[2,128,256]{2,1,0:T(8,128)(2,1)S(1)}, bf16[2,128,256]{2,1,0:T(8,128)(2,1)S(1)}, u32[]{:S(2)}, u32[]{:S(2)}) collective-permute-start(bf16[2,128,256]{2,1,0:T(8,128)(2,1)S(1)} %pad_maximum_fusion.refs_0_), channel_id=1, source_target_pairs={{0,24},{8,16},{16,8},{24,0},{1,25},{9,17},{17,9},{25,1},{2,26},{10... | collective-permute-start | bytes 393224 | tf_op jit(solution)/shard_map/ppermute | solution.py:226
  51.1 1.3 %collective-permute-start.29 = (bf16[2,128,256]{2,1,0:T(8,128)(2,1)S(1)}, bf16[2,128,256]{2,1,0:T(8,128)(2,1)S(1)}, u32[]{:S(2)}, u32[]{:S(2)}) collective-permute-start(bf16[2,128,256]{2,1,0:T(8,128)(2,1)S(1)} %pad_maximum_fusion.refs_0_), channel_id=1, source_target_pairs={{0,16},{8,24},{16,0},{24,8},{1,17},{9,25},{17,1},{25,9},{2,18},{10... | collective-permute-start | bytes 393224 | tf_op jit(solution)/shard_map/ppermute | solution.py:226
  52.4 0.7 collective-permute-start.28
  53.1 4.1 %collective-permute-done.21.refs_1_ = bf16[2,256,256]{2,1,0:T(8,128)(2,1)S(1)} collective-permute-done((bf16[2,256,256]{2,1,0:T(8,128)(2,1)S(1)}, bf16[2,256,256]{2,1,0:T(8,128)(2,1)S(1)}, u32[]{:S(2)}, u32[]{:S(2)}) %collective-permute-start.21) | collective-permute-done | bytes 262176 | tf_op jit(solution)/shard_map/ppermute | solution.py:223
  57.3 1.0 %collective-permute-start.22 = (bf16[1,256,256]{2,1,0:T(8,128)(2,1)S(1)}, bf16[1,256,256]{2,1,0:T(8,128)(2,1)S(1)}, u32[]{:S(2)}, u32[]{:S(2)}) collective-permute-start(bf16[1,256,256]{2,1,0:T(8,128)(2,1)S(1)} %get-tuple-element.19), channel_id=1, source_target_pairs={{0,4},{1,5},{2,6},{3,7},{4,0},{5,1},{6,2},{7,3},{8,12},{9,13},{10,... | collective-permute-start | bytes 393224 | tf_op jit(solution)/shard_map/ppermute | solution.py:223
  58.3 0.6 collective-permute-done.29.refs_2_
  59.0 1.2 %collective-permute-start.31 = (bf16[128,256]{1,0:T(8,128)(2,1)S(1)}, bf16[128,256]{1,0:T(8,128)(2,1)S(1)}, u32[]{:S(2)}, u32[]{:S(2)}) collective-permute-start(bf16[128,256]{1,0:T(8,128)(2,1)S(1)} %get-tuple-element.23.refs_0_), channel_id=1, source_target_pairs={{0,2},{1,3},{2,0},{3,1},{4,6},{5,7},{6,4},{7,5},{8,10},{9,11},{10,... | collective-permute-start | bytes 196616 | tf_op jit(solution)/shard_map/ppermute | solution.py:223
  60.2 3.4 %collective-permute-done.31.refs_1_ = bf16[128,256]{1,0:T(8,128)(2,1)S(1)} collective-permute-done((bf16[128,256]{1,0:T(8,128)(2,1)S(1)}, bf16[128,256]{1,0:T(8,128)(2,1)S(1)}, u32[]{:S(2)}, u32[]{:S(2)}) %collective-permute-start.31) | collective-permute-done | bytes 65568 | tf_op jit(solution)/shard_map/ppermute | solution.py:223
  63.6 1.7 %collective-permute-start.32 = (bf16[128,256]{1,0:T(8,128)(2,1)S(1)}, bf16[128,256]{1,0:T(8,128)(2,1)S(1)}, u32[]{:S(2)}, u32[]{:S(2)}) collective-permute-start(bf16[128,256]{1,0:T(8,128)(2,1)S(1)} %joined.14.refs_0_), channel_id=1, source_target_pairs={{0,4},{1,5},{2,6},{3,7},{4,0},{5,1},{6,2},{7,3},{8,12},{9,13},{10,... | collective-permute-start | bytes 196616 | tf_op jit(solution)/shard_map/ppermute | solution.py:223
  65.4 0.8 %collective-permute-done.22.refs_1_ = bf16[1,256,256]{2,1,0:T(8,128)(2,1)S(1)} collective-permute-done((bf16[1,256,256]{2,1,0:T(8,128)(2,1)S(1)}, bf16[1,256,256]{2,1,0:T(8,128)(2,1)S(1)}, u32[]{:S(2)}, u32[]{:S(2)}) %collective-permute-start.22) | collective-permute-done | bytes 131104 | tf_op jit(solution)/shard_map/ppermute | solution.py:223
  66.2 2.7 %collective-permute-done.32.refs_1_ = bf16[128,256]{1,0:T(8,128)(2,1)S(1)} collective-permute-done((bf16[128,256]{1,0:T(8,128)(2,1)S(1)}, bf16[128,256]{1,0:T(8,128)(2,1)S(1)}, u32[]{:S(2)}, u32[]{:S(2)}) %collective-permute-start.32) | collective-permute-done | bytes 65568 | tf_op jit(solution)/shard_map/ppermute | solution.py:223
  69.0 0.9 %node_gradient.1 = bf16[256,256]{1,0:T(8,128)(2,1)} custom-call(bf16[256,256]{1,0:T(8,128)(2,1)S(1)} %bitcast.63, bf16[256,256]{1,0:T(8,128)(2,1)S(1)} %copy-done.4), custom_call_target="tpu_custom_call" | custom-call | tf_op jit(solution)/shard_map/node_gradient/pallas_call | solution.py:154
  69.9 0.7 %weight_gradients.3 = f32[256,256]{1,0:T(8,128)} custom-call(s32[1]{0:T(128)} %bitcast.odd, f32[1,128,256]{2,1,0:T(8,128)S(1)} %get-tuple-element.22.mine, f32[1,128,256]{2,1,0:T(8,128)S(1)} %bitcast.67), custom_call_target="tpu_custom_call" | custom-call | tf_op jit(solution)/shard_map/weight_gradients/pallas_call | solution.py:204
  70.6 0.7 %weight_gradients.2 = f32[256,256]{1,0:T(8,128)} custom-call(s32[1]{0:T(128)} %bitcast.odd, f32[1,128,256]{2,1,0:T(8,128)S(1)} %bitcast.64, f32[1,128,256]{2,1,0:T(8,128)S(1)} %bitcast.68), custom_call_target="tpu_custom_call" | custom-call | tf_op jit(solution)/shard_map/weight_gradients/pallas_call | solution.py:204
  (74 shorter events, 1.5 us)
Async XLA Ops:
  0.6 14.8 %copy-start = (bf16[256,256]{1,0:T(8,128)(2,1)S(1)}, bf16[256,256]{1,0:T(8,128)(2,1)}, u32[]{:S(2)}) copy-start(bf16[256,256]{1,0:T(8,128)(2,1)} %value.1) | copy-start | bytes 393220
  1.7 16.3 %collective-permute-start.5 = (bf16[256,256]{1,0:T(8,128)(2,1)S(1)}, bf16[256,256]{1,0:T(8,128)(2,1)S(1)}, u32[]{:S(2)}, u32[]{:S(2)}) collective-permute-start(bf16[256,256]{1,0:T(8,128)(2,1)S(1)} %compare_select_fusion.value.refs_1_), channel_id=1, source_target_pairs={{0,6},{1,7},{2,4},{3,5},{4,2},{5,3},{6,0},{7,1},{8,14},{9,15},{10,... | collective-permute-start | bytes 393224 | tf_op jit(solution)/shard_map/ppermute | solution.py:223
  6.8 11.2 %collective-permute-start.3 = (bf16[256,256]{1,0:T(8,128)(2,1)S(1)}, bf16[256,256]{1,0:T(8,128)(2,1)S(1)}, u32[]{:S(2)}, u32[]{:S(2)}) collective-permute-start(bf16[256,256]{1,0:T(8,128)(2,1)S(1)} %compare_select_fusion.value.refs_1_), channel_id=1, source_target_pairs={{0,4},{1,5},{2,6},{3,7},{4,0},{5,1},{6,2},{7,3},{8,12},{9,13},{10,... | collective-permute-start | bytes 393224 | tf_op jit(solution)/shard_map/ppermute | solution.py:223
  6.8 9.5 %collective-permute-start.1 = (bf16[256,256]{1,0:T(8,128)(2,1)S(1)}, bf16[256,256]{1,0:T(8,128)(2,1)S(1)}, u32[]{:S(2)}, u32[]{:S(2)}) collective-permute-start(bf16[256,256]{1,0:T(8,128)(2,1)S(1)} %compare_select_fusion.value.refs_1_), channel_id=1, source_target_pairs={{0,2},{1,3},{2,0},{3,1},{4,6},{5,7},{6,4},{7,5},{8,10},{9,11},{10,... | collective-permute-start | bytes 393224 | tf_op jit(solution)/shard_map/ppermute | solution.py:223
  7.4 11.2 %collective-permute-start.13 = (bf16[256,256]{1,0:T(8,128)(2,1)}, bf16[256,256]{1,0:T(8,128)(2,1)S(1)}, u32[]{:S(2)}, u32[]{:S(2)}) collective-permute-start(bf16[256,256]{1,0:T(8,128)(2,1)} %value.1), channel_id=1, source_target_pairs={{0,1},{1,0},{2,3},{3,2},{4,5},{5,4},{6,7},{7,6},{8,9},{9,8},{10,11... | collective-permute-start | bytes 393224 | tf_op jit(solution)/shard_map/ppermute | solution.py:223
  7.4 11.4 %collective-permute-start.14 = (bf16[256,256]{1,0:T(8,128)(2,1)}, bf16[256,256]{1,0:T(8,128)(2,1)S(1)}, u32[]{:S(2)}, u32[]{:S(2)}) collective-permute-start(bf16[256,256]{1,0:T(8,128)(2,1)} %value.1), channel_id=1, source_target_pairs={{0,2},{1,3},{2,0},{3,1},{4,6},{5,7},{6,4},{7,5},{8,10},{9,11},{10,... | collective-permute-start | bytes 393224 | tf_op jit(solution)/shard_map/ppermute | solution.py:223
  16.3 2.9 %collective-permute-start = (bf16[256,256]{1,0:T(8,128)(2,1)S(1)}, bf16[256,256]{1,0:T(8,128)(2,1)S(1)}, u32[]{:S(2)}, u32[]{:S(2)}) collective-permute-start(bf16[256,256]{1,0:T(8,128)(2,1)S(1)} %after.5), channel_id=1, source_target_pairs={{0,1},{1,0},{2,3},{3,2},{4,5},{5,4},{6,7},{7,6},{8,9},{9,8},{10,11... | collective-permute-start | bytes 393224 | tf_op jit(solution)/shard_map/ppermute | solution.py:223
  18.0 1.3 %collective-permute-start.2 = (bf16[256,256]{1,0:T(8,128)(2,1)S(1)}, bf16[256,256]{1,0:T(8,128)(2,1)S(1)}, u32[]{:S(2)}, u32[]{:S(2)}) collective-permute-start(bf16[256,256]{1,0:T(8,128)(2,1)S(1)} %after.6), channel_id=1, source_target_pairs={{0,1},{1,0},{2,3},{3,2},{4,5},{5,4},{6,7},{7,6},{8,9},{9,8},{10,11... | collective-permute-start | bytes 393224 | tf_op jit(solution)/shard_map/ppermute | solution.py:223
  18.0 1.6 %collective-permute-start.4 = (bf16[256,256]{1,0:T(8,128)(2,1)S(1)}, bf16[256,256]{1,0:T(8,128)(2,1)S(1)}, u32[]{:S(2)}, u32[]{:S(2)}) collective-permute-start(bf16[256,256]{1,0:T(8,128)(2,1)S(1)} %after.7), channel_id=1, source_target_pairs={{0,1},{1,0},{2,3},{3,2},{4,5},{5,4},{6,7},{7,6},{8,9},{9,8},{10,11... | collective-permute-start | bytes 393224 | tf_op jit(solution)/shard_map/ppermute | solution.py:223
  18.6 14.6 %copy-start.1 = (bf16[256,256]{1,0:T(8,128)(2,1)S(1)}, bf16[256,256]{1,0:T(8,128)(2,1)}, u32[]{:S(2)}) copy-start(bf16[256,256]{1,0:T(8,128)(2,1)} %refs_4_.1) | copy-start | bytes 393220
  18.6 14.6 %copy-start.2 = (bf16[256,256]{1,0:T(8,128)(2,1)S(1)}, bf16[256,256]{1,0:T(8,128)(2,1)}, u32[]{:S(2)}) copy-start(bf16[256,256]{1,0:T(8,128)(2,1)} %refs_5_.1) | copy-start | bytes 393220
  18.6 14.6 %copy-start.3 = (bf16[256,256]{1,0:T(8,128)(2,1)S(1)}, bf16[256,256]{1,0:T(8,128)(2,1)}, u32[]{:S(2)}) copy-start(bf16[256,256]{1,0:T(8,128)(2,1)} %refs_6_.1) | copy-start | bytes 393220
  18.6 1.4 %collective-permute-start.6 = (bf16[256,256]{1,0:T(8,128)(2,1)S(1)}, bf16[256,256]{1,0:T(8,128)(2,1)S(1)}, u32[]{:S(2)}, u32[]{:S(2)}) collective-permute-start(bf16[256,256]{1,0:T(8,128)(2,1)S(1)} %after.8), channel_id=1, source_target_pairs={{0,1},{1,0},{2,3},{3,2},{4,5},{5,4},{6,7},{7,6},{8,9},{9,8},{10,11... | collective-permute-start | bytes 393224 | tf_op jit(solution)/shard_map/ppermute | solution.py:223
  18.8 8.3 %collective-permute-start.15 = (bf16[256,256]{1,0:T(8,128)(2,1)S(1)}, bf16[256,256]{1,0:T(8,128)(2,1)S(1)}, u32[]{:S(2)}, u32[]{:S(2)}) collective-permute-start(bf16[256,256]{1,0:T(8,128)(2,1)S(1)} %collective-permute-done.14), channel_id=1, source_target_pairs={{0,1},{1,0},{2,3},{3,2},{4,5},{5,4},{6,7},{7,6},{8,9},{9,8},{10,11... | collective-permute-start | bytes 393224 | tf_op jit(solution)/shard_map/ppermute | solution.py:223
  21.4 15.7 %collective-permute-start.18 = (bf16[256,256]{1,0:T(8,128)(2,1)S(1)}, bf16[256,256]{1,0:T(8,128)(2,1)S(1)}, u32[]{:S(2)}, u32[]{:S(2)}) collective-permute-start(bf16[256,256]{1,0:T(8,128)(2,1)S(1)} %after.9), channel_id=1, source_target_pairs={{0,6},{1,7},{2,4},{3,5},{4,2},{5,3},{6,0},{7,1},{8,14},{9,15},{10,... | collective-permute-start | bytes 393224 | tf_op jit(solution)/shard_map/ppermute | solution.py:223
  24.0 12.6 %collective-permute-start.16 = (bf16[256,256]{1,0:T(8,128)(2,1)S(1)}, bf16[256,256]{1,0:T(8,128)(2,1)S(1)}, u32[]{:S(2)}, u32[]{:S(2)}) collective-permute-start(bf16[256,256]{1,0:T(8,128)(2,1)S(1)} %after.9), channel_id=1, source_target_pairs={{0,4},{1,5},{2,6},{3,7},{4,0},{5,1},{6,2},{7,3},{8,12},{9,13},{10,... | collective-permute-start | bytes 393224 | tf_op jit(solution)/shard_map/ppermute | solution.py:223
  24.1 6.6 %collective-permute-start.9 = (bf16[256,256]{1,0:T(8,128)(2,1)S(1)}, bf16[256,256]{1,0:T(8,128)(2,1)S(1)}, u32[]{:S(2)}, u32[]{:S(2)}) collective-permute-start(bf16[256,256]{1,0:T(8,128)(2,1)S(1)} %get-tuple-element.15), channel_id=1, source_target_pairs={{0,24},{8,16},{16,8},{24,0},{1,25},{9,17},{17,9},{25,1},{2,26},{10... | collective-permute-start | bytes 393224 | tf_op jit(solution)/shard_map/ppermute | solution.py:226
  26.6 6.6 %collective-permute-start.8 = (bf16[256,256]{1,0:T(8,128)(2,1)S(1)}, bf16[256,256]{1,0:T(8,128)(2,1)S(1)}, u32[]{:S(2)}, u32[]{:S(2)}) collective-permute-start(bf16[256,256]{1,0:T(8,128)(2,1)S(1)} %get-tuple-element.16), channel_id=1, source_target_pairs={{0,16},{8,24},{16,0},{24,8},{1,17},{9,25},{17,1},{25,9},{2,18},{10... | collective-permute-start | bytes 393224 | tf_op jit(solution)/shard_map/ppermute | solution.py:226
  27.1 6.1 %collective-permute-start.7 = (bf16[256,256]{1,0:T(8,128)(2,1)S(1)}, bf16[256,256]{1,0:T(8,128)(2,1)S(1)}, u32[]{:S(2)}, u32[]{:S(2)}) collective-permute-start(bf16[256,256]{1,0:T(8,128)(2,1)S(1)} %get-tuple-element.17), channel_id=1, source_target_pairs={{0,8},{8,0},{16,24},{24,16},{1,9},{9,1},{17,25},{25,17},{2,10},{10... | collective-permute-start | bytes 393224 | tf_op jit(solution)/shard_map/ppermute | solution.py:226
  33.5 8.3 %collective-permute-start.12 = (bf16[256,256]{1,0:T(8,128)(2,1)S(1)}, bf16[256,256]{1,0:T(8,128)(2,1)S(1)}, u32[]{:S(2)}, u32[]{:S(2)}) collective-permute-start(bf16[256,256]{1,0:T(8,128)(2,1)S(1)} %get-tuple-element.10.refs_1_), channel_id=1, source_target_pairs={{0,24},{8,16},{16,8},{24,0},{1,25},{9,17},{17,9},{25,1},{2,26},{10... | collective-permute-start | bytes 393224 | tf_op jit(solution)/shard_map/ppermute | solution.py:226
  35.3 7.4 %collective-permute-start.11 = (bf16[256,256]{1,0:T(8,128)(2,1)S(1)}, bf16[256,256]{1,0:T(8,128)(2,1)S(1)}, u32[]{:S(2)}, u32[]{:S(2)}) collective-permute-start(bf16[256,256]{1,0:T(8,128)(2,1)S(1)} %get-tuple-element.10.refs_1_), channel_id=1, source_target_pairs={{0,16},{8,24},{16,0},{24,8},{1,17},{9,25},{17,1},{25,9},{2,18},{10... | collective-permute-start | bytes 393224 | tf_op jit(solution)/shard_map/ppermute | solution.py:226
  36.6 1.3 %collective-permute-start.24 = (bf16[128,256]{1,0:T(8,128)(2,1)S(1)}, bf16[128,256]{1,0:T(8,128)(2,1)S(1)}, u32[]{:S(2)}, u32[]{:S(2)}) collective-permute-start(bf16[128,256]{1,0:T(8,128)(2,1)S(1)} %get-tuple-element.12), channel_id=1, source_target_pairs={{0,1},{1,0},{2,3},{3,2},{4,5},{5,4},{6,7},{7,6},{8,9},{9,8},{10,11... | collective-permute-start | bytes 196616 | tf_op jit(solution)/shard_map/ppermute | solution.py:223
  36.6 1.5 %collective-permute-start.17 = (bf16[256,256]{1,0:T(8,128)(2,1)S(1)}, bf16[256,256]{1,0:T(8,128)(2,1)S(1)}, u32[]{:S(2)}, u32[]{:S(2)}) collective-permute-start(bf16[256,256]{1,0:T(8,128)(2,1)S(1)} %collective-permute-done.16), channel_id=1, source_target_pairs={{0,1},{1,0},{2,3},{3,2},{4,5},{5,4},{6,7},{7,6},{8,9},{9,8},{10,11... | collective-permute-start | bytes 393224 | tf_op jit(solution)/shard_map/ppermute | solution.py:223
  37.1 5.6 %collective-permute-start.10 = (bf16[256,256]{1,0:T(8,128)(2,1)S(1)}, bf16[256,256]{1,0:T(8,128)(2,1)S(1)}, u32[]{:S(2)}, u32[]{:S(2)}) collective-permute-start(bf16[256,256]{1,0:T(8,128)(2,1)S(1)} %get-tuple-element.10.refs_1_), channel_id=1, source_target_pairs={{0,8},{8,0},{16,24},{24,16},{1,9},{9,1},{17,25},{25,17},{2,10},{10... | collective-permute-start | bytes 393224 | tf_op jit(solution)/shard_map/ppermute | solution.py:226
  37.8 1.5 %collective-permute-start.19 = (bf16[256,256]{1,0:T(8,128)(2,1)S(1)}, bf16[256,256]{1,0:T(8,128)(2,1)S(1)}, u32[]{:S(2)}, u32[]{:S(2)}) collective-permute-start(bf16[256,256]{1,0:T(8,128)(2,1)S(1)} %collective-permute-done.18), channel_id=1, source_target_pairs={{0,1},{1,0},{2,3},{3,2},{4,5},{5,4},{6,7},{7,6},{8,9},{9,8},{10,11... | collective-permute-start | bytes 393224 | tf_op jit(solution)/shard_map/ppermute | solution.py:223
  38.1 6.3 %collective-permute-start.27 = (bf16[128,256]{1,0:T(8,128)(2,1)S(1)}, bf16[128,256]{1,0:T(8,128)(2,1)S(1)}, u32[]{:S(2)}, u32[]{:S(2)}) collective-permute-start(bf16[128,256]{1,0:T(8,128)(2,1)S(1)} %joined.11.refs_0_), channel_id=1, source_target_pairs={{0,6},{1,7},{2,4},{3,5},{4,2},{5,3},{6,0},{7,1},{8,14},{9,15},{10,... | collective-permute-start | bytes 196616 | tf_op jit(solution)/shard_map/ppermute | solution.py:223
  39.4 8.2 %collective-permute-start.26 = (bf16[128,256]{1,0:T(8,128)(2,1)S(1)}, bf16[128,256]{1,0:T(8,128)(2,1)S(1)}, u32[]{:S(2)}, u32[]{:S(2)}) collective-permute-start(bf16[128,256]{1,0:T(8,128)(2,1)S(1)} %joined.11.refs_0_), channel_id=1, source_target_pairs={{0,4},{1,5},{2,6},{3,7},{4,0},{5,1},{6,2},{7,3},{8,12},{9,13},{10,... | collective-permute-start | bytes 196616 | tf_op jit(solution)/shard_map/ppermute | solution.py:223
  41.8 5.8 %collective-permute-start.25 = (bf16[128,256]{1,0:T(8,128)(2,1)S(1)}, bf16[128,256]{1,0:T(8,128)(2,1)S(1)}, u32[]{:S(2)}, u32[]{:S(2)}) collective-permute-start(bf16[128,256]{1,0:T(8,128)(2,1)S(1)} %joined.11.refs_0_), channel_id=1, source_target_pairs={{0,2},{1,3},{2,0},{3,1},{4,6},{5,7},{6,4},{7,5},{8,10},{9,11},{10,... | collective-permute-start | bytes 196616 | tf_op jit(solution)/shard_map/ppermute | solution.py:223
  44.3 4.0 %collective-permute-start.20 = (bf16[4,256,256]{2,1,0:T(8,128)(2,1)S(1)}, bf16[4,256,256]{2,1,0:T(8,128)(2,1)S(1)}, u32[]{:S(2)}, u32[]{:S(2)}) collective-permute-start(bf16[4,256,256]{2,1,0:T(8,128)(2,1)S(1)} %slice_bitcast_fusion), channel_id=1, source_target_pairs={{0,1},{1,0},{2,3},{3,2},{4,5},{5,4},{6,7},{7,6},{8,9},{9,8},{10,11... | collective-permute-start | bytes 1572872 | tf_op jit(solution)/shard_map/ppermute | solution.py:223
  48.1 20.9 %copy-start.4 = (bf16[256,256]{1,0:T(8,128)(2,1)S(1)}, bf16[256,256]{1,0:T(8,128)(2,1)}, u32[]{:S(2)}) copy-start(bf16[256,256]{1,0:T(8,128)(2,1)} %w_one.1) | copy-start | bytes 393220
  48.2 1.3 %collective-permute-start.23 = (bf16[128,256]{1,0:T(8,128)(2,1)S(1)}, bf16[128,256]{1,0:T(8,128)(2,1)S(1)}, u32[]{:S(2)}, u32[]{:S(2)}) collective-permute-start(bf16[128,256]{1,0:T(8,128)(2,1)S(1)} %select_convert_fusion), channel_id=1, source_target_pairs={{0,1},{1,0},{2,3},{3,2},{4,5},{5,4},{6,7},{7,6},{8,9},{9,8},{10,11... | collective-permute-start | bytes 196616 | tf_op jit(solution)/shard_map/ppermute | solution.py:223
  48.4 8.8 %collective-permute-start.21 = (bf16[2,256,256]{2,1,0:T(8,128)(2,1)S(1)}, bf16[2,256,256]{2,1,0:T(8,128)(2,1)S(1)}, u32[]{:S(2)}, u32[]{:S(2)}) collective-permute-start(bf16[2,256,256]{2,1,0:T(8,128)(2,1)S(1)} %get-tuple-element.13), channel_id=1, source_target_pairs={{0,2},{1,3},{2,0},{3,1},{4,6},{5,7},{6,4},{7,5},{8,10},{9,11},{10,... | collective-permute-start | bytes 786440 | tf_op jit(solution)/shard_map/ppermute | solution.py:223
  49.5 8.7 %collective-permute-start.30 = (bf16[2,128,256]{2,1,0:T(8,128)(2,1)S(1)}, bf16[2,128,256]{2,1,0:T(8,128)(2,1)S(1)}, u32[]{:S(2)}, u32[]{:S(2)}) collective-permute-start(bf16[2,128,256]{2,1,0:T(8,128)(2,1)S(1)} %pad_maximum_fusion.refs_0_), channel_id=1, source_target_pairs={{0,24},{8,16},{16,8},{24,0},{1,25},{9,17},{17,9},{25,1},{2,26},{10... | collective-permute-start | bytes 393224 | tf_op jit(solution)/shard_map/ppermute | solution.py:226
  51.1 7.7 %collective-permute-start.29 = (bf16[2,128,256]{2,1,0:T(8,128)(2,1)S(1)}, bf16[2,128,256]{2,1,0:T(8,128)(2,1)S(1)}, u32[]{:S(2)}, u32[]{:S(2)}) collective-permute-start(bf16[2,128,256]{2,1,0:T(8,128)(2,1)S(1)} %pad_maximum_fusion.refs_0_), channel_id=1, source_target_pairs={{0,16},{8,24},{16,0},{24,8},{1,17},{9,25},{17,1},{25,9},{2,18},{10... | collective-permute-start | bytes 393224 | tf_op jit(solution)/shard_map/ppermute | solution.py:226
  52.4 6.4 %collective-permute-start.28 = (bf16[2,128,256]{2,1,0:T(8,128)(2,1)S(1)}, bf16[2,128,256]{2,1,0:T(8,128)(2,1)S(1)}, u32[]{:S(2)}, u32[]{:S(2)}) collective-permute-start(bf16[2,128,256]{2,1,0:T(8,128)(2,1)S(1)} %pad_maximum_fusion.refs_0_), channel_id=1, source_target_pairs={{0,8},{8,0},{16,24},{24,16},{1,9},{9,1},{17,25},{25,17},{2,10},{10... | collective-permute-start | bytes 393224 | tf_op jit(solution)/shard_map/ppermute | solution.py:226
  57.3 8.9 %collective-permute-start.22 = (bf16[1,256,256]{2,1,0:T(8,128)(2,1)S(1)}, bf16[1,256,256]{2,1,0:T(8,128)(2,1)S(1)}, u32[]{:S(2)}, u32[]{:S(2)}) collective-permute-start(bf16[1,256,256]{2,1,0:T(8,128)(2,1)S(1)} %get-tuple-element.19), channel_id=1, source_target_pairs={{0,4},{1,5},{2,6},{3,7},{4,0},{5,1},{6,2},{7,3},{8,12},{9,13},{10,... | collective-permute-start | bytes 393224 | tf_op jit(solution)/shard_map/ppermute | solution.py:223
  59.0 4.7 %collective-permute-start.31 = (bf16[128,256]{1,0:T(8,128)(2,1)S(1)}, bf16[128,256]{1,0:T(8,128)(2,1)S(1)}, u32[]{:S(2)}, u32[]{:S(2)}) collective-permute-start(bf16[128,256]{1,0:T(8,128)(2,1)S(1)} %get-tuple-element.23.refs_0_), channel_id=1, source_target_pairs={{0,2},{1,3},{2,0},{3,1},{4,6},{5,7},{6,4},{7,5},{8,10},{9,11},{10,... | collective-permute-start | bytes 196616 | tf_op jit(solution)/shard_map/ppermute | solution.py:223
  63.6 5.2 %collective-permute-start.32 = (bf16[128,256]{1,0:T(8,128)(2,1)S(1)}, bf16[128,256]{1,0:T(8,128)(2,1)S(1)}, u32[]{:S(2)}, u32[]{:S(2)}) collective-permute-start(bf16[128,256]{1,0:T(8,128)(2,1)S(1)} %joined.14.refs_0_), channel_id=1, source_target_pairs={{0,4},{1,5},{2,6},{3,7},{4,0},{5,1},{6,2},{7,3},{8,12},{9,13},{10,... | collective-permute-start | bytes 196616 | tf_op jit(solution)/shard_map/ppermute | solution.py:223
  65.4 4.5 %collective-permute-start.34 = (f32[128,256]{1,0:T(8,128)S(1)}, f32[128,256]{1,0:T(8,128)S(1)}, u32[]{:S(2)}, u32[]{:S(2)}) collective-permute-start(f32[128,256]{1,0:T(8,128)S(1)} %get-tuple-element.21), channel_id=1, source_target_pairs={{0,1},{1,0},{2,3},{3,2},{4,5},{5,4},{6,7},{7,6},{8,9},{9,8},{10,11... | collective-permute-start | bytes 393224 | tf_op jit(solution)/shard_map/ppermute | solution.py:223
  68.9 1.7 %collective-permute-start.33 = (f32[128,256]{1,0:T(8,128)S(1)}, f32[128,256]{1,0:T(8,128)S(1)}, u32[]{:S(2)}, u32[]{:S(2)}) collective-permute-start(f32[128,256]{1,0:T(8,128)S(1)} %joined.15), channel_id=1, source_target_pairs={{0,1},{1,0},{2,3},{3,2},{4,5},{5,4},{6,7},{7,6},{8,9},{9,8},{10,11... | collective-permute-start | bytes 393224 | tf_op jit(solution)/shard_map/ppermute | solution.py:223
